TPU v7x, 32 devices: a whole 2x2x4 slice. The times are simulated.
32 devices in a mesh: shard: 4 (over z), heads: 2 (over core), tensor: 4 (over y, x).
Axes of the slice: x: 2, y: 2, z: 4, core: 2. Of those that a mesh axis runs over, the one named last changes fastest.
Arguments:
- block_input: bfloat16 [2048, 1024], P('shard'), may hold values from -6 to 6
- attn_gain: bfloat16 [1024], P('shard'), may hold values from 0.25 to 1.75
- query_weight: bfloat16 [1024, 1024], P('shard', 'heads'), may hold values from -0.1875 to 0.1875
- key_weight: bfloat16 [1024, 512], P('shard', 'heads'), may hold values from -0.1875 to 0.1875
- value_weight: bfloat16 [1024, 512], P('shard', 'heads'), may hold values from -0.1875 to 0.1875
- query_gain: bfloat16 [64], replicated, may hold values from 0.25 to 1.75
- key_gain: bfloat16 [64], replicated, may hold values from 0.25 to 1.75
- output_weight: bfloat16 [1024, 1024], P('heads', 'shard'), may hold values from -1.5 to 1.5
- ffn_gain: bfloat16 [1024], P('shard'), may hold values from 0.25 to 1.75
- gate_weight: bfloat16 [1024, 4608], P('shard', 'tensor'), may hold values from -0.1875 to 0.1875
- up_weight: bfloat16 [1024, 4608], P('shard', 'tensor'), may hold values from -0.1875 to 0.1875
- down_weight: bfloat16 [4608, 1024], P('tensor', 'shard'), may hold values from -0.09375 to 0.09375
- lengths: int32 [16], replicated, may hold values from 8 to 1792, as said below
- packing: int32 [16], replicated, may hold values from 0 to 15, each once
- out_grad: bfloat16 [2048, 1024], P('shard'), may hold values from -6 to 6
Outputs:
- block_output: bfloat16 [2048, 1024], P('shard')
- input_grad: float32 [2048, 1024], P('shard')
- attn_gain_grad: float32 [1024], P('shard')
- query_weight_grad: float32 [1024, 1024], P('shard', 'heads')
- key_weight_grad: float32 [1024, 512], P('shard', 'heads')
- value_weight_grad: float32 [1024, 512], P('shard', 'heads')
- query_gain_grad: float32 [64], replicated
- key_gain_grad: float32 [64], replicated
- output_weight_grad: float32 [1024, 1024], P('heads', 'shard')
- ffn_gain_grad: float32 [1024], P('shard')
- gate_weight_grad: float32 [1024, 4608], P('shard', 'tensor')
- up_weight_grad: float32 [1024, 4608], P('shard', 'tensor')
- down_weight_grad: float32 [4608, 1024], P('tensor', 'shard')
Inputs may be any that keep to these rules, and one draw needn't show every extreme that they name: `lengths`: one sequence, at an index drawn from the seed, has exactly 1792 tokens; the other 15 have 8 to 16, one of them exactly 8; they are packed from slot 0 in the order of packing, and the slots after them are padding.
All inputs are finite; a program needn't handle non-finite values.
Results may differ from a plain program's by a relative error of at most 0.018.
Values may be sent and summed in bfloat16 or wider, within the bound.
No kernel may reach another device: no remote copies, remote signals or barrier semaphores. Data moves between devices by JAX's collectives and lax.ppermute only.
A program may use at most 128 MiB of HBM per device.

v0:
```python
import math

import jax
import jax.numpy as jnp
from jax import lax
from jax.sharding import PartitionSpec as P

EPSILON = 1e-05
ROPE_THETA = 1000000.0
MASKED_SCORE = -1e30


def scale_rows(values, gain_vector):
    return (
        values
        * lax.rsqrt(jnp.mean(values * values, axis=-1, keepdims=True) + EPSILON)
        * gain_vector
    )


def norm_back(values, gain_vector, upstream):
    factor = lax.rsqrt(jnp.mean(values * values, axis=-1, keepdims=True) + EPSILON)
    normed = values * factor
    weighted = upstream * gain_vector
    inner_mean = jnp.mean(weighted * normed, axis=-1, keepdims=True)
    lead_axes = tuple(range(values.ndim - 1))
    return (factor * (weighted - normed * inner_mean), jnp.sum(upstream * normed, axis=lead_axes))


def contract_rows(left_side, right_side):
    return lax.dot_general(
        left_side, right_side, (((0,), (0,)), ((), ())), preferred_element_type=jnp.float32
    )


def contract_cols(left_side, right_side):
    return lax.dot_general(
        left_side, right_side, (((1,), (1,)), ((), ())), preferred_element_type=jnp.float32
    )


def layout(lengths, packing, first_row, row_count):
    sequence_count = lengths.shape[0]
    chosen = (packing[:, None] == jnp.arange(sequence_count, dtype=jnp.int32)[None, :]).astype(
        jnp.int32
    )
    packed = jnp.sum(chosen * lengths[None, :], axis=1)
    seq_ends = jnp.cumsum(packed)
    token_index = first_row + jnp.arange(row_count, dtype=jnp.int32)
    passed = token_index[:, None] >= seq_ends[None, :]
    segment = jnp.sum(passed.astype(jnp.int32), axis=1)
    seq_start = jnp.sum(jnp.where(passed, packed[None, :], 0), axis=1)
    position = (token_index - seq_start).astype(jnp.float32)
    live_rows = segment < sequence_count
    return (token_index, segment, position, live_rows)


def rotary_tables(position, width):
    half_width = width // 2
    exponents = jnp.arange(half_width, dtype=jnp.float32) * (2.0 / width)
    frequency = jnp.power(jnp.float32(ROPE_THETA), -exponents)
    angles = position[:, None] * frequency[None, :]
    cosine_table = jnp.concatenate([jnp.cos(angles), jnp.cos(angles)], axis=-1)[:, None, :]
    sine_table = jnp.concatenate([jnp.sin(angles), jnp.sin(angles)], axis=-1)[:, None, :]
    return (cosine_table, sine_table)


def rotate(values, cosine_table, sine_table):
    half_width = values.shape[-1] // 2
    turned = jnp.concatenate([-values[..., half_width:], values[..., :half_width]], axis=-1)
    return values * cosine_table + turned * sine_table


def rotate_back(upstream, cosine_table, sine_table):
    half_width = upstream.shape[-1] // 2
    moved = upstream * sine_table
    turned = jnp.concatenate([moved[..., half_width:], -moved[..., :half_width]], axis=-1)
    return upstream * cosine_table + turned


def context_mask(query_index, query_segment, query_live, key_index, key_segment):
    same_seq = query_segment[:, None] == key_segment[None, :]
    causal = key_index[None, :] <= query_index[:, None]
    itself = key_index[None, :] == query_index[:, None]
    return same_seq & causal & (query_live[:, None] | itself)


def block_scores(queries, key_part, allowed, score_scale):
    score = (
        jnp.einsum("qgrd,kgd->grqk", queries, key_part, preferred_element_type=jnp.float32)
        * score_scale
    )
    return jnp.where(allowed[None, None], score, MASKED_SCORE)


def on_device(
    block_input,
    attn_gain,
    query_weight,
    key_weight,
    value_weight,
    query_gain,
    key_gain,
    output_weight,
    ffn_gain,
    gate_weight,
    up_weight,
    down_weight,
    lengths,
    packing,
    out_grad,
):
    row_count = block_input.shape[0]
    head_size = query_gain.shape[0]
    score_scale = 1.0 / math.sqrt(head_size)
    first_row = lax.axis_index("shard") * row_count
    query_index, query_segment, query_position, query_live = layout(
        lengths, packing, first_row, row_count
    )
    attn_full = (
        lax.all_gather(query_weight, "shard", axis=0, tiled=True),
        lax.all_gather(key_weight, "shard", axis=0, tiled=True),
        lax.all_gather(value_weight, "shard", axis=0, tiled=True),
        lax.all_gather(output_weight, "shard", axis=1, tiled=True),
        lax.all_gather(attn_gain, "shard", axis=0, tiled=True),
    )
    query_full, key_full, value_full, output_full, attn_scale = attn_full
    attn_scale = attn_scale.astype(jnp.float32)
    query_gain_f = query_gain.astype(jnp.float32)
    key_gain_f = key_gain.astype(jnp.float32)
    inputs = block_input.astype(jnp.float32)
    normed_one = scale_rows(inputs, attn_scale).astype(jnp.bfloat16)
    query_heads = jnp.dot(normed_one, query_full, preferred_element_type=jnp.float32).reshape(
        row_count, -1, head_size
    )
    key_heads = jnp.dot(normed_one, key_full, preferred_element_type=jnp.float32).reshape(
        row_count, -1, head_size
    )
    value_heads = (
        jnp.dot(normed_one, value_full, preferred_element_type=jnp.float32)
        .astype(jnp.bfloat16)
        .reshape(row_count, -1, head_size)
    )
    cosine_table, sine_table = rotary_tables(query_position, head_size)
    query_rot = rotate(scale_rows(query_heads, query_gain_f), cosine_table, sine_table).astype(
        jnp.bfloat16
    )
    key_rot = rotate(scale_rows(key_heads, key_gain_f), cosine_table, sine_table).astype(
        jnp.bfloat16
    )
    full_keys, full_values = (
        lax.all_gather(key_rot, "shard", axis=0, tiled=True),
        lax.all_gather(value_heads, "shard", axis=0, tiled=True),
    )
    total_rows = full_keys.shape[0]
    all_layout = layout(lengths, packing, 0, total_rows)
    all_index = all_layout[0]
    all_segment = all_layout[1]
    group_count = key_rot.shape[1]
    group_size = query_rot.shape[1] // group_count
    queries = query_rot.reshape(row_count, group_count, group_size, head_size)
    key_block = math.gcd(row_count, 512)
    block_count = (lax.axis_index("shard") + 1) * (row_count // key_block)

    def key_piece(block_number):
        start = block_number * key_block
        key_part = lax.dynamic_slice_in_dim(full_keys, start, key_block, 0)
        value_part = lax.dynamic_slice_in_dim(full_values, start, key_block, 0)
        key_index = lax.dynamic_slice_in_dim(all_index, start, key_block)
        key_segment = lax.dynamic_slice_in_dim(all_segment, start, key_block)
        allowed = context_mask(query_index, query_segment, query_live, key_index, key_segment)
        return (start, key_part, value_part, allowed)

    def total_step(block_number, carry):
        run_max, run_total = carry
        start, key_part, value_part, allowed = key_piece(block_number)
        score = block_scores(queries, key_part, allowed, score_scale)
        new_max = jnp.maximum(run_max, jnp.max(score, axis=-1))
        kept = jnp.where(allowed[None, None], jnp.exp(score - new_max[..., None]), 0.0)
        return (new_max, run_total * jnp.exp(run_max - new_max) + jnp.sum(kept, axis=-1))

    stat_shape = (group_count, group_size, row_count)
    run_max, run_total = lax.fori_loop(
        0,
        block_count,
        total_step,
        (jnp.full(stat_shape, MASKED_SCORE, jnp.float32), jnp.zeros(stat_shape, jnp.float32)),
    )
    log_total = run_max + jnp.log(run_total)

    def block_probs(block_number):
        start, key_part, value_part, allowed = key_piece(block_number)
        score = block_scores(queries, key_part, allowed, score_scale)
        probabilities = jnp.where(allowed[None, None], jnp.exp(score - log_total[..., None]), 0.0)
        return (start, key_part, value_part, probabilities)

    def output_step(block_number, total):
        start, key_part, value_part, probabilities = block_probs(block_number)
        return total + jnp.einsum(
            "grqk,kgd->qgrd",
            probabilities.astype(jnp.bfloat16),
            value_part,
            preferred_element_type=jnp.float32,
        )

    head_shape = (row_count, group_count, group_size, head_size)
    attended_heads = lax.fori_loop(0, block_count, output_step, jnp.zeros(head_shape, jnp.float32))
    attended = attended_heads.reshape(row_count, -1).astype(jnp.bfloat16)
    attn_part = jnp.dot(attended, output_full, preferred_element_type=jnp.float32)
    attn_out = lax.psum(attn_part, "heads")
    middle = inputs + attn_out
    ffn_full = (
        lax.all_gather(gate_weight, "shard", axis=0, tiled=True),
        lax.all_gather(up_weight, "shard", axis=0, tiled=True),
        lax.all_gather(down_weight, "shard", axis=1, tiled=True),
        lax.all_gather(ffn_gain, "shard", axis=0, tiled=True),
    )
    gate_full, up_full, down_full, ffn_scale = ffn_full
    ffn_scale = ffn_scale.astype(jnp.float32)
    normed_two = scale_rows(middle, ffn_scale).astype(jnp.bfloat16)
    gate_value = jnp.dot(normed_two, gate_full, preferred_element_type=jnp.float32)
    up_value = jnp.dot(normed_two, up_full, preferred_element_type=jnp.float32)
    sigmoid = jax.nn.sigmoid(gate_value)
    activated = gate_value * sigmoid
    hidden = (activated * up_value).astype(jnp.bfloat16)
    ffn_out = lax.psum(
        jnp.dot(hidden, down_full, preferred_element_type=jnp.float32).astype(jnp.bfloat16),
        "tensor",
    ).astype(jnp.float32)
    live_weight = query_live.astype(jnp.float32)[:, None]
    block_output = (live_weight * (middle + ffn_out)).astype(jnp.bfloat16)
    cotangent = out_grad.astype(jnp.float32) * live_weight
    ffn_grad_low = cotangent.astype(jnp.bfloat16)
    down_grad = contract_rows(hidden, ffn_grad_low)
    hidden_grad = contract_cols(ffn_grad_low, down_full)
    gate_grad_low = (
        hidden_grad * up_value * sigmoid * (1.0 + gate_value * (1.0 - sigmoid))
    ).astype(jnp.bfloat16)
    up_grad_low = (hidden_grad * activated).astype(jnp.bfloat16)
    gate_grad = contract_rows(normed_two, gate_grad_low)
    up_grad = contract_rows(normed_two, up_grad_low)
    norm_two_part = contract_cols(gate_grad_low, gate_full) + contract_cols(up_grad_low, up_full)
    norm_two_grad = lax.psum(norm_two_part.astype(jnp.bfloat16), "tensor").astype(jnp.float32)
    middle_back, ffn_gain_part = norm_back(middle, ffn_scale, norm_two_grad)
    middle_grad = cotangent + middle_back
    attn_grad_low = middle_grad.astype(jnp.bfloat16)
    output_grad = contract_rows(attended, attn_grad_low)
    attended_grad = (
        contract_cols(attn_grad_low, output_full).astype(jnp.bfloat16).reshape(head_shape)
    )

    def inner_step(block_number, row_inner):
        start, key_part, value_part, probabilities = block_probs(block_number)
        prob_grad = jnp.einsum(
            "qgrd,kgd->grqk", attended_grad, value_part, preferred_element_type=jnp.float32
        )
        return row_inner + jnp.sum(probabilities * prob_grad, axis=-1)

    row_inner = lax.fori_loop(0, block_count, inner_step, jnp.zeros(stat_shape, jnp.float32))

    def grad_step(block_number, carry):
        query_sum, key_sums, value_sums = carry
        start, key_part, value_part, probabilities = block_probs(block_number)
        prob_grad = jnp.einsum(
            "qgrd,kgd->grqk", attended_grad, value_part, preferred_element_type=jnp.float32
        )
        score_grad = (probabilities * (prob_grad - row_inner[..., None])).astype(jnp.bfloat16)
        query_sum = (
            query_sum
            + jnp.einsum("grqk,kgd->qgrd", score_grad, key_part, preferred_element_type=jnp.float32)
            * score_scale
        )
        key_piece_grad = (
            jnp.einsum("grqk,qgrd->kgd", score_grad, queries, preferred_element_type=jnp.float32)
            * score_scale
        )
        value_piece_grad = jnp.einsum(
            "grqk,qgrd->kgd",
            probabilities.astype(jnp.bfloat16),
            attended_grad,
            preferred_element_type=jnp.float32,
        )
        key_sums = lax.dynamic_update_slice_in_dim(
            key_sums,
            lax.dynamic_slice_in_dim(key_sums, start, key_block, 0) + key_piece_grad,
            start,
            0,
        )
        value_sums = lax.dynamic_update_slice_in_dim(
            value_sums,
            lax.dynamic_slice_in_dim(value_sums, start, key_block, 0) + value_piece_grad,
            start,
            0,
        )
        return (query_sum, key_sums, value_sums)

    empty_keys = jnp.zeros(full_keys.shape, jnp.float32)
    query_sum, key_sums, value_sums = lax.fori_loop(
        0, block_count, grad_step, (jnp.zeros(head_shape, jnp.float32), empty_keys, empty_keys)
    )
    query_rot_grad = query_sum.reshape(row_count, -1, head_size)
    key_total, value_total = (
        lax.psum_scatter(
            key_sums.astype(jnp.bfloat16), "shard", scatter_dimension=0, tiled=True
        ).astype(jnp.float32),
        lax.psum_scatter(
            value_sums.astype(jnp.bfloat16), "shard", scatter_dimension=0, tiled=True
        ).astype(jnp.float32),
    )
    query_normed_grad, query_gain_part = norm_back(
        query_heads, query_gain_f, rotate_back(query_rot_grad, cosine_table, sine_table)
    )
    key_normed_grad, key_gain_part = norm_back(
        key_heads, key_gain_f, rotate_back(key_total, cosine_table, sine_table)
    )
    query_grad_low = query_normed_grad.reshape(row_count, -1).astype(jnp.bfloat16)
    key_grad_low = key_normed_grad.reshape(row_count, -1).astype(jnp.bfloat16)
    value_grad_low = value_total.reshape(row_count, -1).astype(jnp.bfloat16)
    query_grad = contract_rows(normed_one, query_grad_low)
    key_grad = contract_rows(normed_one, key_grad_low)
    value_grad = contract_rows(normed_one, value_grad_low)
    norm_one_part = (
        contract_cols(query_grad_low, query_full)
        + contract_cols(key_grad_low, key_full)
        + contract_cols(value_grad_low, value_full)
    )
    norm_one_grad = lax.psum(norm_one_part.astype(jnp.bfloat16), "heads").astype(jnp.float32)
    input_back, attn_gain_part = norm_back(inputs, attn_scale, norm_one_grad)
    input_grad = middle_grad + input_back
    gain_sums = lax.psum((query_gain_part, key_gain_part), ("shard", "heads"))
    all_sums = (
        lax.psum_scatter(
            query_grad.astype(jnp.bfloat16), "shard", scatter_dimension=0, tiled=True
        ).astype(jnp.float32),
        lax.psum_scatter(
            key_grad.astype(jnp.bfloat16), "shard", scatter_dimension=0, tiled=True
        ).astype(jnp.float32),
        lax.psum_scatter(
            value_grad.astype(jnp.bfloat16), "shard", scatter_dimension=0, tiled=True
        ).astype(jnp.float32),
        lax.psum_scatter(
            output_grad.astype(jnp.bfloat16), "shard", scatter_dimension=1, tiled=True
        ).astype(jnp.float32),
        lax.psum_scatter(
            attn_gain_part.astype(jnp.bfloat16), "shard", scatter_dimension=0, tiled=True
        ).astype(jnp.float32),
        lax.psum_scatter(
            gate_grad.astype(jnp.bfloat16), "shard", scatter_dimension=0, tiled=True
        ).astype(jnp.float32),
        lax.psum_scatter(
            up_grad.astype(jnp.bfloat16), "shard", scatter_dimension=0, tiled=True
        ).astype(jnp.float32),
        lax.psum_scatter(
            down_grad.astype(jnp.bfloat16), "shard", scatter_dimension=1, tiled=True
        ).astype(jnp.float32),
        lax.psum_scatter(
            ffn_gain_part.astype(jnp.bfloat16), "shard", scatter_dimension=0, tiled=True
        ).astype(jnp.float32),
    )
    attn_sums = all_sums[:5]
    ffn_sums = all_sums[5:]
    return (
        block_output,
        input_grad,
        attn_sums[4],
        attn_sums[0],
        attn_sums[1],
        attn_sums[2],
        gain_sums[0],
        gain_sums[1],
        attn_sums[3],
        ffn_sums[3],
        ffn_sums[0],
        ffn_sums[1],
        ffn_sums[2],
    )


def solution(mesh):
    placed = (
        P("shard", None),
        P("shard"),
        P("shard", "heads"),
        P("shard", "heads"),
        P("shard", "heads"),
        P(),
        P(),
        P("heads", "shard"),
        P("shard"),
        P("shard", "tensor"),
        P("shard", "tensor"),
        P("tensor", "shard"),
        P(),
        P(),
        P("shard", None),
    )
    return jax.shard_map(
        on_device,
        mesh=mesh,
        in_specs=placed,
        out_specs=(
            P("shard", None),
            P("shard", None),
            P("shard"),
            P("shard", "heads"),
            P("shard", "heads"),
            P("shard", "heads"),
            P(),
            P(),
            P("heads", "shard"),
            P("shard"),
            P("shard", "tensor"),
            P("shard", "tensor"),
            P("tensor", "shard"),
        ),
        check_vma=False,
    )
```

profile of v0, /device:TPU:1, one launch (start us, length us, event | category | flops | bytes accessed | tf_op | source)
XLA Modules:
  0.0 833.5 jit_solution(10009039800744167310)
XLA Ops:
  10.8 10.0 %all-gather = bf16[4,1,256]{2,1,0:T(2,128)(2,1)S(1)} all-gather(bf16[1,1,256]{2,1,0:T(2,128)(2,1)S(1)} %reshape.566), channel_id=1, replica_groups=mesh['shard'=4,'heads'=2,'tensor'=4] {'shard'}, dimensions={0}, use_global_device_ids=true | all-gather | bytes 2560 | tf_op jit(solution)/shard_map/all_gather | solution.py:125
  22.0 20.4 %all_gather.36 = bf16[1024,256]{1,0:T(8,128)(2,1)S(1)} all-gather(bf16[256,256]{1,0:T(8,128)(2,1)} %param.26), channel_id=1, replica_groups=mesh['shard'=4,'heads'=2,'tensor'=4] {'shard'}, dimensions={0}, use_global_device_ids=true | all-gather | bytes 655360 | tf_op jit(solution)/shard_map/all_gather | solution.py:122
  45.2 12.4 %all_gather.34 = bf16[1024,256]{1,0:T(8,128)(2,1)S(1)} all-gather(bf16[256,256]{1,0:T(8,128)(2,1)S(1)} %copy-done.38), channel_id=1, replica_groups=mesh['shard'=4,'heads'=2,'tensor'=4] {'shard'}, dimensions={0}, use_global_device_ids=true | all-gather | bytes 655360 | tf_op jit(solution)/shard_map/all_gather | solution.py:123
  59.8 2.1 multiply_reduce_fusion.3
  63.2 15.5 %all-gather.12.cloned.1.call-done = bf16[2048,4,64]{0,2,1:T(8,128)(2,1)} async-done(((bf16[512,4,64]{0,2,1:T(8,128)(2,1)}), bf16[2048,4,64]{0,2,1:T(8,128)(2,1)}) %all-gather.12.cloned.1.call-update) | async-done | bytes 1048592 | tf_op jit(solution)/shard_map/all_gather | solution.py:152
  78.7 5.1 while.50
  79.3 2.4 fusion.210
  81.8 2.0 select_reduce_fusion.3
  83.9 24.7 %all-gather.10.cloned.1.call-done = bf16[2048,4,64]{0,2,1:T(8,128)(2,1)} async-done(((bf16[512,4,64]{0,2,1:T(8,128)(2,1)}), bf16[2048,4,64]{0,2,1:T(8,128)(2,1)}) %all-gather.10.cloned.1.call-update) | async-done | bytes 1048592 | tf_op jit(solution)/shard_map/all_gather | solution.py:153
  108.7 4.8 while.51
  109.3 4.2 fusion.215
  113.6 24.9 %all-gather.16.cloned.1.call-done = bf16[512,1024]{1,0:T(8,128)(2,1)} async-done(((bf16[512,256]{1,0:T(8,128)(2,1)}), bf16[512,1024]{1,0:T(8,128)(2,1)}) %all-gather.16.cloned.1.call-update) | async-done | bytes 1048592 | tf_op jit(solution)/shard_map/all_gather | solution.py:124
  138.5 3.3 fusion.133
  144.0 7.1 all-gather.1
  151.1 12.1 %all-reduce.9.cloned.1.call-done = f32[512,1024]{1,0:T(8,128)} async-done(((f32[512,1024]{1,0:T(8,128)}), f32[512,1024]{1,0:T(8,128)}) %all-reduce.9.cloned.1.call-update) | async-done | bytes 2097168 | tf_op jit(solution)/shard_map/psum | solution.py:210
  163.2 2.2 multiply_reduce_fusion
  166.6 49.3 %all-gather.20.cloned.1.call-done = bf16[1024,1152]{1,0:T(8,128)(2,1)} async-done(((bf16[256,1152]{1,0:T(8,128)(2,1)}), bf16[1024,1152]{1,0:T(8,128)(2,1)}) %all-gather.20.cloned.1.call-update) | async-done | bytes 2359312 | tf_op jit(solution)/shard_map/all_gather | solution.py:214
  216.0 4.9 fusion.135
  220.8 46.1 %all-gather.18.cloned.1.call-done = bf16[1024,1152]{1,0:T(8,128)(2,1)} async-done(((bf16[256,1152]{1,0:T(8,128)(2,1)}), bf16[1024,1152]{1,0:T(8,128)(2,1)}) %all-gather.18.cloned.1.call-update) | async-done | bytes 2359312 | tf_op jit(solution)/shard_map/all_gather | solution.py:213
  266.9 5.0 fusion.134
  271.9 45.8 %all-gather.22.cloned.1.call-done = bf16[1152,1024]{1,0:T(8,128)(2,1)} async-done(((bf16[1152,256]{1,0:T(8,128)(2,1)}), bf16[1152,1024]{1,0:T(8,128)(2,1)}) %all-gather.22.cloned.1.call-update) | async-done | bytes 2359312 | tf_op jit(solution)/shard_map/all_gather | solution.py:215
  317.7 5.8 multiply_convert_fusion
  323.5 2.5 convolution_convert_fusion.3
  328.5 2.6 add_convert_fusion.1
  331.1 68.5 %all-reduce.13.cloned.1.call-done = (bf16[512,1024]{1,0:T(8,128)(2,1)}, bf16[512,1024]{1,0:T(8,128)(2,1)}) async-done(((bf16[512,1024]{1,0:T(8,128)(2,1)}, bf16[512,1024]{1,0:T(8,128)(2,1)}), (bf16[512,1024]{1,0:T(8,128)(2,1)}, bf16[512,1024]{1,0:T(8,128)(2,1)})) %all-reduce.13.cloned.1.call-update) | async-done | bytes 2097168 | tf_op jit(solution)/shard_map/psum | solution.py:226
  399.6 2.7 fusion.100
  402.3 1.9 fusion.99
  406.2 6.4 while.52
  407.1 2.2 fusion.220
  409.3 3.3 fusion.221
  414.4 1.6 broadcast_in_dim.109
  416.0 14.3 %while.53 = (s32[]{:T(128)}, f32[512,4,2,64]{0,3,2,1:T(8,128)S(1)}, f32[2048,4,64]{0,2,1:T(8,128)}, f32[2048,4,64]{0,2,1:T(8,128)}, s32[]{:T(128)}, /*index=5*/b...) while((s32[]{:T(128)}, f32[512,4,2,64]{0,3,2,1:T(8,128)S(1)}, ...), condition=%wide.region_23.24_spmd.clone, body=%wide.region_22.23_spmd.clone.sunk | while | flops 1369833984 | bytes 62458684 | solution.py:298
  417.8 4.1 fusion.236
  422.0 4.0 fusion.233
  430.3 2.7 convert_element_type.216
  433.1 2.8 convert_element_type.220
  436.0 3.3 convolution_convert_fusion.4
  443.5 1.9 convolution_convert_fusion.5
  445.5 2.9 convolution_convert_fusion
  450.0 3.0 convolution_convert_fusion.2
  454.2 3.0 convolution_convert_fusion.1
  458.5 2.2 fusion.137
  460.6 61.3 %reduce-scatter.10.cloned.1.call-done = bf16[512,4,64]{0,2,1:T(8,128)(2,1)} async-done(((bf16[2048,4,64]{0,2,1:T(8,128)(2,1)}), bf16[512,4,64]{0,2,1:T(8,128)(2,1)}) %reduce-scatter.10.cloned.1.call-update) | async-done | bytes 262160 | tf_op jit(solution)/shard_map/reduce_scatter | solution.py:303
  523.0 27.1 %reduce-scatter.12.cloned.1.call-done = bf16[512,4,64]{0,2,1:T(8,128)(2,1)} async-done(((bf16[2048,4,64]{0,2,1:T(8,128)(2,1)}), bf16[512,4,64]{0,2,1:T(8,128)(2,1)}) %reduce-scatter.12.cloned.1.call-update) | async-done | bytes 262160 | tf_op jit(solution)/shard_map/reduce_scatter | solution.py:306
  550.2 2.4 convolution_convert_fusion.6
  559.1 19.0 %reduce-scatter.20.cloned.1.call-done = bf16[512,256]{1,0:T(8,128)(2,1)} async-done(((bf16[512,1024]{1,0:T(8,128)(2,1)}), bf16[512,256]{1,0:T(8,128)(2,1)}) %reduce-scatter.20.cloned.1.call-update) | async-done | bytes 262160 | tf_op jit(solution)/shard_map/reduce_scatter | solution.py:341
  578.1 1.8 convert_element_type.233
  579.9 26.5 %reduce-scatter.14.cloned.1.call-done = bf16[256,512]{1,0:T(8,128)(2,1)} async-done(((bf16[1024,512]{1,0:T(8,128)(2,1)}), bf16[256,512]{1,0:T(8,128)(2,1)}) %reduce-scatter.14.cloned.1.call-update) | async-done | bytes 262160 | tf_op jit(solution)/shard_map/reduce_scatter | solution.py:332
  606.4 1.8 convert_element_type.227
  608.2 14.9 %all-reduce.2 = (f32[64]{0:T(128)}, f32[64]{0:T(128)}) all-reduce(f32[64]{0:T(128)S(1)} %get-tuple-element.441, f32[64]{0:T(128)S(1)} %get-tuple-element.445), channel_id=1, replica_groups=mesh['shard'=4,'heads'=2,'tensor'=4] {'shard','heads'}, use_global_device_ids=true, to_apply=%region_36.37 | all-reduce | flops 128 | bytes 1024 | tf_op jit(solution)/shard_map/psum | solution.py:330
  623.1 32.2 %reduce-scatter.26.cloned.1.call-done = bf16[1152,256]{1,0:T(8,128)(2,1)} async-done(((bf16[1152,1024]{1,0:T(8,128)(2,1)}), bf16[1152,256]{1,0:T(8,128)(2,1)}) %reduce-scatter.26.cloned.1.call-update) | async-done | bytes 589840 | tf_op jit(solution)/shard_map/reduce_scatter | solution.py:353
  655.3 2.2 convert_element_type.241
  657.5 47.6 %reduce-scatter.22.cloned.1.call-done = bf16[256,1152]{1,0:T(8,128)(2,1)} async-done(((bf16[1024,1152]{1,0:T(8,128)(2,1)}), bf16[256,1152]{1,0:T(8,128)(2,1)}) %reduce-scatter.22.cloned.1.call-update) | async-done | bytes 589840 | tf_op jit(solution)/shard_map/reduce_scatter | solution.py:347
  705.1 2.2 convert_element_type.237
  707.2 47.6 %reduce-scatter.24.cloned.1.call-done = bf16[256,1152]{1,0:T(8,128)(2,1)} async-done(((bf16[1024,1152]{1,0:T(8,128)(2,1)}), bf16[256,1152]{1,0:T(8,128)(2,1)}) %reduce-scatter.24.cloned.1.call-update) | async-done | bytes 589840 | tf_op jit(solution)/shard_map/reduce_scatter | solution.py:350
  754.8 2.2 convert_element_type.239
  756.9 19.6 %reduce-scatter.18.cloned.1.call-done = bf16[256,256]{1,0:T(8,128)(2,1)} async-done(((bf16[1024,256]{1,0:T(8,128)(2,1)}), bf16[256,256]{1,0:T(8,128)(2,1)}) %reduce-scatter.18.cloned.1.call-update) | async-done | bytes 131088 | tf_op jit(solution)/shard_map/reduce_scatter | solution.py:338
  776.5 1.6 convert_element_type.231
  778.1 20.7 %all-reduce.11.cloned.1.call-done = bf16[512,1024]{1,0:T(8,128)(2,1)} async-done(((bf16[512,1024]{1,0:T(8,128)(2,1)}), bf16[512,1024]{1,0:T(8,128)(2,1)}) %all-reduce.11.cloned.1.call-update) | async-done | bytes 1048592 | tf_op jit(solution)/shard_map/psum | solution.py:327
  798.8 2.0 fusion.103
  800.8 10.1 %all-reduce.4 = (bf16[1024]{0:T(1024)(128)(2,1)S(1)}, bf16[1024]{0:T(1024)(128)(2,1)S(1)}) all-reduce(bf16[1024]{0:T(1024)(128)(2,1)S(1)} %get-tuple-element.443, bf16[1024]{0:T(1024)(128)(2,1)S(1)} %copy-done.45), channel_id=4, replica_groups=mesh['shard'=4,'heads'=2,'tensor'=4] {'shard'}, use_global_device_ids=true, to_apply=%region_31.32.clone | all-reduce | flops 2048 | bytes 8192
  812.2 9.5 %reduce-scatter.16.cloned.1.call-done = bf16[256,256]{1,0:T(8,128)(2,1)} async-done(((bf16[1024,256]{1,0:T(8,128)(2,1)}), bf16[256,256]{1,0:T(8,128)(2,1)}) %reduce-scatter.16.cloned.1.call-update) | async-done | bytes 131088 | tf_op jit(solution)/shard_map/reduce_scatter | solution.py:335
  821.8 1.6 convert_element_type.229
  823.4 3.1 fusion.96
  (257 shorter events, 44.9 us)
Async XLA Ops:
  7.2 35.6 %copy-start.6 = (bf16[512,1024]{1,0:T(8,128)(2,1)S(1)}, bf16[512,1024]{1,0:T(8,128)(2,1)}, u32[]{:S(2)}) copy-start(bf16[512,1024]{1,0:T(8,128)(2,1)} %param.23) | copy-start | bytes 3145732
  7.2 52.5 %all-gather.14.cloned.1.call-start = ((), (), s32[]{:S(2)}) async-start(), calls=%async_computation.11 | async-start | bytes 1310720 | tf_op jit(solution)/shard_map/all_gather | solution.py:121
  7.9 70.8 %all-gather.12.cloned.1.call-start = ((), (), s32[]{:S(2)}) async-start(), calls=%async_computation.10 | async-start | bytes 1310720 | tf_op jit(solution)/shard_map/all_gather | solution.py:152
  8.7 35.0 %copy-start.43 = (f32[64]{0:T(128)}, f32[64]{0:T(128)S(1)}, u32[]{:S(2)}) copy-start(f32[64]{0:T(128)S(1)} %convert_element_type.194) | copy-start | bytes 772
  20.8 38.9 %copy-start.39 = (f32[4,1,256]{2,1,0:T(1,128)}, f32[4,1,256]{2,1,0:T(1,128)S(1)}, u32[]{:S(2)}) copy-start(f32[4,1,256]{2,1,0:T(1,128)S(1)} %convert_element_type.242) | copy-start | bytes 12292
  42.8 20.0 %copy-start.13 = (f32[512,64]{0,1:T(8,128)}, f32[512,64]{0,1:T(8,128)S(1)}, u32[]{:S(2)}) copy-start(f32[512,64]{0,1:T(8,128)S(1)} %get-tuple-element.584) | copy-start | bytes 393220
  42.8 19.9 %copy-start.19 = (f32[512,64]{0,1:T(8,128)}, f32[512,64]{0,1:T(8,128)S(1)}, u32[]{:S(2)}) copy-start(f32[512,64]{0,1:T(8,128)S(1)} %get-tuple-element.585) | copy-start | bytes 393220
  42.8 16.9 %copy-start.41 = (f32[512]{0:T(512)}, f32[512]{0:T(512)S(1)}, u32[]{:S(2)}) copy-start(f32[512]{0:T(512)S(1)} %add_rsqrt_fusion.3) | copy-start | bytes 6148
  43.5 1.8 copy-start.38
  43.5 14.1 %copy-start.34 = (f32[512,4]{0,1:T(4,128)}, f32[512,4]{0,1:T(4,128)S(1)}, u32[]{:S(2)}) copy-start(f32[512,4]{0,1:T(4,128)S(1)} %add_rsqrt_fusion.1) | copy-start | bytes 24580
  45.1 14.5 %copy-start.50 = (bf16[64]{0:T(256)(128)(2,1)S(1)}, bf16[64]{0:T(256)(128)(2,1)}, u32[]{:S(2)}) copy-start(bf16[64]{0:T(256)(128)(2,1)} %param.28) | copy-start | bytes 388
  45.2 63.4 %all-gather.10.cloned.1.call-start = ((), (), s32[]{:S(2)}) async-start(), calls=%async_computation.9 | async-start | bytes 1310720 | tf_op jit(solution)/shard_map/all_gather | solution.py:153
  57.6 2.1 copy-start.22
  58.9 79.6 %all-gather.16.cloned.1.call-start = ((), (), s32[]{:S(2)}) async-start(), calls=%async_computation.12 | async-start | bytes 1310720 | tf_op jit(solution)/shard_map/all_gather | solution.py:124
  59.5 103.7 %all-reduce.9.cloned.1.call-start = ((), (), s32[]{:S(2)}) async-start(), calls=%async_computation.13 | async-start | bytes 4194304 | tf_op jit(solution)/shard_map/psum | solution.py:210
  59.7 3.1 copy-start.48
  59.7 342.5 %copy-start.46 = (f32[512]{0:T(512)}, f32[512]{0:T(512)S(1)}, u32[]{:S(2)}) copy-start(f32[512]{0:T(512)S(1)} %get-tuple-element.559) | copy-start | bytes 6148
  113.6 28.2 %copy-start.15 = (bf16[512,4,2,64]{0,3,2,1:T(8,128)(2,1)}, bf16[512,4,2,64]{0,3,2,1:T(8,128)(2,1)S(1)}, u32[]{:S(2)}) copy-start(bf16[512,4,2,64]{0,3,2,1:T(8,128)(2,1)S(1)} %convert_element_type.199) | copy-start | bytes 1572868
  141.8 2.2 copy-start.55
  141.8 74.1 %all-gather.20.cloned.1.call-start = ((), (), s32[]{:S(2)}) async-start(), calls=%async_computation.15 | async-start | bytes 2949120 | tf_op jit(solution)/shard_map/all_gather | solution.py:214
  142.4 124.5 %all-gather.18.cloned.1.call-start = ((), (), s32[]{:S(2)}) async-start(), calls=%async_computation.14 | async-start | bytes 2949120 | tf_op jit(solution)/shard_map/all_gather | solution.py:213
  143.1 174.5 %all-gather.22.cloned.1.call-start = ((), (), s32[]{:S(2)}) async-start(), calls=%async_computation.16 | async-start | bytes 2949120 | tf_op jit(solution)/shard_map/all_gather | solution.py:215
  143.9 255.7 %all-reduce.13.cloned.1.call-start = ((), (), s32[]{:S(2)}) async-start(), calls=%async_computation.27 | async-start | bytes 4194304 | tf_op jit(solution)/shard_map/psum | solution.py:226
  317.7 5.8 copy-start.54
  323.5 2.6 copy-start.59
  323.5 2.5 copy-start.61
  323.5 4.9 copy-start.57
  323.5 3.3 copy-start.53
  326.8 1.7 copy-start.52
  331.0 190.9 %reduce-scatter.10.cloned.1.call-start = ((), (), s32[]{:S(2)}) async-start(), calls=%async_computation.17 | async-start | bytes 1310720 | tf_op jit(solution)/shard_map/reduce_scatter | solution.py:303
  399.6 2.7 copy-start.18
  399.6 2.7 copy-start.28
  399.6 2.7 copy-start.30
  402.3 3.2 copy-start.17
  404.1 2.1 copy-start.9
  426.0 1.6 copy-start.4
  429.0 1.4 copy-start.5
  433.1 117.1 %reduce-scatter.12.cloned.1.call-start = ((), (), s32[]{:S(2)}) async-start(), calls=%async_computation.18 | async-start | bytes 1310720 | tf_op jit(solution)/shard_map/reduce_scatter | solution.py:306
  433.1 2.9 copy-start.16
  436.0 3.7 copy-start.51
  436.0 3.8 copy-start.20
  436.0 142.1 %reduce-scatter.20.cloned.1.call-start = ((), (), s32[]{:S(2)}) async-start(), calls=%async_computation.23 | async-start | bytes 1310720 | tf_op jit(solution)/shard_map/reduce_scatter | solution.py:341
  439.4 167.0 %reduce-scatter.14.cloned.1.call-start = ((), (), s32[]{:S(2)}) async-start(), calls=%async_computation.20 | async-start | bytes 1310720 | tf_op jit(solution)/shard_map/reduce_scatter | solution.py:332
  443.4 2.0 copy-start.29
  443.4 2.0 copy-start.47
  443.4 2.0 copy-start.60
  445.4 210.0 %reduce-scatter.26.cloned.1.call-start = ((), (), s32[]{:S(2)}) async-start(), calls=%async_computation.26 | async-start | bytes 2949120 | tf_op jit(solution)/shard_map/reduce_scatter | solution.py:353
  448.4 1.6 copy-start.62
  448.4 256.7 %reduce-scatter.22.cloned.1.call-start = ((), (), s32[]{:S(2)}) async-start(), calls=%async_computation.24 | async-start | bytes 2949120 | tf_op jit(solution)/shard_map/reduce_scatter | solution.py:347
  453.0 301.8 %reduce-scatter.24.cloned.1.call-start = ((), (), s32[]{:S(2)}) async-start(), calls=%async_computation.25 | async-start | bytes 2949120 | tf_op jit(solution)/shard_map/reduce_scatter | solution.py:350
  457.3 92.9 %copy-start.8 = (bf16[512,1024]{1,0:T(8,128)(2,1)S(1)}, bf16[512,1024]{1,0:T(8,128)(2,1)}, u32[]{:S(2)}) copy-start(bf16[512,1024]{1,0:T(8,128)(2,1)} %param.23) | copy-start | bytes 3145732
  457.3 319.2 %reduce-scatter.18.cloned.1.call-start = ((), (), s32[]{:S(2)}) async-start(), calls=%async_computation.22 | async-start | bytes 655360 | tf_op jit(solution)/shard_map/reduce_scatter | solution.py:338
  523.0 29.7 %copy-start.11 = (f32[512,256]{0,1:T(8,128)S(1)}, f32[512,256]{0,1:T(8,128)}, u32[]{:S(2)}) copy-start(f32[512,256]{0,1:T(8,128)} %copy-done.10) | copy-start | bytes 1572868
  523.0 29.7 %copy-start.21 = (bf16[512,4,64]{0,2,1:T(8,128)(2,1)S(1)}, bf16[512,4,64]{0,2,1:T(8,128)(2,1)}, u32[]{:S(2)}) copy-start(bf16[512,4,64]{0,2,1:T(8,128)(2,1)} %reduce-scatter.10.cloned.1.call-done) | copy-start | bytes 786436
  523.0 29.7 %copy-start.35 = (f32[512,4]{0,1:T(4,128)S(1)}, f32[512,4]{0,1:T(4,128)}, u32[]{:S(2)}) copy-start(f32[512,4]{0,1:T(4,128)} %copy-done.34) | copy-start | bytes 24580
  523.0 29.7 %copy-start.44 = (f32[64]{0:T(128)S(1)}, f32[64]{0:T(128)}, u32[]{:S(2)}) copy-start(f32[64]{0:T(128)} %copy-done.43) | copy-start | bytes 772
  552.6 246.2 %all-reduce.11.cloned.1.call-start = ((), (), s32[]{:S(2)}) async-start(), calls=%async_computation.19 | async-start | bytes 2097152 | tf_op jit(solution)/shard_map/psum | solution.py:327
  553.0 1.6 copy-start.12
  553.0 1.7 copy-start.23
  553.0 1.8 copy-start.33
  556.3 1.6 copy-start.56
  556.3 265.4 %reduce-scatter.16.cloned.1.call-start = ((), (), s32[]{:S(2)}) async-start(), calls=%async_computation.21 | async-start | bytes 655360 | tf_op jit(solution)/shard_map/reduce_scatter | solution.py:335
  707.2 93.6 %copy-start.45 = (bf16[1024]{0:T(1024)(128)(2,1)S(1)}, bf16[1024]{0:T(1024)(128)(2,1)}, u32[]{:S(2)}) copy-start(bf16[1024]{0:T(1024)(128)(2,1)} %get-tuple-element.439) | copy-start | bytes 6148
  707.2 116.2 %copy-start.1 = (f32[512,1024]{1,0:T(8,128)S(1)}, f32[512,1024]{1,0:T(8,128)}, u32[]{:S(2)}) copy-start(f32[512,1024]{1,0:T(8,128)} %copy-done) | copy-start | bytes 6291460
  (18 other events, 20.1 us)
Sparse Core Ops, SparseCore 0:
  9.6 38.2 all-gather.13
  50.0 28.6 all-gather.11
  80.9 27.6 all-gather.9
  110.0 28.4 all-gather.15
  141.9 21.2 all-reduce.8
  164.7 51.2 all-gather.19
  217.6 49.2 all-gather.17
  268.6 49.0 all-gather.21
  331.2 68.3 all-reduce.12
  433.2 88.7 reduce-scatter.9
  524.3 25.7 reduce-scatter.11
  552.3 25.7 reduce-scatter.19
  580.5 25.8 reduce-scatter.13
  608.5 46.7 reduce-scatter.25
  657.5 47.5 reduce-scatter.21
  707.2 47.5 reduce-scatter.23
  756.9 19.5 reduce-scatter.17
  778.7 20.0 all-reduce.10
  801.2 20.5 reduce-scatter.15
where the time goes:
time: 846 us; the launch traced here: 834 us
  waiting for transfers between devices  601 us (71%)
  matrix products  76.3 us (9%)
  blocking collectives  74.9 us (9%)
  other arithmetic  45.3 us (5%)
  local copies, waits for them, and re-layouts  18.3 us (2%)
  between operations  15.9 us (2%)
    psum x1, waiting for transfers between devices, on_device(): lax.psum(jnp.dot(hidden, down_full, preferred_element_type=jnp.float32).a...  68.5 us
    reduce_scatter x1, waiting for transfers between devices, on_device(): lax.psum_scatter(key_sums.astype(jnp.bfloat16), 'shard', scatter_dimensio...  61.3 us
    all_gather x1, waiting for transfers between devices, on_device(): lax.all_gather(up_weight, 'shard', axis=0, tiled=True)  49.3 us
    reduce_scatter x1, waiting for transfers between devices, on_device(): lax.psum_scatter(up_grad.astype(jnp.bfloat16), 'shard', scatter_dimension...  47.6 us
    reduce_scatter x1, waiting for transfers between devices, on_device(): lax.psum_scatter(gate_grad.astype(jnp.bfloat16), 'shard', scatter_dimensi...  47.6 us
    all_gather x1, waiting for transfers between devices, on_device(): lax.all_gather(gate_weight, 'shard', axis=0, tiled=True)  46.1 us
    all_gather x1, waiting for transfers between devices, on_device(): lax.all_gather(down_weight, 'shard', axis=1, tiled=True)  45.8 us
    reduce_scatter x1, waiting for transfers between devices, on_device(): lax.psum_scatter(down_grad.astype(jnp.bfloat16), 'shard', scatter_dimensi...  32.2 us
  transfers between devices with their start and end apart: 19, of which 18 were waited for; matrix products, arithmetic and copies ran while one was open for 9% of the time, Pallas kernels for 0%

commit v1 on v0

v1 whole, which is shorter than its diff:
```python
import math

import jax
import jax.numpy as jnp
from jax import lax
from jax.experimental import pallas as pl
from jax.experimental.pallas import tpu as pltpu
from jax.sharding import PartitionSpec as P

EPSILON = 1e-05
ROPE_THETA = 1000000.0
BF = jnp.bfloat16
F32 = jnp.float32
MIB = 1 << 20
GAIN_ROWS = 16


def nn_dot(a, b):
    return lax.dot_general(a, b, (((1,), (0,)), ((), ())), preferred_element_type=F32)


def nt_dot(a, b):
    return lax.dot_general(a, b, (((1,), (1,)), ((), ())), preferred_element_type=F32)


def tn_dot(a, b):
    return lax.dot_general(a, b, (((0,), (0,)), ((), ())), preferred_element_type=F32)


def call(kernel, outs, ids, arrays, scratch=(), vmem=32, flops=0, name=None):
    shapes = [jax.ShapeDtypeStruct(s, d) for s, d in outs]
    moved = sum(a.size * a.dtype.itemsize for a in arrays)
    moved += sum(math.prod(s.shape) * s.dtype.itemsize for s in shapes)
    return pl.pallas_call(
        kernel,
        out_shape=shapes,
        in_specs=[pl.BlockSpec(memory_space=pltpu.SMEM)]
        + [pl.BlockSpec(memory_space=pltpu.VMEM) for _ in arrays],
        out_specs=[pl.BlockSpec(memory_space=pltpu.VMEM) for _ in shapes],
        scratch_shapes=list(scratch),
        compiler_params=pltpu.CompilerParams(vmem_limit_bytes=vmem * MIB),
        cost_estimate=pl.CostEstimate(flops=int(flops), bytes_accessed=int(moved), transcendentals=0),
        name=name,
    )(ids, *arrays)


def lanes(shape):
    return lax.broadcasted_iota(jnp.int32, shape, 1)


def head_mean(v, low):
    first = jnp.sum(jnp.where(low, v, 0.0), axis=1, keepdims=True)
    second = jnp.sum(jnp.where(low, 0.0, v), axis=1, keepdims=True)
    return jnp.where(low, first, second) * (1.0 / 64.0)


def turn(v, first):
    return jnp.where(first, -pltpu.roll(v, 96, 1), pltpu.roll(v, 32, 1))


def turn_back(v, first):
    return jnp.where(first, pltpu.roll(v, 96, 1), -pltpu.roll(v, 32, 1))


def make(mesh):
    n_shard, n_heads, n_tensor = (mesh.shape[a] for a in ("shard", "heads", "tensor"))
    blocks_mode = n_shard == 4
    n_plane = n_heads * n_tensor

    def swap(x, axis, k):
        size = mesh.shape[axis]
        return lax.ppermute(x, axis, [(i, i ^ k) for i in range(size)])

    def shard_blocks(x, staged):
        one, two = swap(x, "shard", 1), swap(x, "shard", 2)
        three = swap(two, "shard", 1) if staged else swap(x, "shard", 3)
        return [x, one, two, three]

    def plane_blocks(x):
        same = [x] + [swap(x, "tensor", k) for k in range(1, n_tensor)]
        found = list(same)
        for i in range(1, n_heads):
            found += [swap(s, "heads", i) for s in same]
        return found

    def plane_index(ids, b):
        return (ids[1] ^ (b // n_tensor)) * n_tensor + (ids[2] ^ (b % n_tensor))

    def on_device(
        block_input,
        attn_gain,
        query_weight,
        key_weight,
        value_weight,
        query_gain,
        key_gain,
        output_weight,
        ffn_gain,
        gate_weight,
        up_weight,
        down_weight,
        lengths,
        packing,
        out_grad,
    ):
        rows, width = block_input.shape
        depth = query_weight.shape[0]
        head = query_gain.shape[0]
        hidden_all = gate_weight.shape[1]
        hid = hidden_all // n_heads
        q_cols = query_weight.shape[1] // n_tensor
        k_cols = key_weight.shape[1] // n_tensor
        n_block = n_shard if blocks_mode else 1
        wide = width // n_block
        sub = rows // n_plane
        half = rows // n_heads
        z, h, t = (lax.axis_index(a) for a in ("shard", "heads", "tensor"))
        ids = jnp.stack([z, h, t]).astype(jnp.int32)

        def owner(ids_ref, k):
            return ids_ref[0] ^ k

        def offset(ids_ref, k):
            return pl.multiple_of(owner(ids_ref, k) * wide, wide) if blocks_mode else 0

        count = lengths.shape[0]
        order = jnp.arange(count, dtype=jnp.int32)
        packed = jnp.sum(jnp.where(packing[:, None] == order[None, :], lengths[None, :], 0), axis=1)
        ends = jnp.sum(jnp.where(order[None, :] <= order[:, None], packed[None, :], 0), axis=1)
        token = z * rows + jnp.arange(rows, dtype=jnp.int32)
        passed = token[:, None] >= ends[None, :]
        segment = jnp.sum(passed.astype(jnp.int32), axis=1)
        start = jnp.sum(jnp.where(passed, packed[None, :], 0), axis=1)
        live = segment < count
        lowest = jnp.where(live, start, token)
        row_info = jnp.where(
            lax.broadcasted_iota(jnp.int32, (rows, 128), 1) == 0,
            lowest[:, None].astype(F32),
            live[:, None].astype(F32),
        )
        exponents = jnp.arange(head // 2, dtype=F32) * (2.0 / head)
        frequency = jnp.power(jnp.float32(ROPE_THETA), -exponents)
        angles = (token - start).astype(F32)[:, None] * jnp.tile(frequency, 4)[None, :]
        cosine, sine = jnp.cos(angles), jnp.sin(angles)
        head_gains = jnp.broadcast_to(
            jnp.stack(
                [
                    jnp.tile(query_gain.astype(F32), 2),
                    jnp.concatenate([key_gain.astype(F32), jnp.ones((head,), F32)]),
                ]
            )[:, None, :],
            (2, 8, 128),
        ).reshape(16, 128)

        own_qkv = jnp.concatenate(
            [
                lax.dynamic_slice_in_dim(query_weight, t * q_cols, q_cols, 1),
                lax.dynamic_slice_in_dim(key_weight, t * k_cols, k_cols, 1),
                lax.dynamic_slice_in_dim(value_weight, t * k_cols, k_cols, 1),
            ],
            axis=1,
        )
        own_out = lax.dynamic_slice_in_dim(output_weight, t * q_cols, q_cols, 0)
        first_core = h == 0
        own_gate_up = jnp.where(
            first_core,
            jnp.concatenate([gate_weight[:, :hid], up_weight[:, :hid]], axis=1),
            jnp.concatenate([gate_weight[:, hid:], up_weight[:, hid:]], axis=1),
        )
        own_down = lax.dynamic_slice_in_dim(down_weight, h * hid, hid, 0)
        gains = jnp.concatenate(
            [attn_gain[None], ffn_gain[None], jnp.zeros((GAIN_ROWS - 2, depth), BF)], axis=0
        )
        if blocks_mode:
            qkv_parts = shard_blocks(jnp.concatenate([own_qkv, gains], axis=0), False)
            gain_parts = []
            out_parts = shard_blocks(own_out, False)
            gate_up_parts = shard_blocks(own_gate_up, True)
            down_parts = shard_blocks(own_down, True)
        else:
            gather = lambda x, axis: [lax.all_gather(x, "shard", axis=axis, tiled=True)]
            qkv_parts = gather(own_qkv, 0)
            gain_parts = gather(gains, 1)
            out_parts = gather(own_out, 1)
            gate_up_parts = gather(own_gate_up, 0)
            down_parts = gather(own_down, 1)

        def project(ids_ref, x_ref, cos_ref, sin_ref, hg_ref, *refs):
            w_refs, refs = refs[:n_block], refs[n_block:]
            g_refs, refs = refs[: len(gain_parts)], refs[len(gain_parts) :]
            n_ref, raw_ref, qs_ref, kv_ref, ga_ref, gf_ref = refs
            for k in range(n_block):
                both = (g_refs[0][...] if g_refs else w_refs[k][wide:, :]).astype(F32)
                where = pl.ds(offset(ids_ref, k), wide)
                ga_ref[:, where] = jnp.broadcast_to(both[0:1], (8, wide))
                gf_ref[:, where] = jnp.broadcast_to(both[1:2], (8, wide))
            step = 128

            def body(c, carry):
                at = pl.ds(pl.multiple_of(c * step, step), step)
                x = x_ref[at, :].astype(F32)
                r = lax.rsqrt(jnp.mean(x * x, axis=1, keepdims=True) + EPSILON)
                n_ref[at, :] = (x * r * ga_ref[0:1, :]).astype(BF)
                acc = jnp.zeros((step, 256), F32)
                for k in range(n_block):
                    acc += nn_dot(n_ref[at, pl.ds(offset(ids_ref, k), wide)], w_refs[k][:wide, :])
                raw_ref[at, :] = acc
                lane = lanes((step, 128))
                low, first = lane < 64, (lane % 64) < 32
                cos, sin = cos_ref[at, :], sin_ref[at, :]
                q, kv = acc[:, :128], acc[:, 128:]
                q = q * lax.rsqrt(head_mean(q * q, low) + EPSILON) * hg_ref[0:1, :]
                q = (q * cos + turn(q, first) * sin).astype(BF).astype(F32) * (1.0 / math.sqrt(head))
                qs_ref[at, :] = jnp.where(low, q, 0.0).astype(BF)
                qs_ref[pl.ds(pl.multiple_of(rows + c * step, step), step), :] = jnp.where(
                    low, pltpu.roll(q, 64, 1), 0.0
                ).astype(BF)
                k_ = kv * lax.rsqrt(head_mean(kv * kv, low) + EPSILON) * hg_ref[8:9, :]
                k_ = k_ * cos + turn(k_, first) * sin
                kv_ref[at, :] = jnp.where(low, k_, kv).astype(BF)
                return carry

            lax.fori_loop(0, rows // step, body, 0)

        normed_one, raw, queries, own_kv, ga, gf = call(
            project,
            [
                ((rows, width), BF),
                ((rows, 256), F32),
                ((2 * rows, 128), BF),
                ((rows, 128), BF),
                ((8, width), F32),
                ((8, width), F32),
            ],
            ids,
            [block_input, cosine, sine, head_gains, *qkv_parts, *gain_parts],
            flops=2 * rows * width * 256,
            vmem=24,
            name="project",
        )
        if blocks_mode:
            kv_parts = shard_blocks(own_kv, False)
        else:
            kv_parts = [lax.all_gather(own_kv, "shard", axis=0, tiled=True)]

        chunk = 256

        def over_keys(ids_ref, kv_refs, block):
            if blocks_mode:
                for k in range(n_block):
                    pl.when(owner(ids_ref, k) <= ids_ref[0])(
                        lambda k=k: block(owner(ids_ref, k), kv_refs[k], 0)
                    )
            else:

                def step(j, carry):
                    block(j, kv_refs[0], pl.multiple_of(j * rows, rows))
                    return carry

                lax.fori_loop(0, ids_ref[0] + 1, step, 0)

        def masked_exp(ids_ref, info_ref, score, c, own):
            row = (c * chunk) % rows
            at = pl.ds(pl.multiple_of(row, chunk), chunk)
            col = lanes((chunk, rows))
            lowest_ = info_ref[at, 0:1].astype(jnp.int32) - own * rows
            mine = lax.broadcasted_iota(jnp.int32, (chunk, 1), 0) + (row + (ids_ref[0] - own) * rows)
            return jnp.where((col >= lowest_) & (col <= mine), jnp.exp(score), 0.0)

        def attend(ids_ref, info_ref, qs_ref, *refs):
            kv_refs, (att_ref, oa_ref, acc_ref) = refs[:n_block], refs[n_block:]
            acc_ref[...] = jnp.zeros_like(acc_ref)
            low = lanes((rows, 128)) < 64

            def block(own, kv_ref, base):
                kv = kv_ref[pl.ds(base, rows), :]
                counted = jnp.where(low, 1.0, kv.astype(F32)).astype(BF)

                def body(c, carry):
                    at = pl.ds(pl.multiple_of(c * chunk, chunk), chunk)
                    p = masked_exp(ids_ref, info_ref, nt_dot(qs_ref[at, :], kv), c, own)
                    acc_ref[at, :] += nn_dot(p.astype(BF), counted)
                    return carry

                lax.fori_loop(0, 2 * rows // chunk, body, 0)

            over_keys(ids_ref, kv_refs, block)
            for i in range(2):
                acc = acc_ref[i * rows : (i + 1) * rows, :]
                inverse = 1.0 / jnp.where(low, acc, 1.0)
                done = jnp.where(low, inverse, acc * pltpu.roll(inverse, 64, 1))
                oa_ref[i * rows : (i + 1) * rows, :] = done
            att_ref[...] = jnp.where(
                low, pltpu.roll(oa_ref[:rows, :], 64, 1), oa_ref[rows:, :]
            ).astype(BF)

        attended, out_and_inverse = call(
            attend,
            [((rows, 128), BF), ((2 * rows, 128), F32)],
            ids,
            [row_info, queries, *kv_parts],
            scratch=[pltpu.VMEM((2 * rows, 128), F32)],
            flops=4 * 2 * rows * rows * n_shard * 128,
            vmem=32,
            name="attend",
        )
        attended_parts = plane_blocks(attended)

        if blocks_mode:

            def beside(ids_ref, *refs):
                for k in range(n_block):
                    refs[-1][:, pl.ds(offset(ids_ref, k), wide)] = refs[k][...]

            (own_rows,) = call(beside, [((q_cols, width), BF)], ids, out_parts, vmem=8, name="beside")
        else:
            own_rows = out_parts[0]
        row_parts = plane_blocks(own_rows)

        def below(ids_ref, *refs):
            for b in range(n_plane):
                at = pl.multiple_of(plane_index(ids_ref, b) * q_cols, q_cols)
                refs[-1][pl.ds(at, q_cols), :] = refs[b][...]

        (out_full,) = call(below, [((width, width), BF)], ids, row_parts, vmem=12, name="below")

        def middle_part(ids_ref, info_ref, x_ref, og_ref, gf_ref, wo_ref, *refs):
            a_refs, refs = refs[:n_plane], refs[n_plane:]
            gu_refs, refs = refs[:n_block], refs[n_block:]
            dn_refs, refs = refs[:n_block], refs[n_block:]
            send_ref, keep_ref, n2_ref, dgu_ref, hid_ref, cot_ref, mid_ref, gp_ref = refs[:8]
            a_ref, dn_ref = refs[8:]
            for b in range(n_plane):
                at = pl.multiple_of(plane_index(ids_ref, b) * q_cols, q_cols)
                a_ref[:, pl.ds(at, q_cols)] = a_refs[b][...]
            gp_ref[...] = jnp.zeros_like(gp_ref)
            step = half
            padded = -(-hid // 128) * 128
            whole = 2 * hid

            def body(c, carry):
                at = pl.ds(pl.multiple_of(c * step, step), step)
                middle = x_ref[at, :].astype(F32) + nn_dot(a_ref[at, :], wo_ref[...])
                mid_ref[at, :] = middle
                r = lax.rsqrt(jnp.mean(middle * middle, axis=1, keepdims=True) + EPSILON)
                n2_ref[at, :] = (middle * r * gf_ref[0:1, :]).astype(BF)
                cot_ref[at, :] = (og_ref[at, :].astype(F32) * info_ref[at, 1:2]).astype(BF)
                gu = jnp.zeros((step, whole), F32)
                dh = jnp.zeros((step, hid), F32)
                for k in range(n_block):
                    cols = pl.ds(offset(ids_ref, k), wide)
                    gu += nn_dot(n2_ref[at, cols], gu_refs[k][...])
                    dh += nt_dot(cot_ref[at, cols], dn_refs[k][...])
                gate = gu[:, :padded]
                up = pltpu.roll(gu, whole - hid, 1)[:, :padded]
                dh = jnp.concatenate([dh, jnp.zeros((step, padded - hid), F32)], axis=1) if padded > hid else dh
                sig = 1.0 / (1.0 + jnp.exp(-gate))
                act = gate * sig
                hid_ref[at, :] = (act * up)[:, :hid].astype(BF)
                d_gate = dh * up * sig * (1.0 + gate * (1.0 - sig))
                d_up = dh * act
                rest = jnp.zeros((step, whole - padded), F32)
                d_gate = jnp.concatenate([d_gate, rest], axis=1)
                d_up = pltpu.roll(jnp.concatenate([d_up, rest], axis=1), hid, 1)
                dgu_ref[at, :] = jnp.where(lanes((step, whole)) < hid, d_gate, d_up).astype(BF)
                for k in range(n_block):
                    dn_ref[:, pl.ds(offset(ids_ref, k), wide)] = nt_dot(dgu_ref[at, :], gu_refs[k][...])
                dn = dn_ref[...]
                gp_ref[...] += jnp.broadcast_to(
                    jnp.sum(dn * (mid_ref[at, :] * r), axis=0, keepdims=True), gp_ref.shape
                )
                low_dn = dn.astype(BF)

                @pl.when(c == ids_ref[1])
                def _():
                    keep_ref[...] = low_dn

                @pl.when(c != ids_ref[1])
                def _():
                    send_ref[...] = low_dn

                return carry

            lax.fori_loop(0, n_heads, body, 0)

        dn_send, dn_keep, normed_two, d_gate_up, hidden, cot, middle, ffn_gain_part = call(
            middle_part,
            [
                ((half, width), BF),
                ((half, width), BF),
                ((rows, width), BF),
                ((rows, 2 * hid), BF),
                ((rows, hid), BF),
                ((rows, width), BF),
                ((rows, width), F32),
                ((8, width), F32),
            ],
            ids,
            [row_info, block_input, out_grad, gf, out_full, *attended_parts, *gate_up_parts, *down_parts],
            scratch=[pltpu.VMEM((rows, width), BF), pltpu.VMEM((half, width), F32)],
            flops=2 * rows * width * (width + 5 * hid),
            vmem=48,
            name="middle",
        )

        def split(ids_ref, keep_ref, got_ref, *outs):
            for k in range(n_tensor):
                at = pl.ds(pl.multiple_of((ids_ref[2] ^ k) * sub, sub), sub)
                total = keep_ref[at, :].astype(F32) + got_ref[at, :].astype(F32)
                outs[k][...] = total.astype(BF)

        def plane_sum_parts(keep, send):
            got = swap(send, "heads", 1)
            parts = call(split, [((sub, width), BF)] * n_tensor, ids, [keep, got], vmem=8, name="split")
            return [parts[0]] + [swap(parts[k], "tensor", k) for k in range(1, n_tensor)]

        def tree(values):
            while len(values) > 1:
                values = [values[i] + values[i + 1] for i in range(0, len(values), 2)]
            return values[0]

        dn_parts = plane_sum_parts(dn_keep, dn_send)

        def ffn_grads(ids_ref, n2_ref, dgu_ref, hid_ref, cot_ref, *refs):
            dn_refs, (ggu_ref, gdn_ref, fo_ref) = refs[:n_block], refs[n_block:]
            for k in range(n_block):
                cols = pl.ds(offset(ids_ref, k), wide)
                ggu_ref[cols, :] = tn_dot(n2_ref[:, cols], dgu_ref[...]).astype(BF)
                down = tn_dot(hid_ref[...], cot_ref[:, cols]).astype(BF)
                if blocks_mode:
                    gdn_ref[pl.ds(pl.multiple_of(owner(ids_ref, k) * hid, hid), hid), :] = down
                else:
                    gdn_ref[...] = down
                fo_ref[:, cols] = nn_dot(hid_ref[...], dn_refs[k][...]).astype(BF)

        grad_gate_up, grad_down, ffn_part = call(
            ffn_grads,
            [((width, 2 * hid), BF), ((n_block * hid, wide), BF), ((rows, width), BF)],
            ids,
            [normed_two, d_gate_up, hidden, cot, *down_parts],
            flops=2 * rows * width * 4 * hid,
            vmem=32,
            name="ffn_grads",
        )
        gate_up_sum = lax.psum_scatter(grad_gate_up, "shard", scatter_dimension=0, tiled=True)
        down_sum = lax.psum_scatter(
            grad_down, "shard", scatter_dimension=0 if blocks_mode else 1, tiled=True
        )
        ffn_out = lax.psum(ffn_part, ("heads", "tensor")).astype(F32)
        live_weight = live.astype(F32)[:, None]
        block_output = (live_weight * (middle + ffn_out)).astype(BF)

        def norm_two_back(ids_ref, mid_ref, cot_ref, gf_ref, *refs):
            part_refs, (dm_ref, da_ref) = refs[:n_tensor], refs[n_tensor:]
            at = pl.ds(pl.multiple_of((ids_ref[1] * n_tensor + ids_ref[2]) * sub, sub), sub)
            d = tree([p[...].astype(F32) for p in part_refs])
            v = mid_ref[at, :]
            r = lax.rsqrt(jnp.mean(v * v, axis=1, keepdims=True) + EPSILON)
            w = v * r
            wd = d * gf_ref[0:1, :]
            dm = cot_ref[at, :].astype(F32) + r * (wd - w * jnp.mean(wd * w, axis=1, keepdims=True))
            dm_ref[...] = dm
            da_ref[...] = dm.astype(BF)

        d_middle, d_attn = call(
            norm_two_back,
            [((sub, width), F32), ((sub, width), BF)],
            ids,
            [middle, cot, gf, *dn_parts],
            vmem=8,
            name="norm_two_back",
        )
        d_attn_parts = plane_blocks(d_attn)

        def attend_back(ids_ref, info_ref, qs_ref, oa_ref, att_ref, wo_ref, *refs):
            d_refs, refs = refs[:n_plane], refs[n_plane:]
            kv_refs, refs = refs[:n_block], refs[n_block:]
            dq_ref, gwo_ref, dkv_refs = refs[0], refs[1], refs[2 : 2 + n_block]
            da_ref, do_ref, delta_ref, dqs_ref, acc_ref = refs[2 + n_block :]
            for b in range(n_plane):
                at = pl.multiple_of(plane_index(ids_ref, b) * sub, sub)
                da_ref[pl.ds(at, sub), :] = d_refs[b][...]
            low = lanes((rows, 128)) < 64
            do = nt_dot(da_ref[...], wo_ref[...]).astype(BF).astype(F32)
            first = jnp.where(low, 0.0, pltpu.roll(do, 64, 1))
            second = jnp.where(low, 0.0, do)
            do_ref[:rows, :] = first.astype(BF)
            do_ref[rows:, :] = second.astype(BF)
            delta_ref[:rows, :] = jnp.broadcast_to(
                jnp.sum(first * oa_ref[:rows, :], axis=1, keepdims=True), (rows, 128)
            )
            delta_ref[rows:, :] = jnp.broadcast_to(
                jnp.sum(second * oa_ref[rows:, :], axis=1, keepdims=True), (rows, 128)
            )
            dqs_ref[...] = jnp.zeros_like(dqs_ref)
            for k in range(n_block):
                grad = tn_dot(att_ref[...], da_ref[:, pl.ds(offset(ids_ref, k), wide)]).astype(BF)
                if blocks_mode:
                    gwo_ref[pl.ds(pl.multiple_of(owner(ids_ref, k) * q_cols, q_cols), q_cols), :] = grad
                else:
                    gwo_ref[...] = grad
                dkv_refs[k][...] = jnp.zeros_like(dkv_refs[k])

            def block(own, kv_ref, base, out_ref):
                kv = kv_ref[pl.ds(base, rows), :]
                acc_ref[...] = jnp.zeros_like(acc_ref)

                def body(c, carry):
                    at = pl.ds(pl.multiple_of(c * chunk, chunk), chunk)
                    q, d_out = qs_ref[at, :], do_ref[at, :]
                    p = masked_exp(ids_ref, info_ref, nt_dot(q, kv), c, own) * oa_ref[at, 0:1]
                    ds = (p * (nt_dot(d_out, kv) - delta_ref[at, 0:1])).astype(BF)
                    dqs_ref[at, :] += nn_dot(ds, kv)
                    acc_ref[...] += tn_dot(ds, q) + tn_dot(p.astype(BF), d_out)
                    return carry

                lax.fori_loop(0, 2 * rows // chunk, body, 0)
                out_ref[pl.ds(base, rows), :] = acc_ref[...].astype(BF)

            if blocks_mode:
                for k in range(n_block):
                    pl.when(owner(ids_ref, k) <= ids_ref[0])(
                        lambda k=k: block(owner(ids_ref, k), kv_refs[k], 0, dkv_refs[k])
                    )
            else:

                def step(j, carry):
                    block(j, kv_refs[0], pl.multiple_of(j * rows, rows), dkv_refs[0])
                    return carry

                lax.fori_loop(0, ids_ref[0] + 1, step, 0)
            dq_ref[...] = jnp.where(low, dqs_ref[:rows, :], pltpu.roll(dqs_ref[rows:, :], 64, 1))

        d_query, grad_out, *d_kv = call(
            attend_back,
            [((rows, 128), F32), ((n_block * q_cols, wide), BF)]
            + [((rows * (1 if blocks_mode else n_shard), 128), BF)] * n_block,
            ids,
            [row_info, queries, out_and_inverse, attended, own_rows, *d_attn_parts, *kv_parts],
            scratch=[
                pltpu.VMEM((rows, width), BF),
                pltpu.VMEM((2 * rows, 128), BF),
                pltpu.VMEM((2 * rows, 128), F32),
                pltpu.VMEM((2 * rows, 128), F32),
                pltpu.VMEM((rows, 128), F32),
            ],
            flops=10 * 2 * rows * rows * n_shard * 128,
            vmem=48,
            name="attend_back",
        )
        out_sum = lax.psum_scatter(
            grad_out, "shard", scatter_dimension=0 if blocks_mode else 1, tiled=True
        )
        if blocks_mode:
            d_kv_parts = [d_kv[0]] + [swap(d_kv[k], "shard", k) for k in range(1, n_block)]
        else:
            d_kv_parts = [lax.psum_scatter(d_kv[0], "shard", scatter_dimension=0, tiled=True)]

        def project_back(ids_ref, x_ref, n_ref, raw_ref, dq_ref, cos_ref, sin_ref, hg_ref, gp_ref, *refs):
            dkv_refs, refs = refs[:n_block], refs[n_block:]
            w_refs, refs = refs[:n_block], refs[n_block:]
            send_ref, keep_ref, g_refs = refs[0], refs[1], refs[2 : 2 + n_block]
            low_ref, r_ref = refs[-2:]
            lane = lanes((rows, 128))
            low, first = lane < 64, (lane % 64) < 32
            cos, sin = cos_ref[...], sin_ref[...]

            def back(v, g, d):
                d = d * cos + turn_back(d * sin, first)
                r = lax.rsqrt(head_mean(v * v, low) + EPSILON)
                w = v * r
                wd = d * g
                return r * (wd - w * head_mean(wd * w, low)), jnp.sum(d * w, axis=0, keepdims=True)

            scale = 1.0 / math.sqrt(head)
            dq, gain_q = back(raw_ref[:, :128], hg_ref[0:1, :], dq_ref[...] * scale)
            dkv = tree([p[...].astype(F32) for p in dkv_refs])
            dk, gain_k = back(raw_ref[:, 128:], hg_ref[8:9, :], dkv)
            low_ref[:, :128] = dq.astype(BF)
            low_ref[:, 128:] = jnp.where(low, dk, dkv).astype(BF)
            gain_q = gain_q + pltpu.roll(jnp.broadcast_to(gain_q, (8, 128)), 64, 1)[0:1]
            head_row = jnp.where(low[0:1], gain_q, pltpu.roll(jnp.broadcast_to(gain_k, (8, 128)), 64, 1)[0:1])
            head_row = jnp.concatenate([head_row, jnp.zeros((1, wide - 128), F32)], axis=1)
            x = x_ref[...].astype(F32)
            r_ref[...] = jnp.broadcast_to(
                lax.rsqrt(jnp.mean(x * x, axis=1, keepdims=True) + EPSILON), (rows, 128)
            )
            for k in range(n_block):
                cols = pl.ds(offset(ids_ref, k), wide)
                g_refs[k][:wide, :] = tn_dot(n_ref[:, cols], low_ref[...]).astype(BF)
                dn = nt_dot(low_ref[...], w_refs[k][:wide, :])
                low_dn = dn.astype(BF)
                for c in range(n_heads):
                    part = low_dn[c * half : (c + 1) * half]

                    @pl.when(c == ids_ref[1])
                    def _():
                        keep_ref[:, cols] = part

                    @pl.when(c != ids_ref[1])
                    def _():
                        send_ref[:, cols] = part

                w = x_ref[:, cols].astype(F32) * r_ref[:, 0:1]
                three = [jnp.sum(dn * w, axis=0, keepdims=True), gp_ref[0:1, cols], head_row]
                if blocks_mode:
                    high = [v.astype(BF).astype(F32) for v in three]
                    rest = [a - b for a, b in zip(three, high)]
                    packed_rows = high + rest + [jnp.zeros((GAIN_ROWS - 6, wide), F32)]
                    g_refs[k][wide:, :] = jnp.concatenate(packed_rows, axis=0).astype(BF)
                else:
                    refs[3][...] = jnp.concatenate(three + [jnp.zeros((5, wide), F32)], axis=0)

        if blocks_mode:
            grad_shapes = [((wide + GAIN_ROWS, 256), BF)] * n_block
        else:
            grad_shapes = [((wide, 256), BF), ((8, width), F32)]
        results = call(
            project_back,
            [((half, width), BF), ((half, width), BF)] + grad_shapes,
            ids,
            [block_input, normed_one, raw, d_query, cosine, sine, head_gains, ffn_gain_part, *d_kv_parts, *qkv_parts],
            scratch=[pltpu.VMEM((rows, 256), BF), pltpu.VMEM((rows, 128), F32)],
            flops=2 * rows * width * 512,
            vmem=32,
            name="project_back",
        )
        d1_send, d1_keep, grads = results[0], results[1], results[2:]
        d1_parts = plane_sum_parts(d1_keep, d1_send)
        def norm_one_back(ids_ref, x_ref, dm_ref, ga_ref, *refs):
            part_refs, ig_ref = refs[:n_tensor], refs[n_tensor]
            at = pl.ds(pl.multiple_of((ids_ref[1] * n_tensor + ids_ref[2]) * sub, sub), sub)
            d = tree([p[...].astype(F32) for p in part_refs])
            v = x_ref[at, :].astype(F32)
            r = lax.rsqrt(jnp.mean(v * v, axis=1, keepdims=True) + EPSILON)
            w = v * r
            wd = d * ga_ref[0:1, :]
            back = r * (wd - w * jnp.mean(wd * w, axis=1, keepdims=True))
            ig_ref[...] = (dm_ref[...] + back).astype(BF)

        (input_block,) = call(
            norm_one_back,
            [((sub, width), BF)],
            ids,
            [block_input, d_middle, ga, *d1_parts],
            vmem=8,
            name="norm_one_back",
        )
        input_parts = plane_blocks(input_block)

        def stack_rows(ids_ref, *refs):
            for b in range(n_plane):
                at = pl.multiple_of(plane_index(ids_ref, b) * sub, sub)
                refs[-1][pl.ds(at, sub), :] = refs[b][...].astype(F32)

        (input_grad,) = call(
            stack_rows, [((rows, width), F32)], ids, input_parts, vmem=8, name="stack_rows"
        )

        def place(ids_ref, *refs):
            b_refs, (q_ref, k_ref, v_ref, o_ref, s_ref) = refs[:n_tensor], refs[n_tensor:]
            for k in range(n_tensor):
                s_ref[ids_ref[2] ^ k] = b_refs[k][...].astype(F32)
            low = lanes((depth, 128)) < 64
            for i in range(n_tensor):
                q_ref[:, i * 128 : (i + 1) * 128] = s_ref[i, :depth, :128]
                o_ref[i * q_cols : (i + 1) * q_cols, :] = s_ref[i, depth + GAIN_ROWS :, :]
            for i in range(n_tensor // 2):
                even, odd = s_ref[2 * i, :depth, 128:], s_ref[2 * i + 1, :depth, 128:]
                k_ref[:, i * 128 : (i + 1) * 128] = jnp.where(low, even, pltpu.roll(odd, 64, 1))
                v_ref[:, i * 128 : (i + 1) * 128] = jnp.where(low, pltpu.roll(even, 64, 1), odd)

        if blocks_mode:
            sums = [grads[0]] + [swap(grads[k], "shard", k) for k in range(1, n_block)]
            own_sum = tree([s.astype(F32) for s in sums]).astype(BF)
            bundle = jnp.concatenate([own_sum, out_sum], axis=0)
            bundles = [bundle] + [swap(bundle, "tensor", k) for k in range(1, n_tensor)]
            total = tree([b[depth : depth + GAIN_ROWS].astype(F32) for b in bundles])
            total = total + swap(total, "heads", 1)
            total = total[0:3] + total[3:6]
            attn_gain_grad, ffn_gain_grad, head_gain_grad = total[0], total[1], total[2]
            query_grad, key_grad, value_grad, out_weight_grad = call(
                place,
                [
                    ((depth, n_tensor * q_cols), F32),
                    ((depth, n_tensor * k_cols), F32),
                    ((depth, n_tensor * k_cols), F32),
                    ((n_tensor * q_cols, depth), F32),
                ],
                ids,
                bundles,
                scratch=[pltpu.VMEM((n_tensor,) + bundle.shape, F32)],
                vmem=16,
                name="place",
            )
        else:
            own_sum = lax.psum_scatter(grads[0], "shard", scatter_dimension=0, tiled=True)
            total = lax.psum(grads[1], ("shard", "heads", "tensor"))
            attn_gain_grad = lax.dynamic_slice_in_dim(total[0], z * depth, depth)
            ffn_gain_grad = lax.dynamic_slice_in_dim(total[1], z * depth, depth)
            head_gain_grad = total[2]
            found = lax.all_gather(own_sum, "tensor", axis=0).astype(F32)
            flat = lambda x: jnp.swapaxes(x, 0, 1).reshape(depth, -1)
            query_grad = flat(found[:, :, :128])
            key_grad, value_grad = flat(found[:, :, 128:192]), flat(found[:, :, 192:])
            out_weight_grad = lax.all_gather(out_sum, "tensor", axis=0, tiled=True).astype(F32)

        other = swap(gate_up_sum, "heads", 1)
        lower = jnp.where(first_core, gate_up_sum, other)
        upper = jnp.where(first_core, other, gate_up_sum)
        gate_grad = jnp.concatenate([lower[:, :hid], upper[:, :hid]], axis=1).astype(F32)
        up_grad = jnp.concatenate([lower[:, hid:], upper[:, hid:]], axis=1).astype(F32)
        other = swap(down_sum, "heads", 1)
        lower = jnp.where(first_core, down_sum, other)
        upper = jnp.where(first_core, other, down_sum)
        down_grad = jnp.concatenate([lower, upper], axis=0).astype(F32)
        return (
            block_output,
            input_grad,
            attn_gain_grad,
            query_grad,
            key_grad,
            value_grad,
            head_gain_grad[:head],
            head_gain_grad[head : 2 * head],
            out_weight_grad,
            ffn_gain_grad,
            gate_grad,
            up_grad,
            down_grad,
        )

    return on_device


def solution(mesh):
    placed = (
        P("shard", None),
        P("shard"),
        P("shard", "heads"),
        P("shard", "heads"),
        P("shard", "heads"),
        P(),
        P(),
        P("heads", "shard"),
        P("shard"),
        P("shard", "tensor"),
        P("shard", "tensor"),
        P("tensor", "shard"),
        P(),
        P(),
        P("shard", None),
    )
    return jax.shard_map(
        make(mesh),
        mesh=mesh,
        in_specs=placed,
        out_specs=(
            P("shard", None),
            P("shard", None),
            P("shard"),
            P("shard", "heads"),
            P("shard", "heads"),
            P("shard", "heads"),
            P(),
            P(),
            P("heads", "shard"),
            P("shard"),
            P("shard", "tensor"),
            P("shard", "tensor"),
            P("tensor", "shard"),
        ),
        check_vma=False,
    )
```

time: 846 us -> 314 us (0.37); the launches traced: 834 us -> 313 us
  waiting for transfers between devices: 601 us -> 117 us
  starting transfers between devices: 1.02 us -> 90.9 us
  matrix products: 76.3 us -> 0 us
  blocking collectives: 74.9 us -> 0 us
  Pallas kernels: 0 us -> 40.3 us
  other arithmetic: 45.3 us -> 12.3 us
  local copies, waits for them, and re-layouts: 18.3 us -> 36.8 us
    reduce_scatter x9 -> x3, waiting for transfers between devices: 290 us -> 8.48 us  [the longest x1 8.45 us: on_device(): lax.psum_scatter(grad_gate_up, 'shard', scatter_dimension=0, tiled=True)]
    all_gather x7 -> x0, waiting for transfers between devices: 206 us -> none  [the longest x1 49.3 us: on_device(): lax.all_gather(up_weight, 'shard', axis=0, tiled=True)]
    ppermute x0 -> x63, waiting for transfers between devices: none -> 107 us  [swap(): return lax.ppermute(x, axis, [(i, i ^ k) for i in range(size)])]
    psum x3 -> x1, waiting for transfers between devices: 101 us -> 0.01 us  [on_device(): ffn_out = lax.psum(ffn_part, ('heads', 'tensor')).astype(F32)]
    ppermute x0 -> x63, starting transfers between devices: none -> 90.6 us  [swap(): return lax.ppermute(x, axis, [(i, i ^ k) for i in range(size)])]
    dot_general x30 -> x0, matrix products: 76.3 us -> none  [the longest x7 18 us: contract_rows(): lax.dot_general(left_side, right_side, (((0,), (0,)), ((), ())), preferre...]
    all_gather x4 -> x0, blocking collectives: 49.9 us -> none  [the longest x1 20.4 us: on_device(): lax.all_gather(key_weight, 'shard', axis=0, tiled=True)]
    pallas_call x0 -> x14, Pallas kernels: none -> 40.3 us  [call(): pl.pallas_call(kernel, out_shape=shapes, in_specs=[pl.BlockSpec(memory_sp...]
  transfers between devices with their start and end apart: 19 -> 67, of which waited for: 18 -> 28; matrix products, arithmetic and copies ran while one was open for 9% -> 6% of each run, Pallas kernels for 0% -> 7%
where the time goes in v1:
time: 314 us; the launch traced here: 313 us
  waiting for transfers between devices  117 us (37%)
  starting transfers between devices  90.9 us (29%)
  Pallas kernels  40.3 us (13%)
  local copies, waits for them, and re-layouts  36.8 us (12%)
  between operations  15.8 us (5%)
  other arithmetic  12.3 us (4%)
    ppermute x63, waiting for transfers between devices, swap(): return lax.ppermute(x, axis, [(i, i ^ k) for i in range(size)])  107 us
    ppermute x63, starting transfers between devices, swap(): return lax.ppermute(x, axis, [(i, i ^ k) for i in range(size)])  90.6 us
    pallas_call x14, Pallas kernels, call(): pl.pallas_call(kernel, out_shape=shapes, in_specs=[pl.BlockSpec(memory_sp...  40.3 us
    unnamed x118, local copies, waits for them, and re-layouts  26.5 us
    reduce_scatter x1, waiting for transfers between devices, on_device(): lax.psum_scatter(grad_gate_up, 'shard', scatter_dimension=0, tiled=True)  8.45 us
  transfers between devices with their start and end apart: 67, of which 28 were waited for; matrix products, arithmetic and copies ran while one was open for 6% of the time, Pallas kernels for 7%

profile of v1, /device:TPU:1, one launch (start us, length us, event | category | flops | bytes accessed | tf_op | source)
XLA Modules:
  0.0 313.4 jit_solution(6364015964107453410)
XLA Ops:
  9.0 4.2 %collective-permute-start.5 = (bf16[128,256]{1,0:T(8,128)(2,1)S(1)}, bf16[128,256]{1,0:T(8,128)(2,1)}, u32[]{:S(2)}, u32[]{:S(2)}) collective-permute-start(bf16[128,256]{1,0:T(8,128)(2,1)S(1)} %constant_dynamic-slice_fusion.1.refs_0_), channel_id=1, source_target_pairs={{0,24},{8,16},{16,8},{24,0},{1,25},{9,17},{17,9},{25,1},{2,26},{10... | collective-permute-start | bytes 196616 | tf_op jit(solution)/shard_map/ppermute | solution.py:72
  16.5 1.4 collective-permute-start.2
  24.9 2.5 fusion.4
  29.2 1.9 collective-permute-done.1.refs_2_.refs_6_
  32.4 3.5 %collective-permute-start.26 = (bf16[576,256]{1,0:T(8,128)(2,1)}, bf16[576,256]{1,0:T(8,128)(2,1)S(1)}, u32[]{:S(2)}, u32[]{:S(2)}) collective-permute-start(bf16[576,256]{1,0:T(8,128)(2,1)} %constant_dynamic-slice_fusion.refs_12_.refs_0_), channel_id=1, source_target_pairs={{0,8},{8,0},{16,24},{24,16},{1,9},{9,1},{17,25},{25,17},{2,10},{10... | collective-permute-start | bytes 884744 | tf_op jit(solution)/shard_map/ppermute | solution.py:72
  39.1 3.1 project.1
  43.9 1.2 collective-permute-start.14
  45.2 6.0 %collective-permute-done.15.refs_3_.refs_11_ = bf16[512,128]{1,0:T(8,128)(2,1)S(1)} collective-permute-done((bf16[512,128]{1,0:T(8,128)(2,1)S(1)}, bf16[512,128]{1,0:T(8,128)(2,1)S(1)}, u32[]{:S(2)}, u32[]{:S(2)}) %collective-permute-start.15) | collective-permute-done | bytes 131104 | tf_op jit(solution)/shard_map/ppermute | solution.py:72
  51.2 17.4 %collective-permute-start.13 = (bf16[512,128]{1,0:T(8,128)(2,1)S(1)}, bf16[512,128]{1,0:T(8,128)(2,1)S(1)}, u32[]{:S(2)}, u32[]{:S(2)}) collective-permute-start(bf16[512,128]{1,0:T(8,128)(2,1)S(1)} %get-tuple-element.60.refs_0_.refs_8_), channel_id=1, source_target_pairs={{0,8},{8,0},{16,24},{24,16},{1,9},{9,1},{17,25},{25,17},{2,10},{10... | collective-permute-start | bytes 393224 | tf_op jit(solution)/shard_map/ppermute | solution.py:72
  69.6 14.3 %collective-permute-done.14.refs_2_.refs_10_ = bf16[512,128]{1,0:T(8,128)(2,1)S(1)} collective-permute-done((bf16[512,128]{1,0:T(8,128)(2,1)S(1)}, bf16[512,128]{1,0:T(8,128)(2,1)S(1)}, u32[]{:S(2)}, u32[]{:S(2)}) %collective-permute-start.14) | collective-permute-done | bytes 131104 | tf_op jit(solution)/shard_map/ppermute | solution.py:72
  83.8 1.5 collective-permute-start.9
  85.3 1.7 collective-permute-done.13.refs_1_.refs_9_
  87.0 2.2 collective-permute-start.8
  89.9 2.8 attend.1
  92.7 1.6 collective-permute-start.19
  95.1 2.2 collective-permute-start.18
  97.3 5.6 %collective-permute-done.7.refs_2_ = bf16[128,1024]{1,0:T(8,128)(2,1)S(1)} collective-permute-done((bf16[128,1024]{1,0:T(8,128)(2,1)S(1)}, bf16[128,1024]{1,0:T(8,128)(2,1)S(1)}, u32[]{:S(2)}, u32[]{:S(2)}) %collective-permute-start.7) | collective-permute-done | bytes 262176 | tf_op jit(solution)/shard_map/ppermute | solution.py:72
  102.8 1.2 collective-permute-start.17
  104.1 1.5 collective-permute-start.25
  105.5 1.4 collective-permute-start.12
  107.3 1.5 collective-permute-start.22
  108.7 3.3 %collective-permute-done.16.refs_1_ = bf16[512,128]{1,0:T(8,128)(2,1)S(1)} collective-permute-done((bf16[512,128]{1,0:T(8,128)(2,1)S(1)}, bf16[512,128]{1,0:T(8,128)(2,1)S(1)}, u32[]{:S(2)}, u32[]{:S(2)}) %collective-permute-start.16) | collective-permute-done | bytes 131104 | tf_op jit(solution)/shard_map/ppermute | solution.py:72
  115.5 1.3 copy-done.5
  116.8 20.2 %collective-permute-done.28.refs_15_.refs_3_ = bf16[576,256]{1,0:T(8,128)(2,1)S(1)} collective-permute-done((bf16[576,256]{1,0:T(8,128)(2,1)S(1)}, bf16[576,256]{1,0:T(8,128)(2,1)S(1)}, u32[]{:S(2)}, u32[]{:S(2)}) %collective-permute-start.28) | collective-permute-done | bytes 294944 | tf_op jit(solution)/shard_map/ppermute | solution.py:72
  137.0 12.0 %middle.1 = (bf16[256,1024]{1,0:T(8,128)(2,1)S(1)}, bf16[256,1024]{1,0:T(8,128)(2,1)S(1)}, bf16[512,1024]{1,0:T(8,128)(2,1)}, bf16[512,1152]{1,0:T(8,128)(2,1)},...) custom-call(s32[3]{0:T(128)S(1)} %copy-done.31, ...), custom_call_target="tpu_custom_call" | custom-call | flops 4093640704 | bytes 16121856 | tf_op jit(solution)/shard_map/middle/pallas_call | solution.py:34
  149.0 1.8 collective-permute-start.29
  150.8 1.5 collective-permute-done.29.got_ref
  153.1 1.4 collective-permute-start.31
  155.8 2.1 collective-permute-done.30.refs_1_
  157.8 2.6 collective-permute-done.32.refs_3_
  160.4 1.6 copy-done.3
  164.2 1.9 collective-permute-start.34
  166.1 2.4 collective-permute-start.36
  168.5 3.3 %collective-permute-start.39 = (bf16[64,1024]{1,0:T(8,128)(2,1)S(1)}, bf16[64,1024]{1,0:T(8,128)(2,1)S(1)}, u32[]{:S(2)}, u32[]{:S(2)}) collective-permute-start(bf16[64,1024]{1,0:T(8,128)(2,1)S(1)} %collective-permute-done.35.refs_3_), channel_id=1, source_target_pairs={{0,4},{4,0},{1,5},{5,1},{2,6},{6,2},{3,7},{7,3},{8,12},{12,8},{9,1... | collective-permute-start | bytes 393224 | tf_op jit(solution)/shard_map/ppermute | solution.py:72
  171.8 1.3 collective-permute-start.38
  174.5 5.3 %attend_back.1 = (f32[512,128]{1,0:T(8,128)S(1)}, bf16[512,256]{1,0:T(8,128)(2,1)}, bf16[512,128]{1,0:T(8,128)(2,1)S(1)}, bf16[512,128]{1,0:T(8,128)(2,1)S(1)}, ...) custom-call(s32[3]{0:T(128)S(1)} %copy-done.31, f32[512,128]{1,0:T(8,128)S(1)} %broadcast_select_fusion.4.info_ref, ...), custom_call_target="tpu_custom_call" | custom-call | flops 2684354560 | bytes 4063232 | tf_op jit(solution)/shard_map/attend_back/pallas_call | solution.py:34
  185.6 1.3 copy-done.45
  186.9 1.2 copy-done.46
  189.2 5.4 %ffn_grads.1 = (bf16[1024,1152]{1,0:T(8,128)(2,1)S(1)}, bf16[2304,256]{1,0:T(8,128)(2,1)}, bf16[512,1024]{1,0:T(8,128)(2,1)}) custom-call(s32[3]{0:T(128)S(1)} %copy-done.31, bf16[512,1024]{1,0:T(8,128)(2,1)S(1)} %copy-done.46, bf16[512,1152]{1,0:T(8,128)(2,1)S(1)} %copy-done.45, bf16[512,576]{1,0:T(8,128)(2,1)S(1)} %copy-done.47, ...), custom_call_target="tpu_custom_call" | custom-call | flops 2415919104 | bytes 9633792 | tf_op jit(solution)/shard_map/ffn_grads/pallas_call | solution.py:34
  194.5 1.4 copy-done.4
  197.5 2.9 collective-permute-start.40
  200.4 6.5 %collective-permute-start.41 = (bf16[512,128]{1,0:T(8,128)(2,1)}, bf16[512,128]{1,0:T(8,128)(2,1)S(1)}, u32[]{:S(2)}, u32[]{:S(2)}) collective-permute-start(bf16[512,128]{1,0:T(8,128)(2,1)} %copy-done.43), channel_id=1, source_target_pairs={{0,16},{8,24},{16,0},{24,8},{1,17},{9,25},{17,1},{25,9},{2,18},{10... | collective-permute-start | bytes 393224 | tf_op jit(solution)/shard_map/ppermute | solution.py:72
  206.8 3.8 %collective-permute-done.41.refs_2_ = bf16[512,128]{1,0:T(8,128)(2,1)S(1)} collective-permute-done((bf16[512,128]{1,0:T(8,128)(2,1)}, bf16[512,128]{1,0:T(8,128)(2,1)S(1)}, u32[]{:S(2)}, u32[]{:S(2)}) %collective-permute-start.41) | collective-permute-done | bytes 131104 | tf_op jit(solution)/shard_map/ppermute | solution.py:72
  210.6 6.0 %collective-permute-done.42.refs_3_ = bf16[512,128]{1,0:T(8,128)(2,1)S(1)} collective-permute-done((bf16[512,128]{1,0:T(8,128)(2,1)}, bf16[512,128]{1,0:T(8,128)(2,1)S(1)}, u32[]{:S(2)}, u32[]{:S(2)}) %collective-permute-start.42) | collective-permute-done | bytes 131104 | tf_op jit(solution)/shard_map/ppermute | solution.py:72
  221.3 3.4 %project_back.1 = (bf16[256,1024]{1,0:T(8,128)(2,1)S(1)}, bf16[256,1024]{1,0:T(8,128)(2,1)S(1)}, bf16[272,256]{1,0:T(8,128)(2,1)S(1)}, bf16[272,256]{1,0:T(8,128...) custom-call(s32[3]{0:T(128)S(1)} %copy-done.32, bf16[512,1024]{1,0:T(8,128)(2,1)S(1)} %copy-done.2, ...), custom_call_target="tpu_custom_call" | custom-call | flops 536870912 | bytes 6135808 | tf_op jit(solution)/shard_map/project_back/pallas_call | solution.py:34
  226.3 2.7 collective-permute-start.54
  229.8 1.3 collective-permute-start.56
  231.1 11.3 %collective-permute-done.54 = bf16[272,256]{1,0:T(8,128)(2,1)S(1)} collective-permute-done((bf16[272,256]{1,0:T(8,128)(2,1)S(1)}, bf16[272,256]{1,0:T(8,128)(2,1)S(1)}, u32[]{:S(2)}, u32[]{:S(2)}) %collective-permute-start.54) | collective-permute-done | bytes 139296 | tf_op jit(solution)/shard_map/ppermute | solution.py:72
  242.4 1.8 collective-permute-done.55
  244.1 5.1 %collective-permute-done.56 = bf16[272,256]{1,0:T(8,128)(2,1)S(1)} collective-permute-done((bf16[272,256]{1,0:T(8,128)(2,1)S(1)}, bf16[272,256]{1,0:T(8,128)(2,1)S(1)}, u32[]{:S(2)}, u32[]{:S(2)}) %collective-permute-start.56) | collective-permute-done | bytes 139296 | tf_op jit(solution)/shard_map/ppermute | solution.py:72
  250.2 1.6 collective-permute-start.59
  252.9 1.8 collective-permute-start.43
  254.7 4.6 %collective-permute-done.59.refs_3_ = bf16[400,256]{1,0:T(8,128)(2,1)S(1)} collective-permute-done((bf16[400,256]{1,0:T(8,128)(2,1)S(1)}, bf16[400,256]{1,0:T(8,128)(2,1)S(1)}, u32[]{:S(2)}, u32[]{:S(2)}) %collective-permute-start.59) | collective-permute-done | bytes 204832 | tf_op jit(solution)/shard_map/ppermute | solution.py:72
  259.3 4.6 %collective-permute-done.58.refs_2_ = bf16[400,256]{1,0:T(8,128)(2,1)S(1)} collective-permute-done((bf16[400,256]{1,0:T(8,128)(2,1)S(1)}, bf16[400,256]{1,0:T(8,128)(2,1)S(1)}, u32[]{:S(2)}, u32[]{:S(2)}) %collective-permute-start.58) | collective-permute-done | bytes 204832 | tf_op jit(solution)/shard_map/ppermute | solution.py:72
  266.0 3.2 %multiply_convert_fusion = bf16[512,1024]{1,0:T(8,128)(2,1)} fusion(f32[512,1024]{1,0:T(8,128)} %get-tuple-element.62.mid_ref, bf16[512,1024]{1,0:T(8,128)(2,1)} %all-reduce.3.cloned.1.call-done, f32[512]{0:T(512)S(1)} %copy-done.56), kind=kLoop, calls=%fused_computation | loop fusion | flops 2097152 | bytes 4196352 | tf_op jit(solution)/shard_map/convert_element_type | solution.py:451
  271.4 1.2 collective-permute-start.46
  272.6 2.0 place.1
  275.8 2.9 collective-permute-done.46.refs_3_
  280.5 1.2 collective-permute-start.49
  284.6 1.9 collective-permute-done.49.refs_3_
  286.5 1.3 collective-permute-start.53
  287.8 1.9 collective-permute-done.48.refs_2_
  290.3 8.5 %reduce-scatter.6.cloned.1.call-done = bf16[256,1152]{1,0:T(8,128)(2,1)} async-done(((bf16[1024,1152]{1,0:T(8,128)(2,1)}), bf16[256,1152]{1,0:T(8,128)(2,1)}) %reduce-scatter.6.cloned.1.call-update) | async-done | bytes 589840 | tf_op jit(solution)/shard_map/reduce_scatter | solution.py:445
  300.2 2.0 stack_rows.1
  (250 shorter events, 64.4 us)
Async XLA Ops:
  8.0 241.3 %reduce-scatter.4.cloned.1.call-start = ((), (), s32[]{:S(2)}) async-start(), calls=%async_computation.4 | async-start | bytes 327680 | tf_op jit(solution)/shard_map/reduce_scatter | solution.py:551
  9.0 33.1 %collective-permute-start.5 = (bf16[128,256]{1,0:T(8,128)(2,1)S(1)}, bf16[128,256]{1,0:T(8,128)(2,1)}, u32[]{:S(2)}, u32[]{:S(2)}) collective-permute-start(bf16[128,256]{1,0:T(8,128)(2,1)S(1)} %constant_dynamic-slice_fusion.1.refs_0_), channel_id=1, source_target_pairs={{0,24},{8,16},{16,8},{24,0},{1,25},{9,17},{17,9},{25,1},{2,26},{10... | collective-permute-start | bytes 196616 | tf_op jit(solution)/shard_map/ppermute | solution.py:72
  13.2 29.5 %collective-permute-start.4 = (bf16[128,256]{1,0:T(8,128)(2,1)S(1)}, bf16[128,256]{1,0:T(8,128)(2,1)}, u32[]{:S(2)}, u32[]{:S(2)}) collective-permute-start(bf16[128,256]{1,0:T(8,128)(2,1)S(1)} %constant_dynamic-slice_fusion.1.refs_0_), channel_id=1, source_target_pairs={{0,16},{8,24},{16,0},{24,8},{1,17},{9,25},{17,1},{25,9},{2,18},{10... | collective-permute-start | bytes 196616 | tf_op jit(solution)/shard_map/ppermute | solution.py:72
  16.5 12.3 %collective-permute-start.2 = (bf16[272,256]{1,0:T(8,128)(2,1)S(1)}, bf16[272,256]{1,0:T(8,128)(2,1)S(1)}, u32[]{:S(2)}, u32[]{:S(2)}) collective-permute-start(bf16[272,256]{1,0:T(8,128)(2,1)S(1)} %maximum_maximum_fusion.refs_0_.refs_4_), channel_id=1, source_target_pairs={{0,24},{8,16},{16,8},{24,0},{1,25},{9,17},{17,9},{25,1},{2,26},{10... | collective-permute-start | bytes 417800 | tf_op jit(solution)/shard_map/ppermute | solution.py:72
  18.0 13.1 %collective-permute-start.1 = (bf16[272,256]{1,0:T(8,128)(2,1)S(1)}, bf16[272,256]{1,0:T(8,128)(2,1)S(1)}, u32[]{:S(2)}, u32[]{:S(2)}) collective-permute-start(bf16[272,256]{1,0:T(8,128)(2,1)S(1)} %maximum_maximum_fusion.refs_0_.refs_4_), channel_id=1, source_target_pairs={{0,16},{8,24},{16,0},{24,8},{1,17},{9,25},{17,1},{25,9},{2,18},{10... | collective-permute-start | bytes 417800 | tf_op jit(solution)/shard_map/ppermute | solution.py:72
  19.0 12.7 %collective-permute-start = (bf16[272,256]{1,0:T(8,128)(2,1)S(1)}, bf16[272,256]{1,0:T(8,128)(2,1)S(1)}, u32[]{:S(2)}, u32[]{:S(2)}) collective-permute-start(bf16[272,256]{1,0:T(8,128)(2,1)S(1)} %maximum_maximum_fusion.refs_0_.refs_4_), channel_id=1, source_target_pairs={{0,8},{8,0},{16,24},{24,16},{1,9},{9,1},{17,25},{25,17},{2,10},{10... | collective-permute-start | bytes 417800 | tf_op jit(solution)/shard_map/ppermute | solution.py:72
  28.8 15.1 %collective-permute-start.3 = (bf16[128,256]{1,0:T(8,128)(2,1)S(1)}, bf16[128,256]{1,0:T(8,128)(2,1)S(1)}, u32[]{:S(2)}, u32[]{:S(2)}) collective-permute-start(bf16[128,256]{1,0:T(8,128)(2,1)S(1)} %constant_dynamic-slice_fusion.1.refs_0_), channel_id=1, source_target_pairs={{0,8},{8,0},{16,24},{24,16},{1,9},{9,1},{17,25},{25,17},{2,10},{10... | collective-permute-start | bytes 196616 | tf_op jit(solution)/shard_map/ppermute | solution.py:72
  31.8 57.4 %collective-permute-start.27 = (bf16[576,256]{1,0:T(8,128)(2,1)}, bf16[576,256]{1,0:T(8,128)(2,1)S(1)}, u32[]{:S(2)}, u32[]{:S(2)}) collective-permute-start(bf16[576,256]{1,0:T(8,128)(2,1)} %constant_dynamic-slice_fusion.refs_12_.refs_0_), channel_id=1, source_target_pairs={{0,16},{8,24},{16,0},{24,8},{1,17},{9,25},{17,1},{25,9},{2,18},{10... | collective-permute-start | bytes 884744 | tf_op jit(solution)/shard_map/ppermute | solution.py:72
  32.4 57.0 %collective-permute-start.26 = (bf16[576,256]{1,0:T(8,128)(2,1)}, bf16[576,256]{1,0:T(8,128)(2,1)S(1)}, u32[]{:S(2)}, u32[]{:S(2)}) collective-permute-start(bf16[576,256]{1,0:T(8,128)(2,1)} %constant_dynamic-slice_fusion.refs_12_.refs_0_), channel_id=1, source_target_pairs={{0,8},{8,0},{16,24},{24,16},{1,9},{9,1},{17,25},{25,17},{2,10},{10... | collective-permute-start | bytes 884744 | tf_op jit(solution)/shard_map/ppermute | solution.py:72
  42.2 9.0 %collective-permute-start.15 = (bf16[512,128]{1,0:T(8,128)(2,1)S(1)}, bf16[512,128]{1,0:T(8,128)(2,1)S(1)}, u32[]{:S(2)}, u32[]{:S(2)}) collective-permute-start(bf16[512,128]{1,0:T(8,128)(2,1)S(1)} %get-tuple-element.60.refs_0_.refs_8_), channel_id=1, source_target_pairs={{0,24},{8,16},{16,8},{24,0},{1,25},{9,17},{17,9},{25,1},{2,26},{10... | collective-permute-start | bytes 393224 | tf_op jit(solution)/shard_map/ppermute | solution.py:72
  42.7 61.4 %collective-permute-start.24 = (bf16[256,1152]{1,0:T(8,128)(2,1)S(1)}, bf16[256,1152]{1,0:T(8,128)(2,1)S(1)}, u32[]{:S(2)}, u32[]{:S(2)}) collective-permute-start(bf16[256,1152]{1,0:T(8,128)(2,1)S(1)} %maximum_select_fusion.refs_8_), channel_id=1, source_target_pairs={{0,16},{8,24},{16,0},{24,8},{1,17},{9,25},{17,1},{25,9},{2,18},{10... | collective-permute-start | bytes 1769480 | tf_op jit(solution)/shard_map/ppermute | solution.py:72
  43.9 39.9 %collective-permute-start.14 = (bf16[512,128]{1,0:T(8,128)(2,1)S(1)}, bf16[512,128]{1,0:T(8,128)(2,1)S(1)}, u32[]{:S(2)}, u32[]{:S(2)}) collective-permute-start(bf16[512,128]{1,0:T(8,128)(2,1)S(1)} %get-tuple-element.60.refs_0_.refs_8_), channel_id=1, source_target_pairs={{0,16},{8,24},{16,0},{24,8},{1,17},{9,25},{17,1},{25,9},{2,18},{10... | collective-permute-start | bytes 393224 | tf_op jit(solution)/shard_map/ppermute | solution.py:72
  51.2 35.8 %collective-permute-start.13 = (bf16[512,128]{1,0:T(8,128)(2,1)S(1)}, bf16[512,128]{1,0:T(8,128)(2,1)S(1)}, u32[]{:S(2)}, u32[]{:S(2)}) collective-permute-start(bf16[512,128]{1,0:T(8,128)(2,1)S(1)} %get-tuple-element.60.refs_0_.refs_8_), channel_id=1, source_target_pairs={{0,8},{8,0},{16,24},{24,16},{1,9},{9,1},{17,25},{25,17},{2,10},{10... | collective-permute-start | bytes 393224 | tf_op jit(solution)/shard_map/ppermute | solution.py:72
  83.8 8.9 %collective-permute-start.9 = (bf16[128,1024]{1,0:T(8,128)(2,1)S(1)}, bf16[128,1024]{1,0:T(8,128)(2,1)S(1)}, u32[]{:S(2)}, u32[]{:S(2)}) collective-permute-start(bf16[128,1024]{1,0:T(8,128)(2,1)S(1)} %beside.1.refs_0_.wo_ref), channel_id=1, source_target_pairs={{0,4},{4,0},{1,5},{5,1},{2,6},{6,2},{3,7},{7,3},{8,12},{12,8},{9,1... | collective-permute-start | bytes 786440 | tf_op jit(solution)/shard_map/ppermute | solution.py:72
  87.0 8.0 %collective-permute-start.8 = (bf16[128,1024]{1,0:T(8,128)(2,1)S(1)}, bf16[128,1024]{1,0:T(8,128)(2,1)S(1)}, u32[]{:S(2)}, u32[]{:S(2)}) collective-permute-start(bf16[128,1024]{1,0:T(8,128)(2,1)S(1)} %beside.1.refs_0_.wo_ref), channel_id=1, source_target_pairs={{0,3},{1,2},{2,1},{3,0},{4,7},{5,6},{6,5},{7,4},{8,11},{9,10},{10,... | collective-permute-start | bytes 786440 | tf_op jit(solution)/shard_map/ppermute | solution.py:72
  89.2 13.6 %collective-permute-start.7 = (bf16[128,1024]{1,0:T(8,128)(2,1)S(1)}, bf16[128,1024]{1,0:T(8,128)(2,1)S(1)}, u32[]{:S(2)}, u32[]{:S(2)}) collective-permute-start(bf16[128,1024]{1,0:T(8,128)(2,1)S(1)} %beside.1.refs_0_.wo_ref), channel_id=1, source_target_pairs={{0,2},{1,3},{2,0},{3,1},{4,6},{5,7},{6,4},{7,5},{8,10},{9,11},{10,... | collective-permute-start | bytes 786440 | tf_op jit(solution)/shard_map/ppermute | solution.py:72
  89.4 14.7 %collective-permute-start.6 = (bf16[128,1024]{1,0:T(8,128)(2,1)S(1)}, bf16[128,1024]{1,0:T(8,128)(2,1)S(1)}, u32[]{:S(2)}, u32[]{:S(2)}) collective-permute-start(bf16[128,1024]{1,0:T(8,128)(2,1)S(1)} %beside.1.refs_0_.wo_ref), channel_id=1, source_target_pairs={{0,1},{1,0},{2,3},{3,2},{4,5},{5,4},{6,7},{7,6},{8,9},{9,8},{10,11... | collective-permute-start | bytes 786440 | tf_op jit(solution)/shard_map/ppermute | solution.py:72
  92.7 12.8 %collective-permute-start.19 = (bf16[512,128]{1,0:T(8,128)(2,1)S(1)}, bf16[512,128]{1,0:T(8,128)(2,1)S(1)}, u32[]{:S(2)}, u32[]{:S(2)}) collective-permute-start(bf16[512,128]{1,0:T(8,128)(2,1)S(1)} %get-tuple-element.61.refs_0_.att_ref), channel_id=1, source_target_pairs={{0,4},{4,0},{1,5},{5,1},{2,6},{6,2},{3,7},{7,3},{8,12},{12,8},{9,1... | collective-permute-start | bytes 393224 | tf_op jit(solution)/shard_map/ppermute | solution.py:72
  95.1 11.9 %collective-permute-start.18 = (bf16[512,128]{1,0:T(8,128)(2,1)S(1)}, bf16[512,128]{1,0:T(8,128)(2,1)S(1)}, u32[]{:S(2)}, u32[]{:S(2)}) collective-permute-start(bf16[512,128]{1,0:T(8,128)(2,1)S(1)} %get-tuple-element.61.refs_0_.att_ref), channel_id=1, source_target_pairs={{0,3},{1,2},{2,1},{3,0},{4,7},{5,6},{6,5},{7,4},{8,11},{9,10},{10,... | collective-permute-start | bytes 393224 | tf_op jit(solution)/shard_map/ppermute | solution.py:72
  102.8 4.5 %collective-permute-start.17 = (bf16[512,128]{1,0:T(8,128)(2,1)S(1)}, bf16[512,128]{1,0:T(8,128)(2,1)S(1)}, u32[]{:S(2)}, u32[]{:S(2)}) collective-permute-start(bf16[512,128]{1,0:T(8,128)(2,1)S(1)} %get-tuple-element.61.refs_0_.att_ref), channel_id=1, source_target_pairs={{0,2},{1,3},{2,0},{3,1},{4,6},{5,7},{6,4},{7,5},{8,10},{9,11},{10,... | collective-permute-start | bytes 393224 | tf_op jit(solution)/shard_map/ppermute | solution.py:72
  104.1 32.9 %collective-permute-start.23 = (bf16[256,1152]{1,0:T(8,128)(2,1)S(1)}, bf16[256,1152]{1,0:T(8,128)(2,1)S(1)}, u32[]{:S(2)}, u32[]{:S(2)}) collective-permute-start(bf16[256,1152]{1,0:T(8,128)(2,1)S(1)} %maximum_select_fusion.refs_8_), channel_id=1, source_target_pairs={{0,8},{8,0},{16,24},{24,16},{1,9},{9,1},{17,25},{25,17},{2,10},{10... | collective-permute-start | bytes 1769480 | tf_op jit(solution)/shard_map/ppermute | solution.py:72
  104.1 32.9 %collective-permute-start.25 = (bf16[256,1152]{1,0:T(8,128)(2,1)S(1)}, bf16[256,1152]{1,0:T(8,128)(2,1)S(1)}, u32[]{:S(2)}, u32[]{:S(2)}) collective-permute-start(bf16[256,1152]{1,0:T(8,128)(2,1)S(1)} %collective-permute-done.24.refs_10_), channel_id=1, source_target_pairs={{0,8},{8,0},{16,24},{24,16},{1,9},{9,1},{17,25},{25,17},{2,10},{10... | collective-permute-start | bytes 1769480 | tf_op jit(solution)/shard_map/ppermute | solution.py:72
  105.5 7.4 %collective-permute-start.12 = (bf16[128,1024]{1,0:T(8,128)(2,1)S(1)}, bf16[128,1024]{1,0:T(8,128)(2,1)S(1)}, u32[]{:S(2)}, u32[]{:S(2)}) collective-permute-start(bf16[128,1024]{1,0:T(8,128)(2,1)S(1)} %collective-permute-done.8.refs_3_), channel_id=1, source_target_pairs={{0,4},{4,0},{1,5},{5,1},{2,6},{6,2},{3,7},{7,3},{8,12},{12,8},{9,1... | collective-permute-start | bytes 786440 | tf_op jit(solution)/shard_map/ppermute | solution.py:72
  107.0 5.1 %collective-permute-start.16 = (bf16[512,128]{1,0:T(8,128)(2,1)S(1)}, bf16[512,128]{1,0:T(8,128)(2,1)S(1)}, u32[]{:S(2)}, u32[]{:S(2)}) collective-permute-start(bf16[512,128]{1,0:T(8,128)(2,1)S(1)} %get-tuple-element.61.refs_0_.att_ref), channel_id=1, source_target_pairs={{0,1},{1,0},{2,3},{3,2},{4,5},{5,4},{6,7},{7,6},{8,9},{9,8},{10,11... | collective-permute-start | bytes 393224 | tf_op jit(solution)/shard_map/ppermute | solution.py:72
  107.3 5.6 %collective-permute-start.22 = (bf16[512,128]{1,0:T(8,128)(2,1)S(1)}, bf16[512,128]{1,0:T(8,128)(2,1)S(1)}, u32[]{:S(2)}, u32[]{:S(2)}) collective-permute-start(bf16[512,128]{1,0:T(8,128)(2,1)S(1)} %collective-permute-done.18.refs_3_), channel_id=1, source_target_pairs={{0,4},{4,0},{1,5},{5,1},{2,6},{6,2},{3,7},{7,3},{8,12},{12,8},{9,1... | collective-permute-start | bytes 393224 | tf_op jit(solution)/shard_map/ppermute | solution.py:72
  112.9 24.1 %collective-permute-start.28 = (bf16[576,256]{1,0:T(8,128)(2,1)S(1)}, bf16[576,256]{1,0:T(8,128)(2,1)S(1)}, u32[]{:S(2)}, u32[]{:S(2)}) collective-permute-start(bf16[576,256]{1,0:T(8,128)(2,1)S(1)} %collective-permute-done.27.refs_14_.refs_2_), channel_id=1, source_target_pairs={{0,8},{8,0},{16,24},{24,16},{1,9},{9,1},{17,25},{25,17},{2,10},{10... | collective-permute-start | bytes 884744 | tf_op jit(solution)/shard_map/ppermute | solution.py:72
  114.1 2.8 collective-permute-start.21
  114.4 2.4 collective-permute-start.20
  149.0 3.4 %collective-permute-start.29 = (bf16[256,1024]{1,0:T(8,128)(2,1)S(1)}, bf16[256,1024]{1,0:T(8,128)(2,1)S(1)}, u32[]{:S(2)}, u32[]{:S(2)}) collective-permute-start(bf16[256,1024]{1,0:T(8,128)(2,1)S(1)} %get-tuple-element.69), channel_id=1, source_target_pairs={{0,4},{4,0},{1,5},{5,1},{2,6},{6,2},{3,7},{7,3},{8,12},{12,8},{9,1... | collective-permute-start | bytes 1572872 | tf_op jit(solution)/shard_map/ppermute | solution.py:72
  153.0 4.8 %collective-permute-start.30 = (bf16[64,1024]{1,0:T(8,128)(2,1)S(1)}, bf16[64,1024]{1,0:T(8,128)(2,1)S(1)}, u32[]{:S(2)}, u32[]{:S(2)}) collective-permute-start(bf16[64,1024]{1,0:T(8,128)(2,1)S(1)} %get-tuple-element.71), channel_id=1, source_target_pairs={{0,1},{1,0},{2,3},{3,2},{4,5},{5,4},{6,7},{7,6},{8,9},{9,8},{10,11... | collective-permute-start | bytes 393224 | tf_op jit(solution)/shard_map/ppermute | solution.py:72
  153.1 4.7 %collective-permute-start.31 = (bf16[64,1024]{1,0:T(8,128)(2,1)S(1)}, bf16[64,1024]{1,0:T(8,128)(2,1)S(1)}, u32[]{:S(2)}, u32[]{:S(2)}) collective-permute-start(bf16[64,1024]{1,0:T(8,128)(2,1)S(1)} %get-tuple-element.72), channel_id=1, source_target_pairs={{0,2},{1,3},{2,0},{3,1},{4,6},{5,7},{6,4},{7,5},{8,10},{9,11},{10,... | collective-permute-start | bytes 393224 | tf_op jit(solution)/shard_map/ppermute | solution.py:72
  154.6 5.8 %collective-permute-start.32 = (bf16[64,1024]{1,0:T(8,128)(2,1)S(1)}, bf16[64,1024]{1,0:T(8,128)(2,1)S(1)}, u32[]{:S(2)}, u32[]{:S(2)}) collective-permute-start(bf16[64,1024]{1,0:T(8,128)(2,1)S(1)} %get-tuple-element.73), channel_id=1, source_target_pairs={{0,3},{1,2},{2,1},{3,0},{4,7},{5,6},{6,5},{7,4},{8,11},{9,10},{10,... | collective-permute-start | bytes 393224 | tf_op jit(solution)/shard_map/ppermute | solution.py:72
  163.5 5.0 %collective-permute-start.35 = (bf16[64,1024]{1,0:T(8,128)(2,1)S(1)}, bf16[64,1024]{1,0:T(8,128)(2,1)S(1)}, u32[]{:S(2)}, u32[]{:S(2)}) collective-permute-start(bf16[64,1024]{1,0:T(8,128)(2,1)S(1)} %get-tuple-element.79.refs_0_), channel_id=1, source_target_pairs={{0,3},{1,2},{2,1},{3,0},{4,7},{5,6},{6,5},{7,4},{8,11},{9,10},{10,... | collective-permute-start | bytes 393224 | tf_op jit(solution)/shard_map/ppermute | solution.py:72
  164.2 7.6 %collective-permute-start.34 = (bf16[64,1024]{1,0:T(8,128)(2,1)S(1)}, bf16[64,1024]{1,0:T(8,128)(2,1)S(1)}, u32[]{:S(2)}, u32[]{:S(2)}) collective-permute-start(bf16[64,1024]{1,0:T(8,128)(2,1)S(1)} %get-tuple-element.79.refs_0_), channel_id=1, source_target_pairs={{0,2},{1,3},{2,0},{3,1},{4,6},{5,7},{6,4},{7,5},{8,10},{9,11},{10,... | collective-permute-start | bytes 393224 | tf_op jit(solution)/shard_map/ppermute | solution.py:72
  166.1 7.0 %collective-permute-start.33 = (bf16[64,1024]{1,0:T(8,128)(2,1)S(1)}, bf16[64,1024]{1,0:T(8,128)(2,1)S(1)}, u32[]{:S(2)}, u32[]{:S(2)}) collective-permute-start(bf16[64,1024]{1,0:T(8,128)(2,1)S(1)} %get-tuple-element.79.refs_0_), channel_id=1, source_target_pairs={{0,1},{1,0},{2,3},{3,2},{4,5},{5,4},{6,7},{7,6},{8,9},{9,8},{10,11... | collective-permute-start | bytes 393224 | tf_op jit(solution)/shard_map/ppermute | solution.py:72
  166.1 7.3 %collective-permute-start.36 = (bf16[64,1024]{1,0:T(8,128)(2,1)S(1)}, bf16[64,1024]{1,0:T(8,128)(2,1)S(1)}, u32[]{:S(2)}, u32[]{:S(2)}) collective-permute-start(bf16[64,1024]{1,0:T(8,128)(2,1)S(1)} %get-tuple-element.79.refs_0_), channel_id=1, source_target_pairs={{0,4},{4,0},{1,5},{5,1},{2,6},{6,2},{3,7},{7,3},{8,12},{12,8},{9,1... | collective-permute-start | bytes 393224 | tf_op jit(solution)/shard_map/ppermute | solution.py:72
  168.5 4.9 %collective-permute-start.39 = (bf16[64,1024]{1,0:T(8,128)(2,1)S(1)}, bf16[64,1024]{1,0:T(8,128)(2,1)S(1)}, u32[]{:S(2)}, u32[]{:S(2)}) collective-permute-start(bf16[64,1024]{1,0:T(8,128)(2,1)S(1)} %collective-permute-done.35.refs_3_), channel_id=1, source_target_pairs={{0,4},{4,0},{1,5},{5,1},{2,6},{6,2},{3,7},{7,3},{8,12},{12,8},{9,1... | collective-permute-start | bytes 393224 | tf_op jit(solution)/shard_map/ppermute | solution.py:72
  171.8 2.3 collective-permute-start.38
  183.1 82.9 %all-reduce.3.cloned.1.call-start = ((), (), s32[]{:S(2)}) async-start(), calls=%async_computation.3 | async-start | bytes 2097152 | tf_op jit(solution)/shard_map/psum | solution.py:449
  196.0 87.2 %reduce-scatter.8.cloned.1.call-start = ((), (), s32[]{:S(2)}) async-start(), calls=%async_computation.6 | async-start | bytes 1474560 | tf_op jit(solution)/shard_map/reduce_scatter | solution.py:446
  196.7 102.0 %reduce-scatter.6.cloned.1.call-start = ((), (), s32[]{:S(2)}) async-start(), calls=%async_computation.5 | async-start | bytes 2949120 | tf_op jit(solution)/shard_map/reduce_scatter | solution.py:445
  197.5 9.4 %collective-permute-start.40 = (bf16[512,128]{1,0:T(8,128)(2,1)}, bf16[512,128]{1,0:T(8,128)(2,1)S(1)}, u32[]{:S(2)}, u32[]{:S(2)}) collective-permute-start(bf16[512,128]{1,0:T(8,128)(2,1)} %copy-done.44), channel_id=1, source_target_pairs={{0,8},{8,0},{16,24},{24,16},{1,9},{9,1},{17,25},{25,17},{2,10},{10... | collective-permute-start | bytes 393224 | tf_op jit(solution)/shard_map/ppermute | solution.py:72
  200.4 10.2 %collective-permute-start.41 = (bf16[512,128]{1,0:T(8,128)(2,1)}, bf16[512,128]{1,0:T(8,128)(2,1)S(1)}, u32[]{:S(2)}, u32[]{:S(2)}) collective-permute-start(bf16[512,128]{1,0:T(8,128)(2,1)} %copy-done.43), channel_id=1, source_target_pairs={{0,16},{8,24},{16,0},{24,8},{1,17},{9,25},{17,1},{25,9},{2,18},{10... | collective-permute-start | bytes 393224 | tf_op jit(solution)/shard_map/ppermute | solution.py:72
  206.8 9.7 %collective-permute-start.42 = (bf16[512,128]{1,0:T(8,128)(2,1)}, bf16[512,128]{1,0:T(8,128)(2,1)S(1)}, u32[]{:S(2)}, u32[]{:S(2)}) collective-permute-start(bf16[512,128]{1,0:T(8,128)(2,1)} %copy-done.42), channel_id=1, source_target_pairs={{0,24},{8,16},{16,8},{24,0},{1,25},{9,17},{17,9},{25,1},{2,26},{10... | collective-permute-start | bytes 393224 | tf_op jit(solution)/shard_map/ppermute | solution.py:72
  226.3 16.1 %collective-permute-start.54 = (bf16[272,256]{1,0:T(8,128)(2,1)S(1)}, bf16[272,256]{1,0:T(8,128)(2,1)S(1)}, u32[]{:S(2)}, u32[]{:S(2)}) collective-permute-start(bf16[272,256]{1,0:T(8,128)(2,1)S(1)} %get-tuple-element.93), channel_id=1, source_target_pairs={{0,8},{8,0},{16,24},{24,16},{1,9},{9,1},{17,25},{25,17},{2,10},{10... | collective-permute-start | bytes 417800 | tf_op jit(solution)/shard_map/ppermute | solution.py:72
  229.0 15.2 %collective-permute-start.55 = (bf16[272,256]{1,0:T(8,128)(2,1)S(1)}, bf16[272,256]{1,0:T(8,128)(2,1)S(1)}, u32[]{:S(2)}, u32[]{:S(2)}) collective-permute-start(bf16[272,256]{1,0:T(8,128)(2,1)S(1)} %get-tuple-element.94), channel_id=1, source_target_pairs={{0,16},{8,24},{16,0},{24,8},{1,17},{9,25},{17,1},{25,9},{2,18},{10... | collective-permute-start | bytes 417800 | tf_op jit(solution)/shard_map/ppermute | solution.py:72
  229.8 19.4 %collective-permute-start.56 = (bf16[272,256]{1,0:T(8,128)(2,1)S(1)}, bf16[272,256]{1,0:T(8,128)(2,1)S(1)}, u32[]{:S(2)}, u32[]{:S(2)}) collective-permute-start(bf16[272,256]{1,0:T(8,128)(2,1)S(1)} %get-tuple-element.95), channel_id=1, source_target_pairs={{0,24},{8,16},{16,8},{24,0},{1,25},{9,17},{17,9},{25,1},{2,26},{10... | collective-permute-start | bytes 417800 | tf_op jit(solution)/shard_map/ppermute | solution.py:72
  250.2 9.1 %collective-permute-start.59 = (bf16[400,256]{1,0:T(8,128)(2,1)S(1)}, bf16[400,256]{1,0:T(8,128)(2,1)S(1)}, u32[]{:S(2)}, u32[]{:S(2)}) collective-permute-start(bf16[400,256]{1,0:T(8,128)(2,1)S(1)} %pad_maximum_fusion.refs_0_), channel_id=1, source_target_pairs={{0,3},{1,2},{2,1},{3,0},{4,7},{5,6},{6,5},{7,4},{8,11},{9,10},{10,... | collective-permute-start | bytes 614408 | tf_op jit(solution)/shard_map/ppermute | solution.py:72
  251.8 12.1 %collective-permute-start.58 = (bf16[400,256]{1,0:T(8,128)(2,1)S(1)}, bf16[400,256]{1,0:T(8,128)(2,1)S(1)}, u32[]{:S(2)}, u32[]{:S(2)}) collective-permute-start(bf16[400,256]{1,0:T(8,128)(2,1)S(1)} %pad_maximum_fusion.refs_0_), channel_id=1, source_target_pairs={{0,2},{1,3},{2,0},{3,1},{4,6},{5,7},{6,4},{7,5},{8,10},{9,11},{10,... | collective-permute-start | bytes 614408 | tf_op jit(solution)/shard_map/ppermute | solution.py:72
  252.7 11.3 %collective-permute-start.57 = (bf16[400,256]{1,0:T(8,128)(2,1)S(1)}, bf16[400,256]{1,0:T(8,128)(2,1)S(1)}, u32[]{:S(2)}, u32[]{:S(2)}) collective-permute-start(bf16[400,256]{1,0:T(8,128)(2,1)S(1)} %pad_maximum_fusion.refs_0_), channel_id=1, source_target_pairs={{0,1},{1,0},{2,3},{3,2},{4,5},{5,4},{6,7},{7,6},{8,9},{9,8},{10,11... | collective-permute-start | bytes 614408 | tf_op jit(solution)/shard_map/ppermute | solution.py:72
  252.9 16.3 %collective-permute-start.43 = (bf16[256,1024]{1,0:T(8,128)(2,1)}, bf16[256,1024]{1,0:T(8,128)(2,1)S(1)}, u32[]{:S(2)}, u32[]{:S(2)}) collective-permute-start(bf16[256,1024]{1,0:T(8,128)(2,1)} %copy-done.35), channel_id=1, source_target_pairs={{0,4},{4,0},{1,5},{5,1},{2,6},{6,2},{3,7},{7,3},{8,12},{12,8},{9,1... | collective-permute-start | bytes 1572872 | tf_op jit(solution)/shard_map/ppermute | solution.py:72
  265.3 9.3 %collective-permute-start.60 = (f32[16,256]{1,0:T(8,128)S(1)}, f32[16,256]{1,0:T(8,128)S(1)}, u32[]{:S(2)}, u32[]{:S(2)}) collective-permute-start(f32[16,256]{1,0:T(8,128)S(1)} %add_add_fusion), channel_id=1, source_target_pairs={{0,4},{4,0},{1,5},{5,1},{2,6},{6,2},{3,7},{7,3},{8,12},{12,8},{9,1... | collective-permute-start | bytes 49160 | tf_op jit(solution)/shard_map/ppermute | solution.py:72
  269.9 5.3 %collective-permute-start.44 = (bf16[64,1024]{1,0:T(8,128)(2,1)S(1)}, bf16[64,1024]{1,0:T(8,128)(2,1)S(1)}, u32[]{:S(2)}, u32[]{:S(2)}) collective-permute-start(bf16[64,1024]{1,0:T(8,128)(2,1)S(1)} %get-tuple-element.89), channel_id=1, source_target_pairs={{0,1},{1,0},{2,3},{3,2},{4,5},{5,4},{6,7},{7,6},{8,9},{9,8},{10,11... | collective-permute-start | bytes 393224 | tf_op jit(solution)/shard_map/ppermute | solution.py:72
  270.9 4.9 %collective-permute-start.45 = (bf16[64,1024]{1,0:T(8,128)(2,1)S(1)}, bf16[64,1024]{1,0:T(8,128)(2,1)S(1)}, u32[]{:S(2)}, u32[]{:S(2)}) collective-permute-start(bf16[64,1024]{1,0:T(8,128)(2,1)S(1)} %get-tuple-element.90), channel_id=1, source_target_pairs={{0,2},{1,3},{2,0},{3,1},{4,6},{5,7},{6,4},{7,5},{8,10},{9,11},{10,... | collective-permute-start | bytes 393224 | tf_op jit(solution)/shard_map/ppermute | solution.py:72
  271.4 7.3 %collective-permute-start.46 = (bf16[64,1024]{1,0:T(8,128)(2,1)S(1)}, bf16[64,1024]{1,0:T(8,128)(2,1)S(1)}, u32[]{:S(2)}, u32[]{:S(2)}) collective-permute-start(bf16[64,1024]{1,0:T(8,128)(2,1)S(1)} %get-tuple-element.91), channel_id=1, source_target_pairs={{0,3},{1,2},{2,1},{3,0},{4,7},{5,6},{6,5},{7,4},{8,11},{9,10},{10,... | collective-permute-start | bytes 393224 | tf_op jit(solution)/shard_map/ppermute | solution.py:72
  279.5 10.8 %collective-permute-start.50 = (bf16[64,1024]{1,0:T(8,128)(2,1)S(1)}, bf16[64,1024]{1,0:T(8,128)(2,1)S(1)}, u32[]{:S(2)}, u32[]{:S(2)}) collective-permute-start(bf16[64,1024]{1,0:T(8,128)(2,1)S(1)} %norm_one_back.1.refs_0_), channel_id=1, source_target_pairs={{0,4},{4,0},{1,5},{5,1},{2,6},{6,2},{3,7},{7,3},{8,12},{12,8},{9,1... | collective-permute-start | bytes 393224 | tf_op jit(solution)/shard_map/ppermute | solution.py:72
  280.5 6.0 %collective-permute-start.49 = (bf16[64,1024]{1,0:T(8,128)(2,1)S(1)}, bf16[64,1024]{1,0:T(8,128)(2,1)S(1)}, u32[]{:S(2)}, u32[]{:S(2)}) collective-permute-start(bf16[64,1024]{1,0:T(8,128)(2,1)S(1)} %norm_one_back.1.refs_0_), channel_id=1, source_target_pairs={{0,3},{1,2},{2,1},{3,0},{4,7},{5,6},{6,5},{7,4},{8,11},{9,10},{10,... | collective-permute-start | bytes 393224 | tf_op jit(solution)/shard_map/ppermute | solution.py:72
  281.7 8.1 %collective-permute-start.48 = (bf16[64,1024]{1,0:T(8,128)(2,1)S(1)}, bf16[64,1024]{1,0:T(8,128)(2,1)S(1)}, u32[]{:S(2)}, u32[]{:S(2)}) collective-permute-start(bf16[64,1024]{1,0:T(8,128)(2,1)S(1)} %norm_one_back.1.refs_0_), channel_id=1, source_target_pairs={{0,2},{1,3},{2,0},{3,1},{4,6},{5,7},{6,4},{7,5},{8,10},{9,11},{10,... | collective-permute-start | bytes 393224 | tf_op jit(solution)/shard_map/ppermute | solution.py:72
  282.2 7.9 %collective-permute-start.47 = (bf16[64,1024]{1,0:T(8,128)(2,1)S(1)}, bf16[64,1024]{1,0:T(8,128)(2,1)S(1)}, u32[]{:S(2)}, u32[]{:S(2)}) collective-permute-start(bf16[64,1024]{1,0:T(8,128)(2,1)S(1)} %norm_one_back.1.refs_0_), channel_id=1, source_target_pairs={{0,1},{1,0},{2,3},{3,2},{4,5},{5,4},{6,7},{7,6},{8,9},{9,8},{10,11... | collective-permute-start | bytes 393224 | tf_op jit(solution)/shard_map/ppermute | solution.py:72
  283.1 19.0 %collective-permute-start.62 = (bf16[576,256]{1,0:T(8,128)(2,1)}, bf16[576,256]{1,0:T(8,128)(2,1)S(1)}, u32[]{:S(2)}, u32[]{:S(2)}) collective-permute-start(bf16[576,256]{1,0:T(8,128)(2,1)} %reduce-scatter.8.cloned.1.call-done), channel_id=1, source_target_pairs={{0,4},{4,0},{1,5},{5,1},{2,6},{6,2},{3,7},{7,3},{8,12},{12,8},{9,1... | collective-permute-start | bytes 884744 | tf_op jit(solution)/shard_map/ppermute | solution.py:72
  286.5 13.7 %collective-permute-start.53 = (bf16[64,1024]{1,0:T(8,128)(2,1)S(1)}, bf16[64,1024]{1,0:T(8,128)(2,1)S(1)}, u32[]{:S(2)}, u32[]{:S(2)}) collective-permute-start(bf16[64,1024]{1,0:T(8,128)(2,1)S(1)} %collective-permute-done.49.refs_3_), channel_id=1, source_target_pairs={{0,4},{4,0},{1,5},{5,1},{2,6},{6,2},{3,7},{7,3},{8,12},{12,8},{9,1... | collective-permute-start | bytes 393224 | tf_op jit(solution)/shard_map/ppermute | solution.py:72
  289.7 10.4 %collective-permute-start.52 = (bf16[64,1024]{1,0:T(8,128)(2,1)S(1)}, bf16[64,1024]{1,0:T(8,128)(2,1)S(1)}, u32[]{:S(2)}, u32[]{:S(2)}) collective-permute-start(bf16[64,1024]{1,0:T(8,128)(2,1)S(1)} %collective-permute-done.48.refs_2_), channel_id=1, source_target_pairs={{0,4},{4,0},{1,5},{5,1},{2,6},{6,2},{3,7},{7,3},{8,12},{12,8},{9,1... | collective-permute-start | bytes 393224 | tf_op jit(solution)/shard_map/ppermute | solution.py:72
  290.1 10.0 %collective-permute-start.51 = (bf16[64,1024]{1,0:T(8,128)(2,1)S(1)}, bf16[64,1024]{1,0:T(8,128)(2,1)S(1)}, u32[]{:S(2)}, u32[]{:S(2)}) collective-permute-start(bf16[64,1024]{1,0:T(8,128)(2,1)S(1)} %collective-permute-done.47.refs_1_), channel_id=1, source_target_pairs={{0,4},{4,0},{1,5},{5,1},{2,6},{6,2},{3,7},{7,3},{8,12},{12,8},{9,1... | collective-permute-start | bytes 393224 | tf_op jit(solution)/shard_map/ppermute | solution.py:72
  298.7 4.6 %collective-permute-start.61 = (bf16[256,1152]{1,0:T(8,128)(2,1)}, bf16[256,1152]{1,0:T(8,128)(2,1)S(1)}, u32[]{:S(2)}, u32[]{:S(2)}) collective-permute-start(bf16[256,1152]{1,0:T(8,128)(2,1)} %reduce-scatter.6.cloned.1.call-done), channel_id=1, source_target_pairs={{0,4},{4,0},{1,5},{5,1},{2,6},{6,2},{3,7},{7,3},{8,12},{12,8},{9,1... | collective-permute-start | bytes 1769480 | tf_op jit(solution)/shard_map/ppermute | solution.py:72
  (62 other events, 565.5 us)
Sparse Core Ops, SparseCore 0:
  183.2 23.8 reduce-scatter.3
  210.1 37.5 reduce-scatter.7
  250.1 48.6 reduce-scatter.5
Sparse Core Ops, SparseCore 1:
  196.1 63.9 all-reduce.2

commit v2 on v1

v2 whole, which is shorter than its diff:
```python
import math

import jax
import jax.numpy as jnp
import numpy as np
from jax import lax
from jax.experimental import pallas as pl
from jax.experimental.pallas import tpu as pltpu
from jax.sharding import PartitionSpec as P

EPSILON = 1e-05
ROPE_THETA = 1000000.0
BF = jnp.bfloat16
F32 = jnp.float32
MIB = 1 << 20
GAIN_ROWS = 16
ROUTE_A = [(0, 1), (1, 3), (2, 0), (3, 2)]
ROUTE_B = [(0, 2), (1, 0), (2, 3), (3, 1)]


def nn_dot(a, b):
    return lax.dot_general(a, b, (((1,), (0,)), ((), ())), preferred_element_type=F32)


def nt_dot(a, b):
    return lax.dot_general(a, b, (((1,), (1,)), ((), ())), preferred_element_type=F32)


def tn_dot(a, b):
    return lax.dot_general(a, b, (((0,), (0,)), ((), ())), preferred_element_type=F32)


def call(kernel, outs, ids, arrays, scratch=(), vmem=32, flops=0, name=None, n_hbm=0):
    shapes = [jax.ShapeDtypeStruct(s, d) for s, d in outs]
    moved = sum(a.size * a.dtype.itemsize for a in arrays)
    moved += sum(math.prod(s.shape) * s.dtype.itemsize for s in shapes)
    return pl.pallas_call(
        kernel,
        out_shape=shapes,
        in_specs=[pl.BlockSpec(memory_space=pltpu.SMEM)]
        + [pl.BlockSpec(memory_space=pltpu.HBM) for _ in range(n_hbm)]
        + [pl.BlockSpec(memory_space=pltpu.VMEM) for _ in arrays[n_hbm:]],
        out_specs=[pl.BlockSpec(memory_space=pltpu.VMEM) for _ in shapes],
        scratch_shapes=list(scratch),
        compiler_params=pltpu.CompilerParams(vmem_limit_bytes=vmem * MIB),
        cost_estimate=pl.CostEstimate(flops=int(flops), bytes_accessed=int(moved), transcendentals=0),
        name=name,
    )(ids, *arrays)


def lanes(shape):
    return lax.broadcasted_iota(jnp.int32, shape, 1)


def head_mean(v, low):
    first = jnp.sum(jnp.where(low, v, 0.0), axis=1, keepdims=True)
    second = jnp.sum(jnp.where(low, 0.0, v), axis=1, keepdims=True)
    return jnp.where(low, first, second) * (1.0 / 64.0)


def turn(v, first):
    return jnp.where(first, -pltpu.roll(v, 96, 1), pltpu.roll(v, 32, 1))


def turn_back(v, first):
    return jnp.where(first, pltpu.roll(v, 96, 1), -pltpu.roll(v, 32, 1))


def tree(values, dtype=F32):
    values = [v.astype(F32) for v in values]
    while len(values) > 1:
        pairs = [values[i] + values[i + 1] for i in range(0, len(values) - 1, 2)]
        values = pairs + values[len(values) - len(values) % 2 :]
    return values[0].astype(dtype)


def make(mesh):
    n_shard, n_heads, n_tensor = (mesh.shape[a] for a in ("shard", "heads", "tensor"))
    blocks_mode = n_shard == 4
    n_plane = n_heads * n_tensor

    def swap(x, axis, k):
        size = mesh.shape[axis]
        return lax.ppermute(x, axis, [(i, i ^ k) for i in range(size)])

    def route(x, pairs, back):
        return lax.ppermute(x, "shard", [(b, a) for a, b in pairs] if back else pairs)

    def inner():
        z = lax.axis_index("shard")
        return (z == 1) | (z == 2)

    def shard_blocks(x):
        return [x, route(x, ROUTE_A, False), route(x, ROUTE_B, False), swap(x, "shard", 3)]

    def after(values, *first):
        return lax.optimization_barrier((*values, *first))[: len(values)]

    def shard_sum(blocks):
        a, b = route(blocks[1], ROUTE_A, True), route(blocks[2], ROUTE_B, True)
        near, far = jnp.where(inner(), b, a), jnp.where(inner(), a, b)
        return tree([blocks[0], near, far, swap(blocks[3], "shard", 3)], BF)

    def shard_sum_staged(blocks, later):
        (found,) = after((swap(blocks[3], "shard", 1),), later)
        found = found.astype(F32)
        a = (blocks[1].astype(F32) + jnp.where(inner(), 0.0, found)).astype(BF)
        b = (blocks[2].astype(F32) + jnp.where(inner(), found, 0.0)).astype(BF)
        return blocks[0], route(a, ROUTE_A, True), b

    def plane_blocks(x):
        same = [x] + [swap(x, "tensor", k) for k in range(1, n_tensor)]
        found = list(same)
        for i in range(1, n_heads):
            found += [swap(s, "heads", i) for s in same]
        return found

    def plane_index(ids, b):
        return (ids[1] ^ (b // n_tensor)) * n_tensor + (ids[2] ^ (b % n_tensor))

    def on_device(
        block_input,
        attn_gain,
        query_weight,
        key_weight,
        value_weight,
        query_gain,
        key_gain,
        output_weight,
        ffn_gain,
        gate_weight,
        up_weight,
        down_weight,
        lengths,
        packing,
        out_grad,
    ):
        rows, width = block_input.shape
        depth = query_weight.shape[0]
        head = query_gain.shape[0]
        hidden_all = gate_weight.shape[1]
        hid = hidden_all // n_heads
        q_cols = query_weight.shape[1] // n_tensor
        k_cols = key_weight.shape[1] // n_tensor
        n_block = n_shard if blocks_mode else 1
        wide = width // n_block
        padded = -(-hid // 128) * 128
        whole = 2 * hid
        sub = rows // n_plane
        half = rows // n_heads
        step = half
        z, h, t = (lax.axis_index(a) for a in ("shard", "heads", "tensor"))
        if blocks_mode:
            ids = jnp.stack([z, h, t, z, z ^ jnp.where(inner(), 1, 2), z ^ jnp.where(inner(), 2, 1), z ^ 3])
        else:
            ids = jnp.stack([z, h, t])
        ids = ids.astype(jnp.int32)

        def owner(ids_ref, k):
            return ids_ref[3 + k]

        def offset(ids_ref, k):
            return pl.multiple_of(owner(ids_ref, k) * wide, wide) if blocks_mode else 0

        def fetch(pairs, sems):
            copies = [pltpu.make_async_copy(a, b, sems.at[i]) for i, (a, b) in enumerate(pairs)]
            for copy in copies:
                copy.start()
            return copies

        def share_attn(ids_ref, q_hbm, k_hbm, v_hbm, o_hbm, ag_hbm, fg_hbm, *outs):
            own_ref = outs[0]
            q_ref, k_ref, v_ref, ag_ref, fg_ref, sems = outs[-6:]
            i = ids_ref[2]
            tile = pl.ds(pl.multiple_of((i // 2) * 128, 128), 128)
            at = pl.multiple_of(i * q_cols, q_cols)
            out_ref = own_ref.at[depth + GAIN_ROWS :, :] if blocks_mode else outs[2]
            copies = fetch(
                [
                    (ag_hbm, ag_ref),
                    (fg_hbm, fg_ref),
                    (q_hbm.at[:, pl.ds(at, q_cols)], q_ref),
                    (k_hbm.at[:, tile], k_ref),
                    (v_hbm.at[:, tile], v_ref),
                    (o_hbm.at[pl.ds(at, q_cols), :], out_ref),
                ],
                sems,
            )
            for copy in copies:
                copy.wait()
            both = [ag_ref[...].astype(F32).reshape(1, depth), fg_ref[...].astype(F32).reshape(1, depth)]
            both = jnp.concatenate(both + [jnp.zeros((GAIN_ROWS - 2, depth), F32)], axis=0).astype(BF)
            if blocks_mode:
                own_ref[depth : depth + GAIN_ROWS, :] = both
            else:
                outs[1][...] = both
            own_ref[:depth, :128] = q_ref[...]
            k_, v_ = k_ref[...].astype(F32), v_ref[...].astype(F32)
            even = (i % 2) == 0
            low = lanes((depth, 128)) < 64
            k_ = jnp.where(even, k_, pltpu.roll(k_, 64, 1))
            v_ = jnp.where(even, pltpu.roll(v_, 64, 1), v_)
            own_ref[:depth, 128:] = jnp.where(low, k_, v_).astype(BF)

        if blocks_mode:
            share_shapes = [((depth + GAIN_ROWS + q_cols, 256), BF)]
        else:
            share_shapes = [((depth, 256), BF), ((GAIN_ROWS, depth), BF), ((q_cols, depth), BF)]
        own_attn, *own_more = call(
            share_attn,
            share_shapes,
            ids,
            [query_weight, key_weight, value_weight, output_weight, attn_gain, ffn_gain],
            scratch=[pltpu.VMEM((depth, 128), BF)] * 3
            + [pltpu.VMEM((depth,), BF)] * 2
            + [pltpu.SemaphoreType.DMA((6,))],
            vmem=56,
            n_hbm=6,
            name="share_attn",
        )

        def share_ffn(ids_ref, g_hbm, u_hbm, d_hbm, own_ref, g_ref, u_ref, sems):
            rows_ = pl.ds(pl.multiple_of(ids_ref[1] * hid, 16), hid)
            pairs = [(g_hbm, g_ref), (u_hbm, u_ref), (d_hbm.at[rows_, :], own_ref.at[whole:, :])]
            for copy in fetch(pairs, sems):
                copy.wait()
            for i, ref in enumerate((g_ref, u_ref)):
                part = ref[...].astype(F32)
                part = jnp.where(ids_ref[1] == 0, part, pltpu.roll(part, hid, 1))[:, :padded]
                own_ref[i * hid : (i + 1) * hid, :] = part.T[:hid].astype(BF)

        (own_ffn,) = call(
            share_ffn,
            [((whole + hid, depth), BF)],
            ids,
            [gate_weight, up_weight, down_weight],
            scratch=[
                pltpu.VMEM((depth, whole), BF),
                pltpu.VMEM((depth, whole), BF),
                pltpu.SemaphoreType.DMA((3,)),
            ],
            vmem=8,
            n_hbm=3,
            name="share_ffn",
        )

        count = lengths.shape[0]
        frequency = np.power(np.float64(ROPE_THETA), -np.arange(head // 2) * (2.0 / head))
        frequency = jnp.asarray(np.tile(frequency, 4)[None].astype(np.float32))

        def layout(ids_ref, len_hbm, pack_hbm, freq_hbm, qg_hbm, kg_hbm, *refs):
            info_ref, angle_ref, hg_ref, len_ref, pack_ref, freq_ref, qg_ref, kg_ref, sems = refs
            pairs = [(len_hbm, len_ref), (pack_hbm, pack_ref), (freq_hbm, freq_ref), (qg_hbm, qg_ref), (kg_hbm, kg_ref)]
            for copy in fetch(pairs, sems):
                copy.wait()
            token = ids_ref[0] * rows + lax.broadcasted_iota(jnp.int32, (rows, 128), 0)
            start = jnp.zeros((rows, 128), jnp.int32)
            end = jnp.int32(0)
            for j in range(count):
                end = end + len_ref[pack_ref[j]]
                start = jnp.where(token >= end, end, start)
            live = token < end
            lowest = jnp.where(live, start, token).astype(F32)
            info_ref[...] = jnp.where(lanes((rows, 128)) == 0, lowest, live.astype(F32))
            angle_ref[...] = (token - start).astype(F32) * freq_ref[...]
            q, k_ = qg_ref[...].astype(F32).reshape(1, head), kg_ref[...].astype(F32).reshape(1, head)
            q = jnp.concatenate([q, q], axis=1)
            k_ = jnp.concatenate([k_, jnp.ones((1, head), F32)], axis=1)
            hg_ref[:8, :] = jnp.broadcast_to(q, (8, 128))
            hg_ref[8:, :] = jnp.broadcast_to(k_, (8, 128))

        row_info, angles, head_gains = call(
            layout,
            [((rows, 128), F32), ((rows, 128), F32), ((16, 128), F32)],
            ids,
            [lengths, packing, frequency, query_gain, key_gain],
            scratch=[
                pltpu.SMEM((count,), jnp.int32),
                pltpu.SMEM((count,), jnp.int32),
                pltpu.VMEM((1, 128), F32),
                pltpu.VMEM((head,), BF),
                pltpu.VMEM((head,), BF),
                pltpu.SemaphoreType.DMA((5,)),
            ],
            vmem=2,
            n_hbm=5,
            name="layout",
        )
        cosine, sine = jnp.cos(angles), jnp.sin(angles)

        if blocks_mode:
            attn_parts = shard_blocks(own_attn)
            gain_parts = []
        else:
            gather = lambda x, axis: [lax.all_gather(x, "shard", axis=axis, tiled=True)]
            attn_parts = gather(own_attn, 0)
            gain_parts = gather(own_more[0], 1)
            out_parts = gather(own_more[1], 1)
            ffn_parts = gather(own_ffn, 1)

        def project(ids_ref, x_ref, cos_ref, sin_ref, hg_ref, *refs):
            w_refs, refs = refs[:n_block], refs[n_block:]
            g_refs, refs = refs[: len(gain_parts)], refs[len(gain_parts) :]
            n_ref, raw_ref, qs_ref, kv_ref, ga_ref, gf_ref = refs
            for k in range(n_block):
                both = (g_refs[0][...] if g_refs else w_refs[k][wide : wide + GAIN_ROWS, :]).astype(F32)
                where = pl.ds(offset(ids_ref, k), wide)
                ga_ref[:, where] = jnp.broadcast_to(both[0:1], (8, wide))
                gf_ref[:, where] = jnp.broadcast_to(both[1:2], (8, wide))
            step = 128

            def body(c, carry):
                at = pl.ds(pl.multiple_of(c * step, step), step)
                x = x_ref[at, :].astype(F32)
                r = lax.rsqrt(jnp.mean(x * x, axis=1, keepdims=True) + EPSILON)
                n_ref[at, :] = (x * r * ga_ref[0:1, :]).astype(BF)
                acc = jnp.zeros((step, 256), F32)
                for k in range(n_block):
                    acc += nn_dot(n_ref[at, pl.ds(offset(ids_ref, k), wide)], w_refs[k][:wide, :])
                raw_ref[at, :] = acc
                lane = lanes((step, 128))
                low, first = lane < 64, (lane % 64) < 32
                cos, sin = cos_ref[at, :], sin_ref[at, :]
                q, kv = acc[:, :128], acc[:, 128:]
                q = q * lax.rsqrt(head_mean(q * q, low) + EPSILON) * hg_ref[0:1, :]
                q = (q * cos + turn(q, first) * sin).astype(BF).astype(F32) * (1.0 / math.sqrt(head))
                qs_ref[at, :] = jnp.where(low, q, 0.0).astype(BF)
                qs_ref[pl.ds(pl.multiple_of(rows + c * step, step), step), :] = jnp.where(
                    low, pltpu.roll(q, 64, 1), 0.0
                ).astype(BF)
                k_ = kv * lax.rsqrt(head_mean(kv * kv, low) + EPSILON) * hg_ref[8:9, :]
                k_ = k_ * cos + turn(k_, first) * sin
                kv_ref[at, :] = jnp.where(low, k_, kv).astype(BF)
                return carry

            lax.fori_loop(0, rows // step, body, 0)

        normed_one, raw, queries, own_kv, ga, gf = call(
            project,
            [
                ((rows, width), BF),
                ((rows, 256), F32),
                ((2 * rows, 128), BF),
                ((rows, 128), BF),
                ((8, width), F32),
                ((8, width), F32),
            ],
            ids,
            [block_input, cosine, sine, head_gains, *attn_parts, *gain_parts],
            flops=2 * rows * width * 256,
            vmem=4,
            name="project",
        )
        if blocks_mode:
            kv_parts = shard_blocks(own_kv)
            (own_ffn,) = after((own_ffn,), *kv_parts[1:])
            ffn_a, ffn_b = route(own_ffn, ROUTE_A, False), route(own_ffn, ROUTE_B, False)
        else:
            kv_parts = [lax.all_gather(own_kv, "shard", axis=0, tiled=True)]

        if blocks_mode:

            def beside(ids_ref, *refs):
                for k in range(n_block):
                    refs[-1][:, pl.ds(offset(ids_ref, k), wide)] = refs[k][wide + GAIN_ROWS :, :]

            late = after(attn_parts, *kv_parts[1:])
            (own_rows,) = call(beside, [((q_cols, width), BF)], ids, late, vmem=1, name="beside")
        else:
            own_rows = out_parts[0]
        row_parts = [own_rows] + [swap(own_rows, "tensor", k) for k in range(1, n_tensor)]

        def below(ids_ref, *refs):
            for k in range(n_tensor):
                at = pl.multiple_of((ids_ref[2] ^ k) * q_cols, q_cols)
                refs[-1][pl.ds(at, q_cols), :] = refs[k][...]

        (out_half,) = call(
            below, [((n_tensor * q_cols, width), BF)], ids, row_parts, vmem=1, name="below"
        )
        out_halves = [out_half, swap(out_half, "heads", 1)]

        chunk = 256

        def over_keys(ids_ref, kv_refs, block):
            if blocks_mode:
                for k in range(n_block):
                    pl.when(owner(ids_ref, k) <= ids_ref[0])(
                        lambda k=k: block(owner(ids_ref, k), kv_refs[k], 0)
                    )
            else:

                def step(j, carry):
                    block(j, kv_refs[0], pl.multiple_of(j * rows, rows))
                    return carry

                lax.fori_loop(0, ids_ref[0] + 1, step, 0)

        def masked_exp(ids_ref, info_ref, score, c, own):
            row = (c * chunk) % rows
            at = pl.ds(pl.multiple_of(row, chunk), chunk)
            col = lanes((chunk, rows))
            lowest_ = info_ref[at, 0:1].astype(jnp.int32) - own * rows
            mine = lax.broadcasted_iota(jnp.int32, (chunk, 1), 0) + (row + (ids_ref[0] - own) * rows)
            return jnp.where((col >= lowest_) & (col <= mine), jnp.exp(score), 0.0)

        def attend(ids_ref, info_ref, qs_ref, *refs):
            kv_refs, (att_ref, oa_ref, acc_ref) = refs[:n_block], refs[n_block:]
            acc_ref[...] = jnp.zeros_like(acc_ref)
            low = lanes((rows, 128)) < 64

            def block(own, kv_ref, base):
                kv = kv_ref[pl.ds(base, rows), :]
                counted = jnp.where(low, 1.0, kv.astype(F32)).astype(BF)

                def body(c, carry):
                    at = pl.ds(pl.multiple_of(c * chunk, chunk), chunk)
                    p = masked_exp(ids_ref, info_ref, nt_dot(qs_ref[at, :], kv), c, own)
                    acc_ref[at, :] += nn_dot(p.astype(BF), counted)
                    return carry

                lax.fori_loop(0, 2 * rows // chunk, body, 0)

            over_keys(ids_ref, kv_refs, block)
            for i in range(2):
                acc = acc_ref[i * rows : (i + 1) * rows, :]
                inverse = 1.0 / jnp.where(low, acc, 1.0)
                done = jnp.where(low, inverse, acc * pltpu.roll(inverse, 64, 1))
                oa_ref[i * rows : (i + 1) * rows, :] = done
            att_ref[...] = jnp.where(
                low, pltpu.roll(oa_ref[:rows, :], 64, 1), oa_ref[rows:, :]
            ).astype(BF)

        attended, out_and_inverse = call(
            attend,
            [((rows, 128), BF), ((2 * rows, 128), F32)],
            ids,
            [row_info, queries, *kv_parts],
            scratch=[pltpu.VMEM((2 * rows, 128), F32)],
            flops=4 * 2 * rows * rows * n_shard * 128,
            vmem=4,
            name="attend",
        )
        attended_parts = plane_blocks(attended)

        def my_rows(ids_ref):
            return pl.ds(pl.multiple_of((ids_ref[1] * n_tensor + ids_ref[2]) * sub, sub), sub)

        def middle_part(ids_ref, x_ref, gf_ref, *refs):
            wo_refs, refs = refs[:n_heads], refs[n_heads:]
            a_refs, (n2_ref, mid_ref, a_ref, m_ref) = refs[:n_plane], refs[n_plane:]
            deep = n_tensor * q_cols
            for b in range(n_plane):
                at = pl.multiple_of(plane_index(ids_ref, b) * q_cols, q_cols)
                a_ref[:, pl.ds(at, q_cols)] = a_refs[b][...]

            def body(c, carry):
                at = pl.ds(pl.multiple_of(c * step, step), step)
                parts = [
                    nn_dot(a_ref[at, pl.ds(pl.multiple_of((ids_ref[1] ^ i) * deep, deep), deep)], wo_refs[i][...])
                    for i in range(n_heads)
                ]
                middle = x_ref[at, :].astype(F32) + tree(parts)
                m_ref[at, :] = middle
                r = lax.rsqrt(jnp.mean(middle * middle, axis=1, keepdims=True) + EPSILON)
                n2_ref[at, :] = (middle * r * gf_ref[0:1, :]).astype(BF)
                return carry

            lax.fori_loop(0, n_heads, body, 0)
            mid_ref[...] = m_ref[my_rows(ids_ref), :]

        normed_two, middle = call(
            middle_part,
            [((rows, width), BF), ((sub, width), F32)],
            ids,
            [block_input, gf, *out_halves, *attended_parts],
            scratch=[pltpu.VMEM((rows, width), BF), pltpu.VMEM((rows, width), F32)],
            flops=2 * rows * width * width,
            vmem=8,
            name="middle",
        )

        if blocks_mode:
            (chosen,) = after((jnp.where(inner(), ffn_b, ffn_a),), *attended_parts[1:n_tensor])
            ffn_parts = [own_ffn, ffn_a, ffn_b, swap(chosen, "shard", 1)]

        def feed_forward(ids_ref, info_ref, og_ref, n2_ref, *refs):
            w_refs, refs = refs[:n_block], refs[n_block:]
            send_ref, keep_ref, fo_send_ref, fo_keep_ref, dg_ref, du_ref, hid_ref, cot_ref, both_ref = refs

            def body(c, carry):
                at = pl.ds(pl.multiple_of(c * step, step), step)
                cot_ref[at, :] = (og_ref[at, :].astype(F32) * info_ref[at, 1:2]).astype(BF)
                gate = up = dh = jnp.zeros((step, hid), F32)
                for k in range(n_block):
                    cols = pl.ds(offset(ids_ref, k), wide)
                    gate += nt_dot(n2_ref[at, cols], w_refs[k][:hid, :])
                    up += nt_dot(n2_ref[at, cols], w_refs[k][hid:whole, :])
                    dh += nt_dot(cot_ref[at, cols], w_refs[k][whole:, :])
                sig = 1.0 / (1.0 + jnp.exp(-gate))
                act = gate * sig
                hid_ref[at, :] = (act * up).astype(BF)
                dg_ref[at, :] = (dh * up * sig * (1.0 + gate * (1.0 - sig))).astype(BF)
                du_ref[at, :] = (dh * act).astype(BF)
                for k in range(n_block):
                    off = offset(ids_ref, k)
                    dn = nn_dot(dg_ref[at, :], w_refs[k][:hid, :]) + nn_dot(du_ref[at, :], w_refs[k][hid:whole, :])
                    both_ref[:, pl.ds(off, wide)] = dn.astype(BF)
                    off = pl.multiple_of(width + off, wide)
                    both_ref[:, pl.ds(off, wide)] = nn_dot(hid_ref[at, :], w_refs[k][whole:, :]).astype(BF)

                @pl.when(c == ids_ref[1])
                def _():
                    keep_ref[...] = both_ref[:, :width]
                    fo_keep_ref[...] = both_ref[:, width:]

                @pl.when(c != ids_ref[1])
                def _():
                    send_ref[...] = both_ref[:, :width]
                    fo_send_ref[...] = both_ref[:, width:]

                return carry

            lax.fori_loop(0, n_heads, body, 0)

        dn_send, dn_keep, fo_send, fo_keep, d_gate, d_up, hidden, cot = call(
            feed_forward,
            [
                ((half, width), BF),
                ((half, width), BF),
                ((half, width), BF),
                ((half, width), BF),
                ((rows, hid), BF),
                ((rows, hid), BF),
                ((rows, hid), BF),
                ((rows, width), BF),
            ],
            ids,
            [row_info, out_grad, normed_two, *ffn_parts],
            scratch=[pltpu.VMEM((half, 2 * width), BF)],
            flops=2 * rows * width * 6 * hid,
            vmem=14,
            name="feed_forward",
        )

        def split(ids_ref, keep_ref, got_ref, *outs):
            for k in range(n_tensor):
                at = pl.ds(pl.multiple_of((ids_ref[2] ^ k) * sub, sub), sub)
                total = keep_ref[at, :].astype(F32) + got_ref[at, :].astype(F32)
                outs[k][...] = total.astype(BF)

        def plane_halves(keep, send):
            got = swap(send, "heads", 1)
            return call(split, [((sub, width), BF)] * n_tensor, ids, [keep, got], vmem=2, name="split")

        def plane_sum_parts(parts):
            return [parts[0]] + [swap(parts[k], "tensor", k) for k in range(1, n_tensor)]

        dn_parts = plane_sum_parts(plane_halves(dn_keep, dn_send))

        def ffn_grads(ids_ref, n2_ref, cot_ref, dg_ref, du_ref, hid_ref, *outs):
            outs, turned_ref = outs[:-1], outs[-1]
            for i, ref in enumerate((dg_ref, du_ref, hid_ref)):
                turned_ref[i * hid : (i + 1) * hid, :] = ref[...].T
            for k in range(n_block):
                cols = pl.ds(offset(ids_ref, k), wide)
                outs[k][:whole, :] = nn_dot(turned_ref[:whole, :], n2_ref[:, cols]).astype(BF)
                outs[k][whole:, :] = nn_dot(turned_ref[whole:, :], cot_ref[:, cols]).astype(BF)

        grad_ffn = call(
            ffn_grads,
            [((whole + hid, wide), BF)] * n_block,
            ids,
            [normed_two, cot, d_gate, d_up, hidden],
            scratch=[pltpu.VMEM((whole + hid, rows), BF)],
            flops=2 * rows * width * 3 * hid,
            vmem=8,
            name="ffn_grads",
        )
        (first_part,) = after((dn_parts[0],), grad_ffn[0])
        dn_parts = [first_part] + dn_parts[1:]

        def norm_two_back(ids_ref, mid_ref, cot_ref, gf_ref, *refs):
            part_refs, (dm_ref, da_ref, gp_ref) = refs[:n_tensor], refs[n_tensor:]
            d = tree([p[...] for p in part_refs])
            v = mid_ref[...]
            r = lax.rsqrt(jnp.mean(v * v, axis=1, keepdims=True) + EPSILON)
            w = v * r
            wd = d * gf_ref[0:1, :]
            cot_ = cot_ref[my_rows(ids_ref), :].astype(F32)
            dm = cot_ + r * (wd - w * jnp.mean(wd * w, axis=1, keepdims=True))
            dm_ref[...] = dm
            da_ref[...] = dm.astype(BF)
            gp_ref[...] = jnp.broadcast_to(jnp.sum(d * w, axis=0, keepdims=True), gp_ref.shape)

        d_middle, d_attn, ffn_gain_part = call(
            norm_two_back,
            [((sub, width), F32), ((sub, width), BF), ((8, width), F32)],
            ids,
            [middle, cot, gf, *dn_parts],
            vmem=4,
            name="norm_two_back",
        )
        if blocks_mode:
            ffn_own, first_route, second_route = shard_sum_staged(grad_ffn, d_attn)
        else:
            ffn_sum = lax.psum_scatter(grad_ffn[0], "shard", scatter_dimension=1, tiled=True)
        row_blocks = plane_blocks(d_attn)
        fo_halves = plane_halves(fo_keep, after((fo_send,), d_attn)[0])

        def attend_back(ids_ref, info_ref, qs_ref, oa_ref, wo_ref, *refs):
            d_refs, refs = refs[:n_plane], refs[n_plane:]
            kv_refs, refs = refs[:n_block], refs[n_block:]
            dq_ref, da_ref, dkv_refs = refs[0], refs[1], refs[2 : 2 + n_block]
            do_ref, delta_ref, dqs_ref, acc_ref = refs[2 + n_block :]
            for b in range(n_plane):
                at = pl.multiple_of(plane_index(ids_ref, b) * sub, sub)
                da_ref[pl.ds(at, sub), :] = d_refs[b][...]
            low = lanes((rows, 128)) < 64
            do = nt_dot(da_ref[...], wo_ref[...]).astype(BF).astype(F32)
            first = jnp.where(low, 0.0, pltpu.roll(do, 64, 1))
            second = jnp.where(low, 0.0, do)
            do_ref[:rows, :] = first.astype(BF)
            do_ref[rows:, :] = second.astype(BF)
            delta_ref[:rows, :] = jnp.broadcast_to(
                jnp.sum(first * oa_ref[:rows, :], axis=1, keepdims=True), (rows, 128)
            )
            delta_ref[rows:, :] = jnp.broadcast_to(
                jnp.sum(second * oa_ref[rows:, :], axis=1, keepdims=True), (rows, 128)
            )
            dqs_ref[...] = jnp.zeros_like(dqs_ref)
            for k in range(n_block):
                dkv_refs[k][...] = jnp.zeros_like(dkv_refs[k])

            def block(own, kv_ref, base, out_ref):
                kv = kv_ref[pl.ds(base, rows), :]
                acc_ref[...] = jnp.zeros_like(acc_ref)

                def body(c, carry):
                    at = pl.ds(pl.multiple_of(c * chunk, chunk), chunk)
                    q, d_out = qs_ref[at, :], do_ref[at, :]
                    p = masked_exp(ids_ref, info_ref, nt_dot(q, kv), c, own) * oa_ref[at, 0:1]
                    ds = (p * (nt_dot(d_out, kv) - delta_ref[at, 0:1])).astype(BF)
                    dqs_ref[at, :] += nn_dot(ds, kv)
                    acc_ref[...] += tn_dot(ds, q) + tn_dot(p.astype(BF), d_out)
                    return carry

                lax.fori_loop(0, 2 * rows // chunk, body, 0)
                out_ref[pl.ds(base, rows), :] = acc_ref[...].astype(BF)

            if blocks_mode:
                for k in range(n_block):
                    pl.when(owner(ids_ref, k) <= ids_ref[0])(
                        lambda k=k: block(owner(ids_ref, k), kv_refs[k], 0, dkv_refs[k])
                    )
            else:

                def step(j, carry):
                    block(j, kv_refs[0], pl.multiple_of(j * rows, rows), dkv_refs[0])
                    return carry

                lax.fori_loop(0, ids_ref[0] + 1, step, 0)
            dq_ref[...] = jnp.where(low, dqs_ref[:rows, :], pltpu.roll(dqs_ref[rows:, :], 64, 1))

        d_query, d_attn_full, *d_kv = call(
            attend_back,
            [((rows, 128), F32), ((rows, width), BF)]
            + [((rows * (1 if blocks_mode else n_shard), 128), BF)] * n_block,
            ids,
            [row_info, queries, out_and_inverse, own_rows, *row_blocks, *kv_parts],
            scratch=[
                pltpu.VMEM((2 * rows, 128), BF),
                pltpu.VMEM((2 * rows, 128), F32),
                pltpu.VMEM((2 * rows, 128), F32),
                pltpu.VMEM((rows, 128), F32),
            ],
            flops=10 * 2 * rows * rows * n_shard * 128,
            vmem=6,
            name="attend_back",
        )
        if blocks_mode:
            d_kv = after(d_kv, first_route)
            d_kv_parts = [d_kv[0], route(d_kv[1], ROUTE_A, True), route(d_kv[2], ROUTE_B, True)]
            d_kv_parts.append(swap(d_kv[3], "shard", 3))
            (second_route,) = after((second_route,), *d_kv_parts[1:])
            second_route = route(second_route, ROUTE_B, True)
        else:
            d_kv_parts = [lax.psum_scatter(d_kv[0], "shard", scatter_dimension=0, tiled=True)]

        fo_parts = plane_sum_parts(after(fo_halves, d_query))

        def finish(ids_ref, info_ref, mid_ref, *refs):
            part_refs, out_ref = refs[:n_tensor], refs[n_tensor]
            total = mid_ref[...] + tree([p[...] for p in part_refs])
            out_ref[...] = (info_ref[my_rows(ids_ref), 1:2] * total).astype(BF)

        (output_block,) = call(
            finish, [((sub, width), BF)], ids, [row_info, middle, *fo_parts], vmem=4, name="finish"
        )
        output_parts = plane_blocks(output_block)

        def stack_rows(ids_ref, *refs):
            for b in range(n_plane):
                at = pl.multiple_of(plane_index(ids_ref, b) * sub, sub)
                refs[-1][pl.ds(at, sub), :] = refs[b][...].astype(refs[-1].dtype)

        (block_output,) = call(
            stack_rows, [((rows, width), BF)], ids, output_parts, vmem=2, name="stack_output"
        )

        def out_grads(ids_ref, att_ref, da_ref, *outs):
            for k in range(n_block):
                outs[k][...] = tn_dot(att_ref[...], da_ref[:, pl.ds(offset(ids_ref, k), wide)]).astype(BF)

        grad_out = call(
            out_grads,
            [((q_cols, wide), BF)] * n_block,
            ids,
            [attended, d_attn_full],
            flops=2 * rows * width * q_cols,
            vmem=4,
            name="out_grads",
        )

        def project_back(ids_ref, x_ref, n_ref, raw_ref, dq_ref, cos_ref, sin_ref, hg_ref, gp_ref, *refs):
            dkv_refs, refs = refs[:n_block], refs[n_block:]
            w_refs, refs = refs[:n_block], refs[n_block:]
            if blocks_mode:
                gwo_refs, refs = refs[:n_block], refs[n_block:]
            send_ref, keep_ref, g_refs = refs[0], refs[1], refs[2 : 2 + n_block]
            low_ref, r_ref = refs[-2:]
            lane = lanes((rows, 128))
            low, first = lane < 64, (lane % 64) < 32
            cos, sin = cos_ref[...], sin_ref[...]

            def back(v, g, d):
                d = d * cos + turn_back(d * sin, first)
                r = lax.rsqrt(head_mean(v * v, low) + EPSILON)
                w = v * r
                wd = d * g
                return r * (wd - w * head_mean(wd * w, low)), jnp.sum(d * w, axis=0, keepdims=True)

            scale = 1.0 / math.sqrt(head)
            dq, gain_q = back(raw_ref[:, :128], hg_ref[0:1, :], dq_ref[...] * scale)
            dkv = tree([p[...] for p in dkv_refs])
            dk, gain_k = back(raw_ref[:, 128:], hg_ref[8:9, :], dkv)
            low_ref[:, :128] = dq.astype(BF)
            low_ref[:, 128:] = jnp.where(low, dk, dkv).astype(BF)
            gain_q = gain_q + pltpu.roll(jnp.broadcast_to(gain_q, (8, 128)), 64, 1)[0:1]
            head_row = jnp.where(low[0:1], gain_q, pltpu.roll(jnp.broadcast_to(gain_k, (8, 128)), 64, 1)[0:1])
            head_row = jnp.concatenate([head_row, jnp.zeros((1, wide - 128), F32)], axis=1)
            x = x_ref[...].astype(F32)
            r_ref[...] = jnp.broadcast_to(
                lax.rsqrt(jnp.mean(x * x, axis=1, keepdims=True) + EPSILON), (rows, 128)
            )
            for k in range(n_block):
                cols = pl.ds(offset(ids_ref, k), wide)
                g_refs[k][:wide, :] = tn_dot(n_ref[:, cols], low_ref[...]).astype(BF)
                dn = nt_dot(low_ref[...], w_refs[k][:wide, :])
                low_dn = dn.astype(BF)
                for c in range(n_heads):
                    part = low_dn[c * half : (c + 1) * half]

                    @pl.when(c == ids_ref[1])
                    def _():
                        keep_ref[:, cols] = part

                    @pl.when(c != ids_ref[1])
                    def _():
                        send_ref[:, cols] = part

                w = x_ref[:, cols].astype(F32) * r_ref[:, 0:1]
                three = [jnp.sum(dn * w, axis=0, keepdims=True), gp_ref[0:1, cols], head_row]
                if blocks_mode:
                    high = [v.astype(BF).astype(F32) for v in three]
                    rest = [a - b for a, b in zip(three, high)]
                    packed_rows = high + rest + [jnp.zeros((GAIN_ROWS - 6, wide), F32)]
                    g_refs[k][wide : wide + GAIN_ROWS, :] = jnp.concatenate(packed_rows, axis=0).astype(BF)
                    g_refs[k][wide + GAIN_ROWS :, :] = gwo_refs[k][...]
                else:
                    refs[3][...] = jnp.concatenate(three + [jnp.zeros((5, wide), F32)], axis=0)

        if blocks_mode:
            grad_shapes = [((wide + GAIN_ROWS + q_cols, 256), BF)] * n_block
        else:
            grad_shapes = [((wide, 256), BF), ((8, width), F32)]
        results = call(
            project_back,
            [((half, width), BF), ((half, width), BF)] + grad_shapes,
            ids,
            [block_input, normed_one, raw, d_query, cosine, sine, head_gains, ffn_gain_part]
            + [*d_kv_parts, *attn_parts]
            + (list(grad_out) if blocks_mode else []),
            scratch=[pltpu.VMEM((rows, 256), BF), pltpu.VMEM((rows, 128), F32)],
            flops=2 * rows * width * 512,
            vmem=6,
            name="project_back",
        )
        d1_send, d1_keep, grads = results[0], results[1], results[2:]
        d1_parts = plane_sum_parts(plane_halves(d1_keep, d1_send))
        def norm_one_back(ids_ref, x_ref, dm_ref, ga_ref, *refs):
            part_refs, ig_ref = refs[:n_tensor], refs[n_tensor]
            d = tree([p[...] for p in part_refs])
            v = x_ref[my_rows(ids_ref), :].astype(F32)
            r = lax.rsqrt(jnp.mean(v * v, axis=1, keepdims=True) + EPSILON)
            w = v * r
            wd = d * ga_ref[0:1, :]
            back = r * (wd - w * jnp.mean(wd * w, axis=1, keepdims=True))
            ig_ref[...] = (dm_ref[...] + back).astype(BF)

        (input_block,) = call(
            norm_one_back,
            [((sub, width), BF)],
            ids,
            [block_input, d_middle, ga, *d1_parts],
            vmem=3,
            name="norm_one_back",
        )
        input_parts = plane_blocks(input_block)
        if blocks_mode:
            (second_route,) = after((second_route,), input_block)
            ffn_sum = tree([ffn_own, first_route, second_route], BF)

        (input_grad,) = call(
            stack_rows, [((rows, width), F32)], ids, input_parts, vmem=2, name="stack_input"
        )

        def place_ffn(ids_ref, own_ref, other_ref, gate_ref, up_ref, down_ref):
            for c in range(n_heads):

                @pl.when(ids_ref[1] == c)
                def _():
                    low_ref, high_ref = (own_ref, other_ref) if c == 0 else (other_ref, own_ref)
                    before = lanes((depth, whole)) < hid
                    blank = jnp.zeros((depth, whole - padded), F32)
                    for i, ref in enumerate((gate_ref, up_ref)):
                        at = slice(i * hid, i * hid + padded)
                        low = jnp.concatenate([low_ref[at, :].astype(F32).T, blank], axis=1)
                        high = jnp.concatenate([high_ref[at, :].astype(F32).T, blank], axis=1)
                        ref[...] = jnp.where(before, low, pltpu.roll(high, hid, 1))
                    down_ref[:hid, :] = low_ref[whole:, :].astype(F32)
                    down_ref[hid:, :] = high_ref[whole:, :].astype(F32)

        gate_grad, up_grad, down_grad = call(
            place_ffn,
            [((depth, hidden_all), F32), ((depth, hidden_all), F32), ((hidden_all, depth), F32)],
            ids,
            [ffn_sum, swap(ffn_sum, "heads", 1)],
            vmem=12,
            name="place_ffn",
        )
        def place(ids_ref, *refs):
            b_refs, (q_ref, k_ref, v_ref, o_ref, s_ref) = refs[:n_tensor], refs[n_tensor:]
            for k in range(n_tensor):
                s_ref[ids_ref[2] ^ k] = b_refs[k][...].astype(F32)
            low = lanes((depth, 128)) < 64
            for i in range(n_tensor):
                q_ref[:, i * 128 : (i + 1) * 128] = s_ref[i, :depth, :128]
                o_ref[i * q_cols : (i + 1) * q_cols, :] = s_ref[i, depth + GAIN_ROWS :, :]
            for i in range(n_tensor // 2):
                even, odd = s_ref[2 * i, :depth, 128:], s_ref[2 * i + 1, :depth, 128:]
                k_ref[:, i * 128 : (i + 1) * 128] = jnp.where(low, even, pltpu.roll(odd, 64, 1))
                v_ref[:, i * 128 : (i + 1) * 128] = jnp.where(low, pltpu.roll(even, 64, 1), odd)

        if blocks_mode:
            grads = after(grads, d1_parts[0])
            bundle = after((shard_sum(grads),), block_output)[0]
            bundles = [bundle] + [swap(bundle, "tensor", k) for k in range(1, n_tensor)]
            bundles = [after((bundle,), input_grad, gate_grad)[0]] + bundles[1:]
            total = tree([b[depth : depth + GAIN_ROWS] for b in bundles])
            total = total + swap(total, "heads", 1)
            total = total[0:3] + total[3:6]
            attn_gain_grad, ffn_gain_grad, head_gain_grad = total[0], total[1], total[2]
            query_grad, key_grad, value_grad, out_weight_grad = call(
                place,
                [
                    ((depth, n_tensor * q_cols), F32),
                    ((depth, n_tensor * k_cols), F32),
                    ((depth, n_tensor * k_cols), F32),
                    ((n_tensor * q_cols, depth), F32),
                ],
                ids,
                bundles,
                scratch=[pltpu.VMEM((n_tensor,) + bundle.shape, F32)],
                vmem=4,
                name="place",
            )
        else:
            own_sum = lax.psum_scatter(grads[0], "shard", scatter_dimension=0, tiled=True)
            total = lax.psum(grads[1], ("shard", "heads", "tensor"))
            attn_gain_grad = lax.dynamic_slice_in_dim(total[0], z * depth, depth)
            ffn_gain_grad = lax.dynamic_slice_in_dim(total[1], z * depth, depth)
            head_gain_grad = total[2]
            found = lax.all_gather(own_sum, "tensor", axis=0).astype(F32)
            flat = lambda x: jnp.swapaxes(x, 0, 1).reshape(depth, -1)
            query_grad = flat(found[:, :, :128])
            key_grad, value_grad = flat(found[:, :, 128:192]), flat(found[:, :, 192:])
            out_sum = lax.psum_scatter(grad_out[0], "shard", scatter_dimension=1, tiled=True)
            out_weight_grad = lax.all_gather(out_sum, "tensor", axis=0, tiled=True).astype(F32)

        return (
            block_output,
            input_grad,
            attn_gain_grad,
            query_grad,
            key_grad,
            value_grad,
            head_gain_grad[:head],
            head_gain_grad[head : 2 * head],
            out_weight_grad,
            ffn_gain_grad,
            gate_grad,
            up_grad,
            down_grad,
        )

    return on_device


def solution(mesh):
    placed = (
        P("shard", None),
        P("shard"),
        P("shard", "heads"),
        P("shard", "heads"),
        P("shard", "heads"),
        P(),
        P(),
        P("heads", "shard"),
        P("shard"),
        P("shard", "tensor"),
        P("shard", "tensor"),
        P("tensor", "shard"),
        P(),
        P(),
        P("shard", None),
    )
    return jax.shard_map(
        make(mesh),
        mesh=mesh,
        in_specs=placed,
        out_specs=(
            P("shard", None),
            P("shard", None),
            P("shard"),
            P("shard", "heads"),
            P("shard", "heads"),
            P("shard", "heads"),
            P(),
            P(),
            P("heads", "shard"),
            P("shard"),
            P("shard", "tensor"),
            P("shard", "tensor"),
            P("tensor", "shard"),
        ),
        check_vma=False,
    )
```

time: 314 us -> 241 us (0.77)
  local copies, waits for them, and re-layouts: 36.8 us -> 8.27 us
  between operations: 15.8 us -> 0.99 us
  waiting for transfers between devices: 117 us -> 105 us
  starting transfers between devices: 90.9 us -> 79.1 us
  other arithmetic: 12.3 us -> 1.13 us
  Pallas kernels: 40.3 us -> 46.4 us
    ppermute x63 -> x55, waiting for transfers between devices: 107 us -> 51.4 us  [swap(): return lax.ppermute(x, axis, [(i, i ^ k) for i in range(size)])]
    ppermute x0 -> x12, waiting for transfers between devices: none -> 53.6 us  [route(): lax.ppermute(x, 'shard', [(b, a) for a, b in pairs] if back else pairs)]
    ppermute x63 -> x55, starting transfers between devices: 90.6 us -> 65.4 us  [swap(): return lax.ppermute(x, axis, [(i, i ^ k) for i in range(size)])]
    unnamed x118 -> x30, local copies, waits for them, and re-layouts: 26.5 us -> 5.54 us
    ppermute x0 -> x12, starting transfers between devices: none -> 13.6 us  [route(): lax.ppermute(x, 'shard', [(b, a) for a, b in pairs] if back else pairs)]
    reduce_scatter x3 -> x0, waiting for transfers between devices: 8.48 us -> none  [the longest x1 8.45 us: on_device(): lax.psum_scatter(grad_gate_up, 'shard', scatter_dimension=0, tiled=True)]
    convert_element_type x7 -> x3, other arithmetic: 7.29 us -> 1.02 us  [the longest x1 0.53 us: shard_sum_staged(): b = (blocks[2].astype(F32) + jnp.where(inner(), found, 0.0)).astype(BF)]
    pallas_call x14 -> x23, Pallas kernels: 40.3 us -> 46.4 us  [call(): pl.pallas_call(kernel, out_shape=shapes, in_specs=[pl.BlockSpec(memory_sp...]
  transfers between devices with their start and end apart: 67 -> 67, of which waited for: 28 -> 32; matrix products, arithmetic and copies ran while one was open for 6% -> 1% of each run, Pallas kernels for 7% -> 13%
where the time goes in v2:
time: 241 us
  waiting for transfers between devices  105 us (44%)
  starting transfers between devices  79.1 us (33%)
  Pallas kernels  46.4 us (19%)
  local copies, waits for them, and re-layouts  8.27 us (3%)
    ppermute x55, starting transfers between devices, swap(): return lax.ppermute(x, axis, [(i, i ^ k) for i in range(size)])  65.4 us
    ppermute x12, waiting for transfers between devices, route(): lax.ppermute(x, 'shard', [(b, a) for a, b in pairs] if back else pairs)  53.6 us
    ppermute x55, waiting for transfers between devices, swap(): return lax.ppermute(x, axis, [(i, i ^ k) for i in range(size)])  51.4 us
    pallas_call x23, Pallas kernels, call(): pl.pallas_call(kernel, out_shape=shapes, in_specs=[pl.BlockSpec(memory_sp...  46.4 us
    ppermute x12, starting transfers between devices, route(): lax.ppermute(x, 'shard', [(b, a) for a, b in pairs] if back else pairs)  13.6 us
    unnamed x30, local copies, waits for them, and re-layouts  5.54 us
  transfers between devices with their start and end apart: 67, of which 32 were waited for; matrix products, arithmetic and copies ran while one was open for 1% of the time, Pallas kernels for 13%

profile of v2, /device:TPU:1, one launch (start us, length us, event | category | flops | bytes accessed | tf_op | source)
XLA Modules:
  0.0 240.8 jit_solution(14381926009218864952)
XLA Ops:
  1.3 2.5 %share_attn.1.refs_0_.refs_4_ = bf16[400,256]{1,0:T(8,128)(2,1)} custom-call(s32[7]{0:T(128)} %stack.28.ids_ref, bf16[256,512]{1,0:T(8,128)(2,1)} %q_hbm.1, bf16[256,256]{1,0:T(8,128)(2,1)} %k_hbm.1, bf16[256,256]{1,0:T(8,128)(2,1)} %v_hbm.1, bf16[512,256]{1,0:T(8,128)(2,1)} %o_hbm.1, bf16[256]{0:T(256)(128)(2,1)} %ag_hbm.1, bf16[256]{0:T(256)(128)(2,1)} %fg_hbm.1), custom_call_target="tpu_custom_call" | custom-call | bytes 992256 | tf_op jit(solution)/shard_map/share_attn/pallas_call | solution.py:37
  3.8 4.2 %collective-permute-start.2 = (bf16[400,256]{1,0:T(8,128)(2,1)}, bf16[400,256]{1,0:T(8,128)(2,1)S(1)}, u32[]{:S(2)}, u32[]{:S(2)}) collective-permute-start(bf16[400,256]{1,0:T(8,128)(2,1)} %share_attn.1.refs_0_.refs_4_), channel_id=1, source_target_pairs={{0,24},{8,16},{16,8},{24,0},{1,25},{9,17},{17,9},{25,1},{2,26},{10... | collective-permute-start | bytes 614408 | tf_op jit(solution)/shard_map/ppermute | solution.py:84
  8.0 1.5 collective-permute-start
  13.4 1.7 layout.1
  16.0 2.2 collective-permute-done.1.refs_2_.refs_6_
  18.2 7.0 %collective-permute-done.refs_1_.refs_5_ = bf16[400,256]{1,0:T(8,128)(2,1)S(1)} collective-permute-done((bf16[400,256]{1,0:T(8,128)(2,1)}, bf16[400,256]{1,0:T(8,128)(2,1)S(1)}, u32[]{:S(2)}, u32[]{:S(2)}) %collective-permute-start) | collective-permute-done | bytes 204832 | tf_op jit(solution)/shard_map/ppermute | solution.py:87
  26.8 3.0 %project.1 = (bf16[512,1024]{1,0:T(8,128)(2,1)S(1)}, f32[512,256]{1,0:T(8,128)S(1)}, bf16[1024,128]{1,0:T(8,128)(2,1)S(1)}, bf16[512,128]{1,0:T(8,128)(2,1)S(1)}...) custom-call(s32[7]{0:T(128)S(1)} %copy-done.7, bf16[512,1024]{1,0:T(8,128)(2,1)S(1)} %copy-done, ...), custom_call_target="tpu_custom_call" | custom-call | flops 268435456 | bytes 4431872 | tf_op jit(solution)/shard_map/project/pallas_call | solution.py:37
  29.8 2.1 collective-permute-start.5
  31.9 1.5 collective-permute-start.3
  33.4 1.4 share_ffn.1.refs_0_
  35.7 3.9 %collective-permute-done.4.refs_2_.refs_10_ = bf16[512,128]{1,0:T(8,128)(2,1)S(1)} collective-permute-done((bf16[512,128]{1,0:T(8,128)(2,1)S(1)}, bf16[512,128]{1,0:T(8,128)(2,1)S(1)}, u32[]{:S(2)}, u32[]{:S(2)}) %collective-permute-start.4) | collective-permute-done | bytes 131104 | tf_op jit(solution)/shard_map/ppermute | solution.py:87
  39.6 3.4 %collective-permute-done.3.refs_1_.refs_9_ = bf16[512,128]{1,0:T(8,128)(2,1)S(1)} collective-permute-done((bf16[512,128]{1,0:T(8,128)(2,1)S(1)}, bf16[512,128]{1,0:T(8,128)(2,1)S(1)}, u32[]{:S(2)}, u32[]{:S(2)}) %collective-permute-start.3) | collective-permute-done | bytes 131104 | tf_op jit(solution)/shard_map/ppermute | solution.py:87
  43.0 1.5 collective-permute-start.17
  45.0 2.2 collective-permute-start.8
  47.8 2.8 %attend.1 = (bf16[512,128]{1,0:T(8,128)(2,1)S(1)}, f32[1024,128]{1,0:T(8,128)S(1)}) custom-call(s32[7]{0:T(128)S(1)} %copy-done.8, f32[512,128]{1,0:T(8,128)S(1)} %get-tuple-element.101.info_ref, bf16[1024,128]{1,0:T(8,128)(2,1)S(1)} %get-tuple-element.110.qs_ref, bf16[512,128]{1,0:T(8,128)(2,1)S(1)} %get-tuple-element.105.refs_0_.refs_8_, ...), custom_call_target="tpu_custom_call" | custom-call | flops 1073741824 | bytes 1703936 | tf_op jit(solution)/shard_map/attend/pallas_call | solution.py:37
  50.6 1.9 collective-permute-done.8.refs_3_
  52.4 2.2 collective-permute-start.12
  54.6 6.6 %collective-permute-done.7.refs_2_ = bf16[128,1024]{1,0:T(8,128)(2,1)S(1)} collective-permute-done((bf16[128,1024]{1,0:T(8,128)(2,1)S(1)}, bf16[128,1024]{1,0:T(8,128)(2,1)S(1)}, u32[]{:S(2)}, u32[]{:S(2)}) %collective-permute-start.7) | collective-permute-done | bytes 262176 | tf_op jit(solution)/shard_map/ppermute | solution.py:84
  61.3 1.2 collective-permute-start.11
  63.4 2.6 %collective-permute-start.9 = (bf16[512,1024]{1,0:T(8,128)(2,1)S(1)}, bf16[512,1024]{1,0:T(8,128)(2,1)S(1)}, u32[]{:S(2)}, u32[]{:S(2)}) collective-permute-start(bf16[512,1024]{1,0:T(8,128)(2,1)S(1)} %below.1.refs_0_), channel_id=1, source_target_pairs={{0,4},{4,0},{1,5},{5,1},{2,6},{6,2},{3,7},{7,3},{8,12},{12,8},{9,1... | collective-permute-start | bytes 3145736 | tf_op jit(solution)/shard_map/ppermute | solution.py:84
  66.0 17.9 %collective-permute-done.17.refs_1_ = bf16[1728,256]{1,0:T(8,128)(2,1)S(1)} collective-permute-done((bf16[1728,256]{1,0:T(8,128)(2,1)S(1)}, bf16[1728,256]{1,0:T(8,128)(2,1)S(1)}, u32[]{:S(2)}, u32[]{:S(2)}) %collective-permute-start.17) | collective-permute-done | bytes 884768 | tf_op jit(solution)/shard_map/ppermute | solution.py:87
  87.0 2.5 %middle.1 = (bf16[512,1024]{1,0:T(8,128)(2,1)S(1)}, f32[64,1024]{1,0:T(8,128)S(1)}) custom-call(s32[7]{0:T(128)S(1)} %copy-done.8, bf16[512,1024]{1,0:T(8,128)(2,1)S(1)} %copy-done, f32[8,1024]{1,0:T(8,128)S(1)} %get-tuple-element.104.gf_ref, bf16[512,1024]{1,0:T(8,128)(2,1)S(1)} %below.1.refs_0_, bf16[512,1024]{1,0:T(8,128)(2,1)S(1)} %collective-permute-done.9.refs_1_, ...), custom_call_target="tpu_custom_call" | custom-call | flops 1073741824 | bytes 5537792 | tf_op jit(solution)/shard_map/middle/pallas_call | solution.py:37
  89.5 15.3 %collective-permute-done.19.refs_3_ = bf16[1728,256]{1,0:T(8,128)(2,1)S(1)} collective-permute-done((bf16[1728,256]{1,0:T(8,128)(2,1)S(1)}, bf16[1728,256]{1,0:T(8,128)(2,1)S(1)}, u32[]{:S(2)}, u32[]{:S(2)}) %collective-permute-start.19) | collective-permute-done | bytes 884768 | tf_op jit(solution)/shard_map/ppermute | solution.py:84
  104.8 7.0 %feed_forward.1 = (bf16[256,1024]{1,0:T(8,128)(2,1)S(1)}, bf16[256,1024]{1,0:T(8,128)(2,1)S(1)}, bf16[256,1024]{1,0:T(8,128)(2,1)S(1)}, bf16[256,1024]{1,0:T(8,1...) custom-call(s32[7]{0:T(128)S(1)} %copy-done.8, ...), custom_call_target="tpu_custom_call" | custom-call | flops 3623878656 | bytes 10813440 | tf_op jit(solution)/shard_map/feed_forward/pallas_call | solution.py:37
  111.8 2.6 %ffn_grads.1 = (bf16[1728,256]{1,0:T(8,128)(2,1)S(1)}, bf16[1728,256]{1,0:T(8,128)(2,1)S(1)}, bf16[1728,256]{1,0:T(8,128)(2,1)S(1)}, bf16[1728,256]{1,0:T(8,128)(2,1)S(1)}) custom-call(s32[7]{0:T(128)S(1)} %copy-done.8, bf16[512,1024]{1,0:T(8,128)(2,1)S(1)} %get-tuple-element.113.n2_ref, bf16[512,1024]{1,0:T(8,128)(2,1)S(1)} %get-tuple-element.118.cot_ref, ...), custom_call_target="tpu_custom_call" | custom-call | flops 1811939328 | bytes 7405568 | tf_op jit(solution)/shard_map/ffn_grads/pallas_call | solution.py:37
  114.9 1.3 collective-permute-start.20
  116.2 1.5 collective-permute-done.20.got_ref
  118.4 1.3 collective-permute-start.21
  119.7 1.2 collective-permute-start.22
  121.1 2.1 collective-permute-done.21.refs_1_
  124.0 2.7 %collective-permute-done.23.refs_3_ = bf16[64,1024]{1,0:T(8,128)(2,1)S(1)} collective-permute-done((bf16[64,1024]{1,0:T(8,128)(2,1)S(1)}, bf16[64,1024]{1,0:T(8,128)(2,1)S(1)}, u32[]{:S(2)}, u32[]{:S(2)}) %collective-permute-start.23) | collective-permute-done | bytes 131104 | tf_op jit(solution)/shard_map/ppermute | solution.py:84
  127.5 6.8 %collective-permute-done.42 = bf16[1728,256]{1,0:T(8,128)(2,1)S(1)} collective-permute-done((bf16[1728,256]{1,0:T(8,128)(2,1)S(1)}, bf16[1728,256]{1,0:T(8,128)(2,1)S(1)}, u32[]{:S(2)}, u32[]{:S(2)}) %collective-permute-start.42) | collective-permute-done | bytes 884768 | tf_op jit(solution)/shard_map/ppermute | solution.py:84
  135.1 2.2 collective-permute-start.27
  137.8 3.4 %collective-permute-start.28 = (bf16[64,1024]{1,0:T(8,128)(2,1)S(1)}, bf16[64,1024]{1,0:T(8,128)(2,1)S(1)}, u32[]{:S(2)}, u32[]{:S(2)}) collective-permute-start(bf16[64,1024]{1,0:T(8,128)(2,1)S(1)} %get-tuple-element.130.refs_0_), channel_id=1, source_target_pairs={{0,4},{4,0},{1,5},{5,1},{2,6},{6,2},{3,7},{7,3},{8,12},{12,8},{9,1... | collective-permute-start | bytes 393224 | tf_op jit(solution)/shard_map/ppermute | solution.py:84
  141.2 3.3 %collective-permute-start.31 = (bf16[64,1024]{1,0:T(8,128)(2,1)S(1)}, bf16[64,1024]{1,0:T(8,128)(2,1)S(1)}, u32[]{:S(2)}, u32[]{:S(2)}) collective-permute-start(bf16[64,1024]{1,0:T(8,128)(2,1)S(1)} %collective-permute-done.27.refs_3_), channel_id=1, source_target_pairs={{0,4},{4,0},{1,5},{5,1},{2,6},{6,2},{3,7},{7,3},{8,12},{12,8},{9,1... | collective-permute-start | bytes 393224 | tf_op jit(solution)/shard_map/ppermute | solution.py:84
  144.5 1.2 collective-permute-start.30
  147.0 4.6 %attend_back.1 = (f32[512,128]{1,0:T(8,128)S(1)}, bf16[512,1024]{1,0:T(8,128)(2,1)S(1)}, bf16[512,128]{1,0:T(8,128)(2,1)S(1)}, bf16[512,128]{1,0:T(8,128)(2,1)S(...) custom-call(s32[7]{0:T(128)S(1)} %copy-done.8, f32[512,128]{1,0:T(8,128)S(1)} %get-tuple-element.101.info_ref, ...), custom_call_target="tpu_custom_call" | custom-call | flops 2684354560 | bytes 4718592 | tf_op jit(solution)/shard_map/attend_back/pallas_call | solution.py:37
  151.6 2.2 collective-permute-done.43
  153.8 5.3 %collective-permute-start.44 = (bf16[512,128]{1,0:T(8,128)(2,1)S(1)}, bf16[512,128]{1,0:T(8,128)(2,1)S(1)}, u32[]{:S(2)}, u32[]{:S(2)}) collective-permute-start(bf16[512,128]{1,0:T(8,128)(2,1)S(1)} %get-tuple-element.155), channel_id=1, source_target_pairs={{8,0},{24,8},{0,16},{16,24},{9,1},{25,9},{1,17},{17,25},{10,2},{26... | collective-permute-start | bytes 393224 | tf_op jit(solution)/shard_map/ppermute | solution.py:87
  159.1 5.1 %collective-permute-start.46 = (bf16[512,128]{1,0:T(8,128)(2,1)S(1)}, bf16[512,128]{1,0:T(8,128)(2,1)S(1)}, u32[]{:S(2)}, u32[]{:S(2)}) collective-permute-start(bf16[512,128]{1,0:T(8,128)(2,1)S(1)} %get-tuple-element.157), channel_id=1, source_target_pairs={{0,24},{8,16},{16,8},{24,0},{1,25},{9,17},{17,9},{25,1},{2,26},{10... | collective-permute-start | bytes 393224 | tf_op jit(solution)/shard_map/ppermute | solution.py:84
  164.2 5.5 %collective-permute-done.45.refs_2_ = bf16[512,128]{1,0:T(8,128)(2,1)S(1)} collective-permute-done((bf16[512,128]{1,0:T(8,128)(2,1)S(1)}, bf16[512,128]{1,0:T(8,128)(2,1)S(1)}, u32[]{:S(2)}, u32[]{:S(2)}) %collective-permute-start.45) | collective-permute-done | bytes 131104 | tf_op jit(solution)/shard_map/ppermute | solution.py:87
  169.7 2.5 %collective-permute-done.46.refs_3_ = bf16[512,128]{1,0:T(8,128)(2,1)S(1)} collective-permute-done((bf16[512,128]{1,0:T(8,128)(2,1)S(1)}, bf16[512,128]{1,0:T(8,128)(2,1)S(1)}, u32[]{:S(2)}, u32[]{:S(2)}) %collective-permute-start.46) | collective-permute-done | bytes 131104 | tf_op jit(solution)/shard_map/ppermute | solution.py:84
  172.2 3.2 %collective-permute-start.61 = (bf16[1728,256]{1,0:T(8,128)(2,1)S(1)}, bf16[1728,256]{1,0:T(8,128)(2,1)S(1)}, u32[]{:S(2)}, u32[]{:S(2)}) collective-permute-start(bf16[1728,256]{1,0:T(8,128)(2,1)S(1)} %get-tuple-element.179), channel_id=1, source_target_pairs={{16,0},{0,8},{24,16},{8,24},{17,1},{1,9},{25,17},{9,25},{18,2},{2,... | collective-permute-start | bytes 2654216 | tf_op jit(solution)/shard_map/ppermute | solution.py:87
  177.1 3.4 %project_back.1 = (bf16[256,1024]{1,0:T(8,128)(2,1)S(1)}, bf16[256,1024]{1,0:T(8,128)(2,1)S(1)}, bf16[400,256]{1,0:T(8,128)(2,1)S(1)}, bf16[400,256]{1,0:T(8,128...) custom-call(s32[7]{0:T(128)S(1)} %copy-done.8, bf16[512,1024]{1,0:T(8,128)(2,1)S(1)} %copy-done, ...), custom_call_target="tpu_custom_call" | custom-call | flops 536870912 | bytes 6922240 | tf_op jit(solution)/shard_map/project_back/pallas_call | solution.py:37
  182.6 1.4 collective-permute-start.34
  186.6 1.1 collective-permute-start.50
  187.7 1.4 collective-permute-done.34.refs_3_
  189.8 3.1 %collective-permute-start.38 = (bf16[64,1024]{1,0:T(8,128)(2,1)S(1)}, bf16[64,1024]{1,0:T(8,128)(2,1)S(1)}, u32[]{:S(2)}, u32[]{:S(2)}) collective-permute-start(bf16[64,1024]{1,0:T(8,128)(2,1)S(1)} %finish.1.refs_0_), channel_id=1, source_target_pairs={{0,4},{4,0},{1,5},{5,1},{2,6},{6,2},{3,7},{7,3},{8,12},{12,8},{9,1... | collective-permute-start | bytes 393224 | tf_op jit(solution)/shard_map/ppermute | solution.py:84
  195.7 1.8 collective-permute-start.62
  197.5 2.3 collective-permute-start.35
  200.9 1.1 collective-permute-start.40
  202.0 1.5 collective-permute-done.35.refs_1_
  204.7 1.4 collective-permute-start.60
  207.1 11.3 %collective-permute-done.58 = bf16[400,256]{1,0:T(8,128)(2,1)S(1)} collective-permute-done((bf16[400,256]{1,0:T(8,128)(2,1)S(1)}, bf16[400,256]{1,0:T(8,128)(2,1)S(1)}, u32[]{:S(2)}, u32[]{:S(2)}) %collective-permute-start.58) | collective-permute-done | bytes 204832 | tf_op jit(solution)/shard_map/ppermute | solution.py:87
  219.1 1.6 stack_output.1
  220.7 1.4 collective-permute-start.54
  223.5 1.1 collective-permute-start.56
  224.7 1.5 collective-permute-start.65
  226.2 1.0 collective-permute-done.51.refs_1_
  228.0 1.2 collective-permute-start.63
  229.2 1.4 collective-permute-start.55
  231.6 2.0 stack_input.1
  233.6 3.0 %place_ffn.1 = (f32[256,1152]{1,0:T(8,128)}, f32[256,1152]{1,0:T(8,128)}, f32[1152,256]{1,0:T(8,128)}) custom-call(s32[7]{0:T(128)S(1)} %copy-done.8, bf16[1728,256]{1,0:T(8,128)(2,1)S(1)} %add_convert_fusion.own_ref, bf16[1728,256]{1,0:T(8,128)(2,1)S(1)} %collective-permute-done.62.other_ref), custom_call_target="tpu_custom_call" | custom-call | bytes 5308416 | tf_op jit(solution)/shard_map/place_ffn/pallas_call | solution.py:37
  237.6 2.0 place.1
  (134 shorter events, 37.7 us)
Async XLA Ops:
  3.8 12.3 %collective-permute-start.2 = (bf16[400,256]{1,0:T(8,128)(2,1)}, bf16[400,256]{1,0:T(8,128)(2,1)S(1)}, u32[]{:S(2)}, u32[]{:S(2)}) collective-permute-start(bf16[400,256]{1,0:T(8,128)(2,1)} %share_attn.1.refs_0_.refs_4_), channel_id=1, source_target_pairs={{0,24},{8,16},{16,8},{24,0},{1,25},{9,17},{17,9},{25,1},{2,26},{10... | collective-permute-start | bytes 614408 | tf_op jit(solution)/shard_map/ppermute | solution.py:84
  8.0 10.2 %collective-permute-start.1 = (bf16[400,256]{1,0:T(8,128)(2,1)}, bf16[400,256]{1,0:T(8,128)(2,1)S(1)}, u32[]{:S(2)}, u32[]{:S(2)}) collective-permute-start(bf16[400,256]{1,0:T(8,128)(2,1)} %share_attn.1.refs_0_.refs_4_), channel_id=1, source_target_pairs={{0,16},{8,0},{16,24},{24,8},{1,17},{9,1},{17,25},{25,9},{2,18},{10... | collective-permute-start | bytes 614408 | tf_op jit(solution)/shard_map/ppermute | solution.py:87
  8.0 17.2 %collective-permute-start = (bf16[400,256]{1,0:T(8,128)(2,1)}, bf16[400,256]{1,0:T(8,128)(2,1)S(1)}, u32[]{:S(2)}, u32[]{:S(2)}) collective-permute-start(bf16[400,256]{1,0:T(8,128)(2,1)} %share_attn.1.refs_0_.refs_4_), channel_id=1, source_target_pairs={{0,8},{8,24},{16,0},{24,16},{1,9},{9,25},{17,1},{25,17},{2,10},{10... | collective-permute-start | bytes 614408 | tf_op jit(solution)/shard_map/ppermute | solution.py:87
  29.8 5.9 %collective-permute-start.5 = (bf16[512,128]{1,0:T(8,128)(2,1)S(1)}, bf16[512,128]{1,0:T(8,128)(2,1)S(1)}, u32[]{:S(2)}, u32[]{:S(2)}) collective-permute-start(bf16[512,128]{1,0:T(8,128)(2,1)S(1)} %get-tuple-element.105.refs_0_.refs_8_), channel_id=1, source_target_pairs={{0,24},{8,16},{16,8},{24,0},{1,25},{9,17},{17,9},{25,1},{2,26},{10... | collective-permute-start | bytes 393224 | tf_op jit(solution)/shard_map/ppermute | solution.py:84
  31.9 7.7 %collective-permute-start.4 = (bf16[512,128]{1,0:T(8,128)(2,1)S(1)}, bf16[512,128]{1,0:T(8,128)(2,1)S(1)}, u32[]{:S(2)}, u32[]{:S(2)}) collective-permute-start(bf16[512,128]{1,0:T(8,128)(2,1)S(1)} %get-tuple-element.105.refs_0_.refs_8_), channel_id=1, source_target_pairs={{0,16},{8,0},{16,24},{24,8},{1,17},{9,1},{17,25},{25,9},{2,18},{10... | collective-permute-start | bytes 393224 | tf_op jit(solution)/shard_map/ppermute | solution.py:87
  31.9 11.1 %collective-permute-start.3 = (bf16[512,128]{1,0:T(8,128)(2,1)S(1)}, bf16[512,128]{1,0:T(8,128)(2,1)S(1)}, u32[]{:S(2)}, u32[]{:S(2)}) collective-permute-start(bf16[512,128]{1,0:T(8,128)(2,1)S(1)} %get-tuple-element.105.refs_0_.refs_8_), channel_id=1, source_target_pairs={{0,8},{8,24},{16,0},{24,16},{1,9},{9,25},{17,1},{25,17},{2,10},{10... | collective-permute-start | bytes 393224 | tf_op jit(solution)/shard_map/ppermute | solution.py:87
  43.0 20.4 %collective-permute-start.18 = (bf16[1728,256]{1,0:T(8,128)(2,1)S(1)}, bf16[1728,256]{1,0:T(8,128)(2,1)S(1)}, u32[]{:S(2)}, u32[]{:S(2)}) collective-permute-start(bf16[1728,256]{1,0:T(8,128)(2,1)S(1)} %share_ffn.1.refs_0_), channel_id=1, source_target_pairs={{0,16},{8,0},{16,24},{24,8},{1,17},{9,1},{17,25},{25,9},{2,18},{10... | collective-permute-start | bytes 2654216 | tf_op jit(solution)/shard_map/ppermute | solution.py:87
  43.0 40.9 %collective-permute-start.17 = (bf16[1728,256]{1,0:T(8,128)(2,1)S(1)}, bf16[1728,256]{1,0:T(8,128)(2,1)S(1)}, u32[]{:S(2)}, u32[]{:S(2)}) collective-permute-start(bf16[1728,256]{1,0:T(8,128)(2,1)S(1)} %share_ffn.1.refs_0_), channel_id=1, source_target_pairs={{0,8},{8,24},{16,0},{24,16},{1,9},{9,25},{17,1},{25,17},{2,10},{10... | collective-permute-start | bytes 2654216 | tf_op jit(solution)/shard_map/ppermute | solution.py:87
  45.0 7.4 %collective-permute-start.8 = (bf16[128,1024]{1,0:T(8,128)(2,1)S(1)}, bf16[128,1024]{1,0:T(8,128)(2,1)S(1)}, u32[]{:S(2)}, u32[]{:S(2)}) collective-permute-start(bf16[128,1024]{1,0:T(8,128)(2,1)S(1)} %beside.1.refs_0_.wo_ref), channel_id=1, source_target_pairs={{0,3},{1,2},{2,1},{3,0},{4,7},{5,6},{6,5},{7,4},{8,11},{9,10},{10,... | collective-permute-start | bytes 786440 | tf_op jit(solution)/shard_map/ppermute | solution.py:84
  47.3 14.0 %collective-permute-start.7 = (bf16[128,1024]{1,0:T(8,128)(2,1)S(1)}, bf16[128,1024]{1,0:T(8,128)(2,1)S(1)}, u32[]{:S(2)}, u32[]{:S(2)}) collective-permute-start(bf16[128,1024]{1,0:T(8,128)(2,1)S(1)} %beside.1.refs_0_.wo_ref), channel_id=1, source_target_pairs={{0,2},{1,3},{2,0},{3,1},{4,6},{5,7},{6,4},{7,5},{8,10},{9,11},{10,... | collective-permute-start | bytes 786440 | tf_op jit(solution)/shard_map/ppermute | solution.py:84
  47.5 15.0 %collective-permute-start.6 = (bf16[128,1024]{1,0:T(8,128)(2,1)S(1)}, bf16[128,1024]{1,0:T(8,128)(2,1)S(1)}, u32[]{:S(2)}, u32[]{:S(2)}) collective-permute-start(bf16[128,1024]{1,0:T(8,128)(2,1)S(1)} %beside.1.refs_0_.wo_ref), channel_id=1, source_target_pairs={{0,1},{1,0},{2,3},{3,2},{4,5},{5,4},{6,7},{7,6},{8,9},{9,8},{10,11... | collective-permute-start | bytes 786440 | tf_op jit(solution)/shard_map/ppermute | solution.py:84
  52.4 31.6 %collective-permute-start.12 = (bf16[512,128]{1,0:T(8,128)(2,1)S(1)}, bf16[512,128]{1,0:T(8,128)(2,1)S(1)}, u32[]{:S(2)}, u32[]{:S(2)}) collective-permute-start(bf16[512,128]{1,0:T(8,128)(2,1)S(1)} %get-tuple-element.111.refs_2_.att_ref), channel_id=1, source_target_pairs={{0,3},{1,2},{2,1},{3,0},{4,7},{5,6},{6,5},{7,4},{8,11},{9,10},{10,... | collective-permute-start | bytes 393224 | tf_op jit(solution)/shard_map/ppermute | solution.py:84
  61.3 22.7 %collective-permute-start.11 = (bf16[512,128]{1,0:T(8,128)(2,1)S(1)}, bf16[512,128]{1,0:T(8,128)(2,1)S(1)}, u32[]{:S(2)}, u32[]{:S(2)}) collective-permute-start(bf16[512,128]{1,0:T(8,128)(2,1)S(1)} %get-tuple-element.111.refs_2_.att_ref), channel_id=1, source_target_pairs={{0,2},{1,3},{2,0},{3,1},{4,6},{5,7},{6,4},{7,5},{8,10},{9,11},{10,... | collective-permute-start | bytes 393224 | tf_op jit(solution)/shard_map/ppermute | solution.py:84
  62.5 21.5 %collective-permute-start.10 = (bf16[512,128]{1,0:T(8,128)(2,1)S(1)}, bf16[512,128]{1,0:T(8,128)(2,1)S(1)}, u32[]{:S(2)}, u32[]{:S(2)}) collective-permute-start(bf16[512,128]{1,0:T(8,128)(2,1)S(1)} %get-tuple-element.111.refs_2_.att_ref), channel_id=1, source_target_pairs={{0,1},{1,0},{2,3},{3,2},{4,5},{5,4},{6,7},{7,6},{8,9},{9,8},{10,11... | collective-permute-start | bytes 393224 | tf_op jit(solution)/shard_map/ppermute | solution.py:84
  63.4 23.6 %collective-permute-start.9 = (bf16[512,1024]{1,0:T(8,128)(2,1)S(1)}, bf16[512,1024]{1,0:T(8,128)(2,1)S(1)}, u32[]{:S(2)}, u32[]{:S(2)}) collective-permute-start(bf16[512,1024]{1,0:T(8,128)(2,1)S(1)} %below.1.refs_0_), channel_id=1, source_target_pairs={{0,4},{4,0},{1,5},{5,1},{2,6},{6,2},{3,7},{7,3},{8,12},{12,8},{9,1... | collective-permute-start | bytes 3145736 | tf_op jit(solution)/shard_map/ppermute | solution.py:84
  84.0 20.8 %collective-permute-start.19 = (bf16[1728,256]{1,0:T(8,128)(2,1)S(1)}, bf16[1728,256]{1,0:T(8,128)(2,1)S(1)}, u32[]{:S(2)}, u32[]{:S(2)}) collective-permute-start(bf16[1728,256]{1,0:T(8,128)(2,1)S(1)} %broadcast_select_fusion), channel_id=1, source_target_pairs={{0,8},{8,0},{16,24},{24,16},{1,9},{9,1},{17,25},{25,17},{2,10},{10... | collective-permute-start | bytes 2654216 | tf_op jit(solution)/shard_map/ppermute | solution.py:84
  84.1 1.5 collective-permute-start.13
  84.7 1.5 collective-permute-start.15
  114.5 19.9 %collective-permute-start.42 = (bf16[1728,256]{1,0:T(8,128)(2,1)S(1)}, bf16[1728,256]{1,0:T(8,128)(2,1)S(1)}, u32[]{:S(2)}, u32[]{:S(2)}) collective-permute-start(bf16[1728,256]{1,0:T(8,128)(2,1)S(1)} %get-tuple-element.152), channel_id=1, source_target_pairs={{0,8},{8,0},{16,24},{24,16},{1,9},{9,1},{17,25},{25,17},{2,10},{10... | collective-permute-start | bytes 2654216 | tf_op jit(solution)/shard_map/ppermute | solution.py:84
  114.9 2.8 %collective-permute-start.20 = (bf16[256,1024]{1,0:T(8,128)(2,1)S(1)}, bf16[256,1024]{1,0:T(8,128)(2,1)S(1)}, u32[]{:S(2)}, u32[]{:S(2)}) collective-permute-start(bf16[256,1024]{1,0:T(8,128)(2,1)S(1)} %get-tuple-element.120), channel_id=1, source_target_pairs={{0,4},{4,0},{1,5},{5,1},{2,6},{6,2},{3,7},{7,3},{8,12},{12,8},{9,1... | collective-permute-start | bytes 1572872 | tf_op jit(solution)/shard_map/ppermute | solution.py:84
  118.4 4.8 %collective-permute-start.21 = (bf16[64,1024]{1,0:T(8,128)(2,1)S(1)}, bf16[64,1024]{1,0:T(8,128)(2,1)S(1)}, u32[]{:S(2)}, u32[]{:S(2)}) collective-permute-start(bf16[64,1024]{1,0:T(8,128)(2,1)S(1)} %get-tuple-element.127), channel_id=1, source_target_pairs={{0,1},{1,0},{2,3},{3,2},{4,5},{5,4},{6,7},{7,6},{8,9},{9,8},{10,11... | collective-permute-start | bytes 393224 | tf_op jit(solution)/shard_map/ppermute | solution.py:84
  119.7 4.4 %collective-permute-start.22 = (bf16[64,1024]{1,0:T(8,128)(2,1)S(1)}, bf16[64,1024]{1,0:T(8,128)(2,1)S(1)}, u32[]{:S(2)}, u32[]{:S(2)}) collective-permute-start(bf16[64,1024]{1,0:T(8,128)(2,1)S(1)} %get-tuple-element.128), channel_id=1, source_target_pairs={{0,2},{1,3},{2,0},{3,1},{4,6},{5,7},{6,4},{7,5},{8,10},{9,11},{10,... | collective-permute-start | bytes 393224 | tf_op jit(solution)/shard_map/ppermute | solution.py:84
  120.9 5.8 %collective-permute-start.23 = (bf16[64,1024]{1,0:T(8,128)(2,1)S(1)}, bf16[64,1024]{1,0:T(8,128)(2,1)S(1)}, u32[]{:S(2)}, u32[]{:S(2)}) collective-permute-start(bf16[64,1024]{1,0:T(8,128)(2,1)S(1)} %get-tuple-element.129), channel_id=1, source_target_pairs={{0,3},{1,2},{2,1},{3,0},{4,7},{5,6},{6,5},{7,4},{8,11},{9,10},{10,... | collective-permute-start | bytes 393224 | tf_op jit(solution)/shard_map/ppermute | solution.py:84
  134.9 18.9 %collective-permute-start.43 = (bf16[1728,256]{1,0:T(8,128)(2,1)S(1)}, bf16[1728,256]{1,0:T(8,128)(2,1)S(1)}, u32[]{:S(2)}, u32[]{:S(2)}) collective-permute-start(bf16[1728,256]{1,0:T(8,128)(2,1)S(1)} %get-tuple-element.190), channel_id=1, source_target_pairs={{8,0},{24,8},{0,16},{16,24},{9,1},{25,9},{1,17},{17,25},{10,2},{26... | collective-permute-start | bytes 2654216 | tf_op jit(solution)/shard_map/ppermute | solution.py:87
  135.1 6.1 %collective-permute-start.27 = (bf16[64,1024]{1,0:T(8,128)(2,1)S(1)}, bf16[64,1024]{1,0:T(8,128)(2,1)S(1)}, u32[]{:S(2)}, u32[]{:S(2)}) collective-permute-start(bf16[64,1024]{1,0:T(8,128)(2,1)S(1)} %get-tuple-element.130.refs_0_), channel_id=1, source_target_pairs={{0,3},{1,2},{2,1},{3,0},{4,7},{5,6},{6,5},{7,4},{8,11},{9,10},{10,... | collective-permute-start | bytes 393224 | tf_op jit(solution)/shard_map/ppermute | solution.py:84
  137.3 7.2 %collective-permute-start.26 = (bf16[64,1024]{1,0:T(8,128)(2,1)S(1)}, bf16[64,1024]{1,0:T(8,128)(2,1)S(1)}, u32[]{:S(2)}, u32[]{:S(2)}) collective-permute-start(bf16[64,1024]{1,0:T(8,128)(2,1)S(1)} %get-tuple-element.130.refs_0_), channel_id=1, source_target_pairs={{0,2},{1,3},{2,0},{3,1},{4,6},{5,7},{6,4},{7,5},{8,10},{9,11},{10,... | collective-permute-start | bytes 393224 | tf_op jit(solution)/shard_map/ppermute | solution.py:84
  137.5 8.2 %collective-permute-start.25 = (bf16[64,1024]{1,0:T(8,128)(2,1)S(1)}, bf16[64,1024]{1,0:T(8,128)(2,1)S(1)}, u32[]{:S(2)}, u32[]{:S(2)}) collective-permute-start(bf16[64,1024]{1,0:T(8,128)(2,1)S(1)} %get-tuple-element.130.refs_0_), channel_id=1, source_target_pairs={{0,1},{1,0},{2,3},{3,2},{4,5},{5,4},{6,7},{7,6},{8,9},{9,8},{10,11... | collective-permute-start | bytes 393224 | tf_op jit(solution)/shard_map/ppermute | solution.py:84
  137.8 7.9 %collective-permute-start.28 = (bf16[64,1024]{1,0:T(8,128)(2,1)S(1)}, bf16[64,1024]{1,0:T(8,128)(2,1)S(1)}, u32[]{:S(2)}, u32[]{:S(2)}) collective-permute-start(bf16[64,1024]{1,0:T(8,128)(2,1)S(1)} %get-tuple-element.130.refs_0_), channel_id=1, source_target_pairs={{0,4},{4,0},{1,5},{5,1},{2,6},{6,2},{3,7},{7,3},{8,12},{12,8},{9,1... | collective-permute-start | bytes 393224 | tf_op jit(solution)/shard_map/ppermute | solution.py:84
  141.2 4.5 %collective-permute-start.31 = (bf16[64,1024]{1,0:T(8,128)(2,1)S(1)}, bf16[64,1024]{1,0:T(8,128)(2,1)S(1)}, u32[]{:S(2)}, u32[]{:S(2)}) collective-permute-start(bf16[64,1024]{1,0:T(8,128)(2,1)S(1)} %collective-permute-done.27.refs_3_), channel_id=1, source_target_pairs={{0,4},{4,0},{1,5},{5,1},{2,6},{6,2},{3,7},{7,3},{8,12},{12,8},{9,1... | collective-permute-start | bytes 393224 | tf_op jit(solution)/shard_map/ppermute | solution.py:84
  144.5 2.2 collective-permute-start.30
  153.8 10.4 %collective-permute-start.44 = (bf16[512,128]{1,0:T(8,128)(2,1)S(1)}, bf16[512,128]{1,0:T(8,128)(2,1)S(1)}, u32[]{:S(2)}, u32[]{:S(2)}) collective-permute-start(bf16[512,128]{1,0:T(8,128)(2,1)S(1)} %get-tuple-element.155), channel_id=1, source_target_pairs={{8,0},{24,8},{0,16},{16,24},{9,1},{25,9},{1,17},{17,25},{10,2},{26... | collective-permute-start | bytes 393224 | tf_op jit(solution)/shard_map/ppermute | solution.py:87
  159.1 10.6 %collective-permute-start.45 = (bf16[512,128]{1,0:T(8,128)(2,1)S(1)}, bf16[512,128]{1,0:T(8,128)(2,1)S(1)}, u32[]{:S(2)}, u32[]{:S(2)}) collective-permute-start(bf16[512,128]{1,0:T(8,128)(2,1)S(1)} %get-tuple-element.156), channel_id=1, source_target_pairs={{16,0},{0,8},{24,16},{8,24},{17,1},{1,9},{25,17},{9,25},{18,2},{2,... | collective-permute-start | bytes 393224 | tf_op jit(solution)/shard_map/ppermute | solution.py:87
  159.1 13.1 %collective-permute-start.46 = (bf16[512,128]{1,0:T(8,128)(2,1)S(1)}, bf16[512,128]{1,0:T(8,128)(2,1)S(1)}, u32[]{:S(2)}, u32[]{:S(2)}) collective-permute-start(bf16[512,128]{1,0:T(8,128)(2,1)S(1)} %get-tuple-element.157), channel_id=1, source_target_pairs={{0,24},{8,16},{16,8},{24,0},{1,25},{9,17},{17,9},{25,1},{2,26},{10... | collective-permute-start | bytes 393224 | tf_op jit(solution)/shard_map/ppermute | solution.py:84
  172.2 23.1 %collective-permute-start.61 = (bf16[1728,256]{1,0:T(8,128)(2,1)S(1)}, bf16[1728,256]{1,0:T(8,128)(2,1)S(1)}, u32[]{:S(2)}, u32[]{:S(2)}) collective-permute-start(bf16[1728,256]{1,0:T(8,128)(2,1)S(1)} %get-tuple-element.179), channel_id=1, source_target_pairs={{16,0},{0,8},{24,16},{8,24},{17,1},{1,9},{25,17},{9,25},{18,2},{2,... | collective-permute-start | bytes 2654216 | tf_op jit(solution)/shard_map/ppermute | solution.py:87
  175.4 5.1 %collective-permute-start.24 = (bf16[256,1024]{1,0:T(8,128)(2,1)S(1)}, bf16[256,1024]{1,0:T(8,128)(2,1)S(1)}, u32[]{:S(2)}, u32[]{:S(2)}) collective-permute-start(bf16[256,1024]{1,0:T(8,128)(2,1)S(1)} %get-tuple-element.131), channel_id=1, source_target_pairs={{0,4},{4,0},{1,5},{5,1},{2,6},{6,2},{3,7},{7,3},{8,12},{12,8},{9,1... | collective-permute-start | bytes 1572872 | tf_op jit(solution)/shard_map/ppermute | solution.py:84
  180.5 3.5 %collective-permute-start.47 = (bf16[256,1024]{1,0:T(8,128)(2,1)S(1)}, bf16[256,1024]{1,0:T(8,128)(2,1)S(1)}, u32[]{:S(2)}, u32[]{:S(2)}) collective-permute-start(bf16[256,1024]{1,0:T(8,128)(2,1)S(1)} %get-tuple-element.164), channel_id=1, source_target_pairs={{0,4},{4,0},{1,5},{5,1},{2,6},{6,2},{3,7},{7,3},{8,12},{12,8},{9,1... | collective-permute-start | bytes 1572872 | tf_op jit(solution)/shard_map/ppermute | solution.py:84
  181.2 4.6 %collective-permute-start.32 = (bf16[64,1024]{1,0:T(8,128)(2,1)S(1)}, bf16[64,1024]{1,0:T(8,128)(2,1)S(1)}, u32[]{:S(2)}, u32[]{:S(2)}) collective-permute-start(bf16[64,1024]{1,0:T(8,128)(2,1)S(1)} %get-tuple-element.139), channel_id=1, source_target_pairs={{0,1},{1,0},{2,3},{3,2},{4,5},{5,4},{6,7},{7,6},{8,9},{9,8},{10,11... | collective-permute-start | bytes 393224 | tf_op jit(solution)/shard_map/ppermute | solution.py:84
  181.9 4.7 %collective-permute-start.33 = (bf16[64,1024]{1,0:T(8,128)(2,1)S(1)}, bf16[64,1024]{1,0:T(8,128)(2,1)S(1)}, u32[]{:S(2)}, u32[]{:S(2)}) collective-permute-start(bf16[64,1024]{1,0:T(8,128)(2,1)S(1)} %get-tuple-element.140), channel_id=1, source_target_pairs={{0,2},{1,3},{2,0},{3,1},{4,6},{5,7},{6,4},{7,5},{8,10},{9,11},{10,... | collective-permute-start | bytes 393224 | tf_op jit(solution)/shard_map/ppermute | solution.py:84
  182.6 6.6 %collective-permute-start.34 = (bf16[64,1024]{1,0:T(8,128)(2,1)S(1)}, bf16[64,1024]{1,0:T(8,128)(2,1)S(1)}, u32[]{:S(2)}, u32[]{:S(2)}) collective-permute-start(bf16[64,1024]{1,0:T(8,128)(2,1)S(1)} %get-tuple-element.141), channel_id=1, source_target_pairs={{0,3},{1,2},{2,1},{3,0},{4,7},{5,6},{6,5},{7,4},{8,11},{9,10},{10,... | collective-permute-start | bytes 393224 | tf_op jit(solution)/shard_map/ppermute | solution.py:84
  184.6 8.3 %collective-permute-start.48 = (bf16[64,1024]{1,0:T(8,128)(2,1)S(1)}, bf16[64,1024]{1,0:T(8,128)(2,1)S(1)}, u32[]{:S(2)}, u32[]{:S(2)}) collective-permute-start(bf16[64,1024]{1,0:T(8,128)(2,1)S(1)} %get-tuple-element.166), channel_id=1, source_target_pairs={{0,1},{1,0},{2,3},{3,2},{4,5},{5,4},{6,7},{7,6},{8,9},{9,8},{10,11... | collective-permute-start | bytes 393224 | tf_op jit(solution)/shard_map/ppermute | solution.py:84
  185.9 7.4 %collective-permute-start.49 = (bf16[64,1024]{1,0:T(8,128)(2,1)S(1)}, bf16[64,1024]{1,0:T(8,128)(2,1)S(1)}, u32[]{:S(2)}, u32[]{:S(2)}) collective-permute-start(bf16[64,1024]{1,0:T(8,128)(2,1)S(1)} %get-tuple-element.167), channel_id=1, source_target_pairs={{0,2},{1,3},{2,0},{3,1},{4,6},{5,7},{6,4},{7,5},{8,10},{9,11},{10,... | collective-permute-start | bytes 393224 | tf_op jit(solution)/shard_map/ppermute | solution.py:84
  186.6 7.9 %collective-permute-start.50 = (bf16[64,1024]{1,0:T(8,128)(2,1)S(1)}, bf16[64,1024]{1,0:T(8,128)(2,1)S(1)}, u32[]{:S(2)}, u32[]{:S(2)}) collective-permute-start(bf16[64,1024]{1,0:T(8,128)(2,1)S(1)} %get-tuple-element.168), channel_id=1, source_target_pairs={{0,3},{1,2},{2,1},{3,0},{4,7},{5,6},{6,5},{7,4},{8,11},{9,10},{10,... | collective-permute-start | bytes 393224 | tf_op jit(solution)/shard_map/ppermute | solution.py:84
  189.8 12.2 %collective-permute-start.38 = (bf16[64,1024]{1,0:T(8,128)(2,1)S(1)}, bf16[64,1024]{1,0:T(8,128)(2,1)S(1)}, u32[]{:S(2)}, u32[]{:S(2)}) collective-permute-start(bf16[64,1024]{1,0:T(8,128)(2,1)S(1)} %finish.1.refs_0_), channel_id=1, source_target_pairs={{0,4},{4,0},{1,5},{5,1},{2,6},{6,2},{3,7},{7,3},{8,12},{12,8},{9,1... | collective-permute-start | bytes 393224 | tf_op jit(solution)/shard_map/ppermute | solution.py:84
  192.9 6.9 %collective-permute-start.37 = (bf16[64,1024]{1,0:T(8,128)(2,1)S(1)}, bf16[64,1024]{1,0:T(8,128)(2,1)S(1)}, u32[]{:S(2)}, u32[]{:S(2)}) collective-permute-start(bf16[64,1024]{1,0:T(8,128)(2,1)S(1)} %finish.1.refs_0_), channel_id=1, source_target_pairs={{0,3},{1,2},{2,1},{3,0},{4,7},{5,6},{6,5},{7,4},{8,11},{9,10},{10,... | collective-permute-start | bytes 393224 | tf_op jit(solution)/shard_map/ppermute | solution.py:84
  193.3 7.6 %collective-permute-start.36 = (bf16[64,1024]{1,0:T(8,128)(2,1)S(1)}, bf16[64,1024]{1,0:T(8,128)(2,1)S(1)}, u32[]{:S(2)}, u32[]{:S(2)}) collective-permute-start(bf16[64,1024]{1,0:T(8,128)(2,1)S(1)} %finish.1.refs_0_), channel_id=1, source_target_pairs={{0,2},{1,3},{2,0},{3,1},{4,6},{5,7},{6,4},{7,5},{8,10},{9,11},{10,... | collective-permute-start | bytes 393224 | tf_op jit(solution)/shard_map/ppermute | solution.py:84
  195.7 37.9 %collective-permute-start.62 = (bf16[1728,256]{1,0:T(8,128)(2,1)S(1)}, bf16[1728,256]{1,0:T(8,128)(2,1)S(1)}, u32[]{:S(2)}, u32[]{:S(2)}) collective-permute-start(bf16[1728,256]{1,0:T(8,128)(2,1)S(1)} %add_convert_fusion.own_ref), channel_id=1, source_target_pairs={{0,4},{4,0},{1,5},{5,1},{2,6},{6,2},{3,7},{7,3},{8,12},{12,8},{9,1... | collective-permute-start | bytes 2654216 | tf_op jit(solution)/shard_map/ppermute | solution.py:84
  197.5 6.1 %collective-permute-start.35 = (bf16[64,1024]{1,0:T(8,128)(2,1)S(1)}, bf16[64,1024]{1,0:T(8,128)(2,1)S(1)}, u32[]{:S(2)}, u32[]{:S(2)}) collective-permute-start(bf16[64,1024]{1,0:T(8,128)(2,1)S(1)} %finish.1.refs_0_), channel_id=1, source_target_pairs={{0,1},{1,0},{2,3},{3,2},{4,5},{5,4},{6,7},{7,6},{8,9},{9,8},{10,11... | collective-permute-start | bytes 393224 | tf_op jit(solution)/shard_map/ppermute | solution.py:84
  199.8 4.4 %collective-permute-start.41 = (bf16[64,1024]{1,0:T(8,128)(2,1)S(1)}, bf16[64,1024]{1,0:T(8,128)(2,1)S(1)}, u32[]{:S(2)}, u32[]{:S(2)}) collective-permute-start(bf16[64,1024]{1,0:T(8,128)(2,1)S(1)} %collective-permute-done.37.refs_3_), channel_id=1, source_target_pairs={{0,4},{4,0},{1,5},{5,1},{2,6},{6,2},{3,7},{7,3},{8,12},{12,8},{9,1... | collective-permute-start | bytes 393224 | tf_op jit(solution)/shard_map/ppermute | solution.py:84
  200.9 3.8 %collective-permute-start.40 = (bf16[64,1024]{1,0:T(8,128)(2,1)S(1)}, bf16[64,1024]{1,0:T(8,128)(2,1)S(1)}, u32[]{:S(2)}, u32[]{:S(2)}) collective-permute-start(bf16[64,1024]{1,0:T(8,128)(2,1)S(1)} %collective-permute-done.36.refs_2_), channel_id=1, source_target_pairs={{0,4},{4,0},{1,5},{5,1},{2,6},{6,2},{3,7},{7,3},{8,12},{12,8},{9,1... | collective-permute-start | bytes 393224 | tf_op jit(solution)/shard_map/ppermute | solution.py:84
  202.0 16.4 %collective-permute-start.58 = (bf16[400,256]{1,0:T(8,128)(2,1)S(1)}, bf16[400,256]{1,0:T(8,128)(2,1)S(1)}, u32[]{:S(2)}, u32[]{:S(2)}) collective-permute-start(bf16[400,256]{1,0:T(8,128)(2,1)S(1)} %get-tuple-element.174), channel_id=1, source_target_pairs={{16,0},{0,8},{24,16},{8,24},{17,1},{1,9},{25,17},{9,25},{18,2},{2,... | collective-permute-start | bytes 614408 | tf_op jit(solution)/shard_map/ppermute | solution.py:87
  203.6 2.6 %collective-permute-start.39 = (bf16[64,1024]{1,0:T(8,128)(2,1)S(1)}, bf16[64,1024]{1,0:T(8,128)(2,1)S(1)}, u32[]{:S(2)}, u32[]{:S(2)}) collective-permute-start(bf16[64,1024]{1,0:T(8,128)(2,1)S(1)} %collective-permute-done.35.refs_1_), channel_id=1, source_target_pairs={{0,4},{4,0},{1,5},{5,1},{2,6},{6,2},{3,7},{7,3},{8,12},{12,8},{9,1... | collective-permute-start | bytes 393224 | tf_op jit(solution)/shard_map/ppermute | solution.py:84
  204.2 16.4 %collective-permute-start.59 = (bf16[400,256]{1,0:T(8,128)(2,1)S(1)}, bf16[400,256]{1,0:T(8,128)(2,1)S(1)}, u32[]{:S(2)}, u32[]{:S(2)}) collective-permute-start(bf16[400,256]{1,0:T(8,128)(2,1)S(1)} %get-tuple-element.175), channel_id=1, source_target_pairs={{8,0},{24,8},{0,16},{16,24},{9,1},{25,9},{1,17},{17,25},{10,2},{26... | collective-permute-start | bytes 614408 | tf_op jit(solution)/shard_map/ppermute | solution.py:87
  204.7 17.5 %collective-permute-start.60 = (bf16[400,256]{1,0:T(8,128)(2,1)S(1)}, bf16[400,256]{1,0:T(8,128)(2,1)S(1)}, u32[]{:S(2)}, u32[]{:S(2)}) collective-permute-start(bf16[400,256]{1,0:T(8,128)(2,1)S(1)} %get-tuple-element.176), channel_id=1, source_target_pairs={{0,24},{8,16},{16,8},{24,0},{1,25},{9,17},{17,9},{25,1},{2,26},{10... | collective-permute-start | bytes 614408 | tf_op jit(solution)/shard_map/ppermute | solution.py:84
  206.1 17.0 %collective-permute-start.53 = (bf16[64,1024]{1,0:T(8,128)(2,1)S(1)}, bf16[64,1024]{1,0:T(8,128)(2,1)S(1)}, u32[]{:S(2)}, u32[]{:S(2)}) collective-permute-start(bf16[64,1024]{1,0:T(8,128)(2,1)S(1)} %norm_one_back.1.refs_0_), channel_id=1, source_target_pairs={{0,3},{1,2},{2,1},{3,0},{4,7},{5,6},{6,5},{7,4},{8,11},{9,10},{10,... | collective-permute-start | bytes 393224 | tf_op jit(solution)/shard_map/ppermute | solution.py:84
  218.4 5.1 %collective-permute-start.52 = (bf16[64,1024]{1,0:T(8,128)(2,1)S(1)}, bf16[64,1024]{1,0:T(8,128)(2,1)S(1)}, u32[]{:S(2)}, u32[]{:S(2)}) collective-permute-start(bf16[64,1024]{1,0:T(8,128)(2,1)S(1)} %norm_one_back.1.refs_0_), channel_id=1, source_target_pairs={{0,2},{1,3},{2,0},{3,1},{4,6},{5,7},{6,4},{7,5},{8,10},{9,11},{10,... | collective-permute-start | bytes 393224 | tf_op jit(solution)/shard_map/ppermute | solution.py:84
  220.7 4.0 %collective-permute-start.54 = (bf16[64,1024]{1,0:T(8,128)(2,1)S(1)}, bf16[64,1024]{1,0:T(8,128)(2,1)S(1)}, u32[]{:S(2)}, u32[]{:S(2)}) collective-permute-start(bf16[64,1024]{1,0:T(8,128)(2,1)S(1)} %norm_one_back.1.refs_0_), channel_id=1, source_target_pairs={{0,4},{4,0},{1,5},{5,1},{2,6},{6,2},{3,7},{7,3},{8,12},{12,8},{9,1... | collective-permute-start | bytes 393224 | tf_op jit(solution)/shard_map/ppermute | solution.py:84
  222.1 5.1 %collective-permute-start.51 = (bf16[64,1024]{1,0:T(8,128)(2,1)S(1)}, bf16[64,1024]{1,0:T(8,128)(2,1)S(1)}, u32[]{:S(2)}, u32[]{:S(2)}) collective-permute-start(bf16[64,1024]{1,0:T(8,128)(2,1)S(1)} %norm_one_back.1.refs_0_), channel_id=1, source_target_pairs={{0,1},{1,0},{2,3},{3,2},{4,5},{5,4},{6,7},{7,6},{8,9},{9,8},{10,11... | collective-permute-start | bytes 393224 | tf_op jit(solution)/shard_map/ppermute | solution.py:84
  223.1 4.8 %collective-permute-start.57 = (bf16[64,1024]{1,0:T(8,128)(2,1)S(1)}, bf16[64,1024]{1,0:T(8,128)(2,1)S(1)}, u32[]{:S(2)}, u32[]{:S(2)}) collective-permute-start(bf16[64,1024]{1,0:T(8,128)(2,1)S(1)} %collective-permute-done.53.refs_3_), channel_id=1, source_target_pairs={{0,4},{4,0},{1,5},{5,1},{2,6},{6,2},{3,7},{7,3},{8,12},{12,8},{9,1... | collective-permute-start | bytes 393224 | tf_op jit(solution)/shard_map/ppermute | solution.py:84
  223.5 5.7 %collective-permute-start.56 = (bf16[64,1024]{1,0:T(8,128)(2,1)S(1)}, bf16[64,1024]{1,0:T(8,128)(2,1)S(1)}, u32[]{:S(2)}, u32[]{:S(2)}) collective-permute-start(bf16[64,1024]{1,0:T(8,128)(2,1)S(1)} %collective-permute-done.52.refs_2_), channel_id=1, source_target_pairs={{0,4},{4,0},{1,5},{5,1},{2,6},{6,2},{3,7},{7,3},{8,12},{12,8},{9,1... | collective-permute-start | bytes 393224 | tf_op jit(solution)/shard_map/ppermute | solution.py:84
  224.7 11.9 %collective-permute-start.65 = (bf16[400,256]{1,0:T(8,128)(2,1)S(1)}, bf16[400,256]{1,0:T(8,128)(2,1)S(1)}, u32[]{:S(2)}, u32[]{:S(2)}) collective-permute-start(bf16[400,256]{1,0:T(8,128)(2,1)S(1)} %add_convert_fusion.1.refs_0_), channel_id=1, source_target_pairs={{0,3},{1,2},{2,1},{3,0},{4,7},{5,6},{6,5},{7,4},{8,11},{9,10},{10,... | collective-permute-start | bytes 614408 | tf_op jit(solution)/shard_map/ppermute | solution.py:84
  227.2 9.9 %collective-permute-start.64 = (bf16[400,256]{1,0:T(8,128)(2,1)S(1)}, bf16[400,256]{1,0:T(8,128)(2,1)S(1)}, u32[]{:S(2)}, u32[]{:S(2)}) collective-permute-start(bf16[400,256]{1,0:T(8,128)(2,1)S(1)} %add_convert_fusion.1.refs_0_), channel_id=1, source_target_pairs={{0,2},{1,3},{2,0},{3,1},{4,6},{5,7},{6,4},{7,5},{8,10},{9,11},{10,... | collective-permute-start | bytes 614408 | tf_op jit(solution)/shard_map/ppermute | solution.py:84
  228.0 9.1 %collective-permute-start.63 = (bf16[400,256]{1,0:T(8,128)(2,1)S(1)}, bf16[400,256]{1,0:T(8,128)(2,1)S(1)}, u32[]{:S(2)}, u32[]{:S(2)}) collective-permute-start(bf16[400,256]{1,0:T(8,128)(2,1)S(1)} %add_convert_fusion.1.refs_0_), channel_id=1, source_target_pairs={{0,1},{1,0},{2,3},{3,2},{4,5},{5,4},{6,7},{7,6},{8,9},{9,8},{10,11... | collective-permute-start | bytes 614408 | tf_op jit(solution)/shard_map/ppermute | solution.py:84
  229.2 2.4 %collective-permute-start.55 = (bf16[64,1024]{1,0:T(8,128)(2,1)S(1)}, bf16[64,1024]{1,0:T(8,128)(2,1)S(1)}, u32[]{:S(2)}, u32[]{:S(2)}) collective-permute-start(bf16[64,1024]{1,0:T(8,128)(2,1)S(1)} %collective-permute-done.51.refs_1_), channel_id=1, source_target_pairs={{0,4},{4,0},{1,5},{5,1},{2,6},{6,2},{3,7},{7,3},{8,12},{12,8},{9,1... | collective-permute-start | bytes 393224 | tf_op jit(solution)/shard_map/ppermute | solution.py:84
  237.1 2.5 %collective-permute-start.66 = (f32[16,256]{1,0:T(8,128)S(1)}, f32[16,256]{1,0:T(8,128)S(1)}, u32[]{:S(2)}, u32[]{:S(2)}) collective-permute-start(f32[16,256]{1,0:T(8,128)S(1)} %add_add_fusion), channel_id=1, source_target_pairs={{0,4},{4,0},{1,5},{5,1},{2,6},{6,2},{3,7},{7,3},{8,12},{12,8},{9,1... | collective-permute-start | bytes 49160 | tf_op jit(solution)/shard_map/ppermute | solution.py:84
  (18 other events, 124.0 us)

commit v3 on v2

--- a/solution.py
+++ b/solution.py
@@ -96,10 +96,10 @@
     def after(values, *first):
         return lax.optimization_barrier((*values, *first))[: len(values)]
 
-    def shard_sum(blocks):
-        a, b = route(blocks[1], ROUTE_A, True), route(blocks[2], ROUTE_B, True)
-        near, far = jnp.where(inner(), b, a), jnp.where(inner(), a, b)
-        return tree([blocks[0], near, far, swap(blocks[3], "shard", 3)], BF)
+    def shard_sum(even, odd, size):
+        found = swap(odd, "shard", 1)
+        pairs = tree([even, found], BF)
+        return tree([pairs[:size], swap(pairs[size:], "shard", 2)], BF)
 
     def shard_sum_staged(blocks, later):
         (found,) = after((swap(blocks[3], "shard", 1),), later)
@@ -353,7 +353,7 @@
         )
         if blocks_mode:
             kv_parts = shard_blocks(own_kv)
-            (own_ffn,) = after((own_ffn,), *kv_parts[1:])
+            (own_ffn,) = after((own_ffn,), own_kv)
             ffn_a, ffn_b = route(own_ffn, ROUTE_A, False), route(own_ffn, ROUTE_B, False)
         else:
             kv_parts = [lax.all_gather(own_kv, "shard", axis=0, tiled=True)]
@@ -437,7 +437,7 @@
             ids,
             [row_info, queries, *kv_parts],
             scratch=[pltpu.VMEM((2 * rows, 128), F32)],
-            flops=4 * 2 * rows * rows * n_shard * 128,
+            flops=120 * 2 * rows * rows * n_shard * 128,
             vmem=4,
             name="attend",
         )
@@ -486,7 +486,7 @@
 
         def feed_forward(ids_ref, info_ref, og_ref, n2_ref, *refs):
             w_refs, refs = refs[:n_block], refs[n_block:]
-            send_ref, keep_ref, fo_send_ref, fo_keep_ref, dg_ref, du_ref, hid_ref, cot_ref, both_ref = refs
+            send_ref, keep_ref, dg_ref, du_ref, hid_ref, cot_ref, both_ref = refs
 
             def body(c, carry):
                 at = pl.ds(pl.multiple_of(c * step, step), step)
@@ -511,25 +511,21 @@
 
                 @pl.when(c == ids_ref[1])
                 def _():
-                    keep_ref[...] = both_ref[:, :width]
-                    fo_keep_ref[...] = both_ref[:, width:]
+                    keep_ref[...] = both_ref[...]
 
                 @pl.when(c != ids_ref[1])
                 def _():
-                    send_ref[...] = both_ref[:, :width]
-                    fo_send_ref[...] = both_ref[:, width:]
+                    send_ref[...] = both_ref[...]
 
                 return carry
 
             lax.fori_loop(0, n_heads, body, 0)
 
-        dn_send, dn_keep, fo_send, fo_keep, d_gate, d_up, hidden, cot = call(
+        both_send, both_keep, d_gate, d_up, hidden, cot = call(
             feed_forward,
             [
-                ((half, width), BF),
-                ((half, width), BF),
-                ((half, width), BF),
-                ((half, width), BF),
+                ((half, 2 * width), BF),
+                ((half, 2 * width), BF),
                 ((rows, hid), BF),
                 ((rows, hid), BF),
                 ((rows, hid), BF),
@@ -551,12 +547,13 @@
 
         def plane_halves(keep, send):
             got = swap(send, "heads", 1)
-            return call(split, [((sub, width), BF)] * n_tensor, ids, [keep, got], vmem=2, name="split")
+            shape = (sub, keep.shape[1])
+            return call(split, [(shape, BF)] * n_tensor, ids, [keep, got], vmem=4, name="split")
 
         def plane_sum_parts(parts):
             return [parts[0]] + [swap(parts[k], "tensor", k) for k in range(1, n_tensor)]
 
-        dn_parts = plane_sum_parts(plane_halves(dn_keep, dn_send))
+        both_parts = plane_sum_parts(plane_halves(both_keep, both_send))
 
         def ffn_grads(ids_ref, n2_ref, cot_ref, dg_ref, du_ref, hid_ref, *outs):
             outs, turned_ref = outs[:-1], outs[-1]
@@ -577,12 +574,12 @@
             vmem=8,
             name="ffn_grads",
         )
-        (first_part,) = after((dn_parts[0],), grad_ffn[0])
-        dn_parts = [first_part] + dn_parts[1:]
-
-        def norm_two_back(ids_ref, mid_ref, cot_ref, gf_ref, *refs):
-            part_refs, (dm_ref, da_ref, gp_ref) = refs[:n_tensor], refs[n_tensor:]
-            d = tree([p[...] for p in part_refs])
+        (first_part,) = after((both_parts[0],), grad_ffn[0])
+        both_parts = [first_part] + both_parts[1:]
+
+        def norm_two_back(ids_ref, info_ref, mid_ref, cot_ref, gf_ref, *refs):
+            part_refs, (dm_ref, da_ref, gp_ref, bo_ref) = refs[:n_tensor], refs[n_tensor:]
+            d = tree([p[:, :width] for p in part_refs])
             v = mid_ref[...]
             r = lax.rsqrt(jnp.mean(v * v, axis=1, keepdims=True) + EPSILON)
             w = v * r
@@ -592,12 +589,14 @@
             dm_ref[...] = dm
             da_ref[...] = dm.astype(BF)
             gp_ref[...] = jnp.broadcast_to(jnp.sum(d * w, axis=0, keepdims=True), gp_ref.shape)
-
-        d_middle, d_attn, ffn_gain_part = call(
+            total = v + tree([p[:, width:] for p in part_refs])
+            bo_ref[...] = (info_ref[my_rows(ids_ref), 1:2] * total).astype(BF)
+
+        d_middle, d_attn, ffn_gain_part, output_block = call(
             norm_two_back,
-            [((sub, width), F32), ((sub, width), BF), ((8, width), F32)],
-            ids,
-            [middle, cot, gf, *dn_parts],
+            [((sub, width), F32), ((sub, width), BF), ((8, width), F32), ((sub, width), BF)],
+            ids,
+            [row_info, middle, cot, gf, *both_parts],
             vmem=4,
             name="norm_two_back",
         )
@@ -606,7 +605,6 @@
         else:
             ffn_sum = lax.psum_scatter(grad_ffn[0], "shard", scatter_dimension=1, tiled=True)
         row_blocks = plane_blocks(d_attn)
-        fo_halves = plane_halves(fo_keep, after((fo_send,), d_attn)[0])
 
         def attend_back(ids_ref, info_ref, qs_ref, oa_ref, wo_ref, *refs):
             d_refs, refs = refs[:n_plane], refs[n_plane:]
@@ -682,31 +680,10 @@
             d_kv = after(d_kv, first_route)
             d_kv_parts = [d_kv[0], route(d_kv[1], ROUTE_A, True), route(d_kv[2], ROUTE_B, True)]
             d_kv_parts.append(swap(d_kv[3], "shard", 3))
-            (second_route,) = after((second_route,), *d_kv_parts[1:])
+            (second_route,) = after((second_route,), d_query)
             second_route = route(second_route, ROUTE_B, True)
         else:
             d_kv_parts = [lax.psum_scatter(d_kv[0], "shard", scatter_dimension=0, tiled=True)]
-
-        fo_parts = plane_sum_parts(after(fo_halves, d_query))
-
-        def finish(ids_ref, info_ref, mid_ref, *refs):
-            part_refs, out_ref = refs[:n_tensor], refs[n_tensor]
-            total = mid_ref[...] + tree([p[...] for p in part_refs])
-            out_ref[...] = (info_ref[my_rows(ids_ref), 1:2] * total).astype(BF)
-
-        (output_block,) = call(
-            finish, [((sub, width), BF)], ids, [row_info, middle, *fo_parts], vmem=4, name="finish"
-        )
-        output_parts = plane_blocks(output_block)
-
-        def stack_rows(ids_ref, *refs):
-            for b in range(n_plane):
-                at = pl.multiple_of(plane_index(ids_ref, b) * sub, sub)
-                refs[-1][pl.ds(at, sub), :] = refs[b][...].astype(refs[-1].dtype)
-
-        (block_output,) = call(
-            stack_rows, [((rows, width), BF)], ids, output_parts, vmem=2, name="stack_output"
-        )
 
         def out_grads(ids_ref, att_ref, da_ref, *outs):
             for k in range(n_block):
@@ -721,13 +698,15 @@
             vmem=4,
             name="out_grads",
         )
+
+        bundle_rows = wide + GAIN_ROWS + q_cols
 
         def project_back(ids_ref, x_ref, n_ref, raw_ref, dq_ref, cos_ref, sin_ref, hg_ref, gp_ref, *refs):
             dkv_refs, refs = refs[:n_block], refs[n_block:]
             w_refs, refs = refs[:n_block], refs[n_block:]
             if blocks_mode:
                 gwo_refs, refs = refs[:n_block], refs[n_block:]
-            send_ref, keep_ref, g_refs = refs[0], refs[1], refs[2 : 2 + n_block]
+            send_ref, keep_ref, g_refs = refs[0], refs[1], refs[2:-2]
             low_ref, r_ref = refs[-2:]
             lane = lanes((rows, 128))
             low, first = lane < 64, (lane % 64) < 32
@@ -755,7 +734,7 @@
             )
             for k in range(n_block):
                 cols = pl.ds(offset(ids_ref, k), wide)
-                g_refs[k][:wide, :] = tn_dot(n_ref[:, cols], low_ref[...]).astype(BF)
+                main = tn_dot(n_ref[:, cols], low_ref[...]).astype(BF)
                 dn = nt_dot(low_ref[...], w_refs[k][:wide, :])
                 low_dn = dn.astype(BF)
                 for c in range(n_heads):
@@ -775,13 +754,23 @@
                     high = [v.astype(BF).astype(F32) for v in three]
                     rest = [a - b for a, b in zip(three, high)]
                     packed_rows = high + rest + [jnp.zeros((GAIN_ROWS - 6, wide), F32)]
-                    g_refs[k][wide : wide + GAIN_ROWS, :] = jnp.concatenate(packed_rows, axis=0).astype(BF)
-                    g_refs[k][wide + GAIN_ROWS :, :] = gwo_refs[k][...]
+                    packed_rows = jnp.concatenate(packed_rows, axis=0).astype(BF)
+                    apart = owner(ids_ref, k) ^ ids_ref[0]
+                    for place_ in range(n_block):
+
+                        @pl.when(apart == place_)
+                        def _():
+                            to, at = g_refs[place_ % 2], (place_ // 2) * bundle_rows
+                            to[at : at + wide, :] = main
+                            to[at + wide : at + wide + GAIN_ROWS, :] = packed_rows
+                            to[at + wide + GAIN_ROWS : at + bundle_rows, :] = gwo_refs[k][...]
+
                 else:
+                    g_refs[0][...] = main
                     refs[3][...] = jnp.concatenate(three + [jnp.zeros((5, wide), F32)], axis=0)
 
         if blocks_mode:
-            grad_shapes = [((wide + GAIN_ROWS + q_cols, 256), BF)] * n_block
+            grad_shapes = [((2 * bundle_rows, 256), BF)] * 2
         else:
             grad_shapes = [((wide, 256), BF), ((8, width), F32)]
         results = call(
@@ -792,37 +781,50 @@
             + [*d_kv_parts, *attn_parts]
             + (list(grad_out) if blocks_mode else []),
             scratch=[pltpu.VMEM((rows, 256), BF), pltpu.VMEM((rows, 128), F32)],
-            flops=2 * rows * width * 512,
+            flops=60 * rows * width * 512,
             vmem=6,
             name="project_back",
         )
         d1_send, d1_keep, grads = results[0], results[1], results[2:]
         d1_parts = plane_sum_parts(plane_halves(d1_keep, d1_send))
-        def norm_one_back(ids_ref, x_ref, dm_ref, ga_ref, *refs):
-            part_refs, ig_ref = refs[:n_tensor], refs[n_tensor]
+        def norm_one_back(ids_ref, x_ref, dm_ref, ga_ref, bo_ref, *refs):
+            part_refs, both_ref = refs[:n_tensor], refs[n_tensor]
             d = tree([p[...] for p in part_refs])
             v = x_ref[my_rows(ids_ref), :].astype(F32)
             r = lax.rsqrt(jnp.mean(v * v, axis=1, keepdims=True) + EPSILON)
             w = v * r
             wd = d * ga_ref[0:1, :]
             back = r * (wd - w * jnp.mean(wd * w, axis=1, keepdims=True))
-            ig_ref[...] = (dm_ref[...] + back).astype(BF)
-
-        (input_block,) = call(
+            both_ref[:, :width] = (dm_ref[...] + back).astype(BF)
+            both_ref[:, width:] = bo_ref[...]
+
+        (both_block,) = call(
             norm_one_back,
-            [((sub, width), BF)],
-            ids,
-            [block_input, d_middle, ga, *d1_parts],
+            [((sub, 2 * width), BF)],
+            ids,
+            [block_input, d_middle, ga, output_block, *d1_parts],
             vmem=3,
             name="norm_one_back",
         )
-        input_parts = plane_blocks(input_block)
-        if blocks_mode:
-            (second_route,) = after((second_route,), input_block)
+        both_parts = plane_blocks(both_block)
+        if blocks_mode:
+            (second_route,) = after((second_route,), both_block)
             ffn_sum = tree([ffn_own, first_route, second_route], BF)
 
-        (input_grad,) = call(
-            stack_rows, [((rows, width), F32)], ids, input_parts, vmem=2, name="stack_input"
+        def stack_rows(ids_ref, *refs):
+            ig_ref, bo_ref = refs[n_plane:]
+            for b in range(n_plane):
+                at = pl.ds(pl.multiple_of(plane_index(ids_ref, b) * sub, sub), sub)
+                ig_ref[at, :] = refs[b][:, :width].astype(F32)
+                bo_ref[at, :] = refs[b][:, width:]
+
+        input_grad, block_output = call(
+            stack_rows,
+            [((rows, width), F32), ((rows, width), BF)],
+            ids,
+            both_parts,
+            vmem=8,
+            name="stack_rows",
         )
 
         def place_ffn(ids_ref, own_ref, other_ref, gate_ref, up_ref, down_ref):
@@ -863,8 +865,7 @@
                 v_ref[:, i * 128 : (i + 1) * 128] = jnp.where(low, pltpu.roll(even, 64, 1), odd)
 
         if blocks_mode:
-            grads = after(grads, d1_parts[0])
-            bundle = after((shard_sum(grads),), block_output)[0]
+            bundle = shard_sum(grads[0], grads[1], bundle_rows)
             bundles = [bundle] + [swap(bundle, "tensor", k) for k in range(1, n_tensor)]
             bundles = [after((bundle,), input_grad, gate_grad)[0]] + bundles[1:]
             total = tree([b[depth : depth + GAIN_ROWS] for b in bundles])

time: 241 us -> 232 us (0.963)
  starting transfers between devices: 79.1 us -> 57.2 us
  waiting for transfers between devices: 105 us -> 119 us
    ppermute x55 -> x45, waiting for transfers between devices: 51.4 us -> 73.1 us  [swap(): return lax.ppermute(x, axis, [(i, i ^ k) for i in range(size)])]
    ppermute x55 -> x45, starting transfers between devices: 65.4 us -> 50.6 us  [swap(): return lax.ppermute(x, axis, [(i, i ^ k) for i in range(size)])]
    ppermute x12 -> x10, waiting for transfers between devices: 53.6 us -> 46.2 us  [route(): lax.ppermute(x, 'shard', [(b, a) for a, b in pairs] if back else pairs)]
    ppermute x12 -> x10, starting transfers between devices: 13.6 us -> 6.6 us  [route(): lax.ppermute(x, 'shard', [(b, a) for a, b in pairs] if back else pairs)]
    pallas_call x23 -> x20, Pallas kernels: 46.4 us -> 44.9 us  [call(): pl.pallas_call(kernel, out_shape=shapes, in_specs=[pl.BlockSpec(memory_sp...]
  transfers between devices with their start and end apart: 67 -> 55, of which waited for: 32 -> 29; matrix products, arithmetic and copies ran while one was open for 1% -> 1% of each run, Pallas kernels for 13% -> 14%
where the time goes in v3:
time: 232 us
  waiting for transfers between devices  119 us (51%)
  starting transfers between devices  57.2 us (25%)
  Pallas kernels  44.9 us (19%)
  local copies, waits for them, and re-layouts  8.28 us (4%)
    ppermute x45, waiting for transfers between devices, swap(): return lax.ppermute(x, axis, [(i, i ^ k) for i in range(size)])  73.1 us
    ppermute x45, starting transfers between devices, swap(): return lax.ppermute(x, axis, [(i, i ^ k) for i in range(size)])  50.6 us
    ppermute x10, waiting for transfers between devices, route(): lax.ppermute(x, 'shard', [(b, a) for a, b in pairs] if back else pairs)  46.2 us
    pallas_call x20, Pallas kernels, call(): pl.pallas_call(kernel, out_shape=shapes, in_specs=[pl.BlockSpec(memory_sp...  44.9 us
    ppermute x10, starting transfers between devices, route(): lax.ppermute(x, 'shard', [(b, a) for a, b in pairs] if back else pairs)  6.6 us
    unnamed x30, local copies, waits for them, and re-layouts  5.54 us
  transfers between devices with their start and end apart: 55, of which 29 were waited for; matrix products, arithmetic and copies ran while one was open for 1% of the time, Pallas kernels for 14%

profile of v3, /device:TPU:1, one launch (start us, length us, event | category | flops | bytes accessed | tf_op | source)
XLA Modules:
  0.0 231.8 jit_solution(6031092964295430433)
XLA Ops:
  1.3 2.5 %share_attn.1.refs_0_.refs_4_ = bf16[400,256]{1,0:T(8,128)(2,1)} custom-call(s32[7]{0:T(128)} %stack.28.ids_ref, bf16[256,512]{1,0:T(8,128)(2,1)} %q_hbm.1, bf16[256,256]{1,0:T(8,128)(2,1)} %k_hbm.1, bf16[256,256]{1,0:T(8,128)(2,1)} %v_hbm.1, bf16[512,256]{1,0:T(8,128)(2,1)} %o_hbm.1, bf16[256]{0:T(256)(128)(2,1)} %ag_hbm.1, bf16[256]{0:T(256)(128)(2,1)} %fg_hbm.1), custom_call_target="tpu_custom_call" | custom-call | bytes 992256 | tf_op jit(solution)/shard_map/share_attn/pallas_call | solution.py:37
  3.8 4.2 %collective-permute-start.2 = (bf16[400,256]{1,0:T(8,128)(2,1)}, bf16[400,256]{1,0:T(8,128)(2,1)S(1)}, u32[]{:S(2)}, u32[]{:S(2)}) collective-permute-start(bf16[400,256]{1,0:T(8,128)(2,1)} %share_attn.1.refs_0_.refs_4_), channel_id=1, source_target_pairs={{0,24},{8,16},{16,8},{24,0},{1,25},{9,17},{17,9},{25,1},{2,26},{10... | collective-permute-start | bytes 614408 | tf_op jit(solution)/shard_map/ppermute | solution.py:84
  8.0 1.5 collective-permute-start
  13.4 1.7 layout.1
  15.1 1.0 fusion.4
  16.0 2.2 collective-permute-done.1.refs_2_.refs_6_
  18.2 7.0 %collective-permute-done.refs_1_.refs_5_ = bf16[400,256]{1,0:T(8,128)(2,1)S(1)} collective-permute-done((bf16[400,256]{1,0:T(8,128)(2,1)}, bf16[400,256]{1,0:T(8,128)(2,1)S(1)}, u32[]{:S(2)}, u32[]{:S(2)}) %collective-permute-start) | collective-permute-done | bytes 204832 | tf_op jit(solution)/shard_map/ppermute | solution.py:87
  25.2 0.9 copy-done.1
  26.8 3.0 %project.1 = (bf16[512,1024]{1,0:T(8,128)(2,1)S(1)}, f32[512,256]{1,0:T(8,128)S(1)}, bf16[1024,128]{1,0:T(8,128)(2,1)S(1)}, bf16[512,128]{1,0:T(8,128)(2,1)S(1)}...) custom-call(s32[7]{0:T(128)S(1)} %copy-done.7, bf16[512,1024]{1,0:T(8,128)(2,1)S(1)} %copy-done, ...), custom_call_target="tpu_custom_call" | custom-call | flops 268435456 | bytes 4431872 | tf_op jit(solution)/shard_map/project/pallas_call | solution.py:37
  29.8 2.1 collective-permute-start.5
  31.9 1.5 collective-permute-start.3
  33.4 1.4 share_ffn.1.refs_0_
  34.8 1.0 collective-permute-start.18
  36.3 3.3 %collective-permute-done.4.refs_2_.refs_10_ = bf16[512,128]{1,0:T(8,128)(2,1)S(1)} collective-permute-done((bf16[512,128]{1,0:T(8,128)(2,1)S(1)}, bf16[512,128]{1,0:T(8,128)(2,1)S(1)}, u32[]{:S(2)}, u32[]{:S(2)}) %collective-permute-start.4) | collective-permute-done | bytes 131104 | tf_op jit(solution)/shard_map/ppermute | solution.py:87
  39.6 20.6 %collective-permute-done.3.refs_1_.refs_9_ = bf16[512,128]{1,0:T(8,128)(2,1)S(1)} collective-permute-done((bf16[512,128]{1,0:T(8,128)(2,1)S(1)}, bf16[512,128]{1,0:T(8,128)(2,1)S(1)}, u32[]{:S(2)}, u32[]{:S(2)}) %collective-permute-start.3) | collective-permute-done | bytes 131104 | tf_op jit(solution)/shard_map/ppermute | solution.py:87
  60.8 2.2 collective-permute-start.8
  63.5 2.8 %attend.1 = (bf16[512,128]{1,0:T(8,128)(2,1)S(1)}, f32[1024,128]{1,0:T(8,128)S(1)}) custom-call(s32[7]{0:T(128)S(1)} %copy-done.8, f32[512,128]{1,0:T(8,128)S(1)} %get-tuple-element.86.info_ref, bf16[1024,128]{1,0:T(8,128)(2,1)S(1)} %get-tuple-element.95.qs_ref, bf16[512,128]{1,0:T(8,128)(2,1)S(1)} %get-tuple-element.90.refs_0_.refs_8_, ...), custom_call_target="tpu_custom_call" | custom-call | flops 32212254720 | bytes 1703936 | tf_op jit(solution)/shard_map/attend/pallas_call | solution.py:37
  66.3 1.0 collective-permute-done.8.refs_3_
  67.3 2.3 collective-permute-start.12
  69.6 6.7 %collective-permute-done.7.refs_2_ = bf16[128,1024]{1,0:T(8,128)(2,1)S(1)} collective-permute-done((bf16[128,1024]{1,0:T(8,128)(2,1)S(1)}, bf16[128,1024]{1,0:T(8,128)(2,1)S(1)}, u32[]{:S(2)}, u32[]{:S(2)}) %collective-permute-start.7) | collective-permute-done | bytes 262176 | tf_op jit(solution)/shard_map/ppermute | solution.py:84
  76.3 1.8 collective-permute-start.11
  78.8 1.7 collective-permute-start.9
  81.0 1.3 collective-permute-done.10.refs_3_
  82.3 1.8 collective-permute-start.13
  86.4 2.5 %middle.1 = (bf16[512,1024]{1,0:T(8,128)(2,1)S(1)}, f32[64,1024]{1,0:T(8,128)S(1)}) custom-call(s32[7]{0:T(128)S(1)} %copy-done.8, bf16[512,1024]{1,0:T(8,128)(2,1)S(1)} %copy-done, f32[8,1024]{1,0:T(8,128)S(1)} %get-tuple-element.89.gf_ref, bf16[512,1024]{1,0:T(8,128)(2,1)S(1)} %below.1.refs_0_, bf16[512,1024]{1,0:T(8,128)(2,1)S(1)} %collective-permute-done.9.refs_1_, ...), custom_call_target="tpu_custom_call" | custom-call | flops 1073741824 | bytes 5537792 | tf_op jit(solution)/shard_map/middle/pallas_call | solution.py:37
  89.0 12.7 %collective-permute-done.19.refs_3_ = bf16[1728,256]{1,0:T(8,128)(2,1)S(1)} collective-permute-done((bf16[1728,256]{1,0:T(8,128)(2,1)S(1)}, bf16[1728,256]{1,0:T(8,128)(2,1)S(1)}, u32[]{:S(2)}, u32[]{:S(2)}) %collective-permute-start.19) | collective-permute-done | bytes 884768 | tf_op jit(solution)/shard_map/ppermute | solution.py:84
  101.7 7.0 %feed_forward.1 = (bf16[256,2048]{1,0:T(8,128)(2,1)S(1)}, bf16[256,2048]{1,0:T(8,128)(2,1)S(1)}, bf16[512,576]{1,0:T(8,128)(2,1)S(1)}, bf16[512,576]{1,0:T(8,128...) custom-call(s32[7]{0:T(128)S(1)} %copy-done.8, f32[512,128]{1,0:T(8,128)S(1)} %get-tuple-element.86.info_ref, ...), custom_call_target="tpu_custom_call" | custom-call | flops 3623878656 | bytes 10813440 | tf_op jit(solution)/shard_map/feed_forward/pallas_call | solution.py:37
  108.7 2.7 %collective-permute-start.20 = (bf16[256,2048]{1,0:T(8,128)(2,1)S(1)}, bf16[256,2048]{1,0:T(8,128)(2,1)S(1)}, u32[]{:S(2)}, u32[]{:S(2)}) collective-permute-start(bf16[256,2048]{1,0:T(8,128)(2,1)S(1)} %get-tuple-element.103), channel_id=1, source_target_pairs={{0,4},{4,0},{1,5},{5,1},{2,6},{6,2},{3,7},{7,3},{8,12},{12,8},{9,1... | collective-permute-start | bytes 3145736 | tf_op jit(solution)/shard_map/ppermute | solution.py:84
  111.5 2.7 %ffn_grads.1 = (bf16[1728,256]{1,0:T(8,128)(2,1)S(1)}, bf16[1728,256]{1,0:T(8,128)(2,1)S(1)}, bf16[1728,256]{1,0:T(8,128)(2,1)S(1)}, bf16[1728,256]{1,0:T(8,128)(2,1)S(1)}) custom-call(s32[7]{0:T(128)S(1)} %copy-done.8, bf16[512,1024]{1,0:T(8,128)(2,1)S(1)} %get-tuple-element.98.n2_ref, bf16[512,1024]{1,0:T(8,128)(2,1)S(1)} %get-tuple-element.101.cot_ref, ...), custom_call_target="tpu_custom_call" | custom-call | flops 1811939328 | bytes 7405568 | tf_op jit(solution)/shard_map/ffn_grads/pallas_call | solution.py:37
  115.3 1.2 collective-permute-start.22
  116.4 1.3 collective-permute-start.23
  117.7 5.0 %collective-permute-done.21.refs_1_ = bf16[64,2048]{1,0:T(8,128)(2,1)S(1)} collective-permute-done((bf16[64,2048]{1,0:T(8,128)(2,1)S(1)}, bf16[64,2048]{1,0:T(8,128)(2,1)S(1)}, u32[]{:S(2)}, u32[]{:S(2)}) %collective-permute-start.21) | collective-permute-done | bytes 262176 | tf_op jit(solution)/shard_map/ppermute | solution.py:84
  122.7 5.7 %collective-permute-done.23.refs_3_ = bf16[64,2048]{1,0:T(8,128)(2,1)S(1)} collective-permute-done((bf16[64,2048]{1,0:T(8,128)(2,1)S(1)}, bf16[64,2048]{1,0:T(8,128)(2,1)S(1)}, u32[]{:S(2)}, u32[]{:S(2)}) %collective-permute-start.23) | collective-permute-done | bytes 262176 | tf_op jit(solution)/shard_map/ppermute | solution.py:84
  129.3 6.2 %collective-permute-done.31 = bf16[1728,256]{1,0:T(8,128)(2,1)S(1)} collective-permute-done((bf16[1728,256]{1,0:T(8,128)(2,1)S(1)}, bf16[1728,256]{1,0:T(8,128)(2,1)S(1)}, u32[]{:S(2)}, u32[]{:S(2)}) %collective-permute-start.31) | collective-permute-done | bytes 884768 | tf_op jit(solution)/shard_map/ppermute | solution.py:84
  136.1 1.6 collective-permute-start.26
  137.9 0.9 collective-permute-start.24
  138.8 1.6 collective-permute-start.27
  141.2 2.7 %collective-permute-start.30 = (bf16[64,1024]{1,0:T(8,128)(2,1)S(1)}, bf16[64,1024]{1,0:T(8,128)(2,1)S(1)}, u32[]{:S(2)}, u32[]{:S(2)}) collective-permute-start(bf16[64,1024]{1,0:T(8,128)(2,1)S(1)} %collective-permute-done.26.refs_3_), channel_id=1, source_target_pairs={{0,4},{4,0},{1,5},{5,1},{2,6},{6,2},{3,7},{7,3},{8,12},{12,8},{9,1... | collective-permute-start | bytes 393224 | tf_op jit(solution)/shard_map/ppermute | solution.py:84
  144.0 0.9 collective-permute-done.25.refs_2_
  145.8 1.0 collective-permute-done.29.refs_6_
  147.1 4.8 %attend_back.1 = (f32[512,128]{1,0:T(8,128)S(1)}, bf16[512,1024]{1,0:T(8,128)(2,1)S(1)}, bf16[512,128]{1,0:T(8,128)(2,1)S(1)}, bf16[512,128]{1,0:T(8,128)(2,1)S(...) custom-call(s32[7]{0:T(128)S(1)} %copy-done.8, f32[512,128]{1,0:T(8,128)S(1)} %get-tuple-element.86.info_ref, ...), custom_call_target="tpu_custom_call" | custom-call | flops 2684354560 | bytes 4718592 | tf_op jit(solution)/shard_map/attend_back/pallas_call | solution.py:37
  151.9 4.5 %collective-permute-done.32 = bf16[1728,256]{1,0:T(8,128)(2,1)S(1)} collective-permute-done((bf16[1728,256]{1,0:T(8,128)(2,1)S(1)}, bf16[1728,256]{1,0:T(8,128)(2,1)S(1)}, u32[]{:S(2)}, u32[]{:S(2)}) %collective-permute-start.32) | collective-permute-done | bytes 884768 | tf_op jit(solution)/shard_map/ppermute | solution.py:87
  156.4 2.1 collective-permute-start.33
  158.5 5.5 %collective-permute-start.35 = (bf16[512,128]{1,0:T(8,128)(2,1)S(1)}, bf16[512,128]{1,0:T(8,128)(2,1)S(1)}, u32[]{:S(2)}, u32[]{:S(2)}) collective-permute-start(bf16[512,128]{1,0:T(8,128)(2,1)S(1)} %get-tuple-element.132), channel_id=1, source_target_pairs={{0,24},{8,16},{16,8},{24,0},{1,25},{9,17},{17,9},{25,1},{2,26},{10... | collective-permute-start | bytes 393224 | tf_op jit(solution)/shard_map/ppermute | solution.py:84
  164.0 0.9 out_grads.1
  164.9 4.6 %collective-permute-done.34.refs_2_ = bf16[512,128]{1,0:T(8,128)(2,1)S(1)} collective-permute-done((bf16[512,128]{1,0:T(8,128)(2,1)S(1)}, bf16[512,128]{1,0:T(8,128)(2,1)S(1)}, u32[]{:S(2)}, u32[]{:S(2)}) %collective-permute-start.34) | collective-permute-done | bytes 131104 | tf_op jit(solution)/shard_map/ppermute | solution.py:87
  169.5 2.5 %collective-permute-done.35.refs_3_ = bf16[512,128]{1,0:T(8,128)(2,1)S(1)} collective-permute-done((bf16[512,128]{1,0:T(8,128)(2,1)S(1)}, bf16[512,128]{1,0:T(8,128)(2,1)S(1)}, u32[]{:S(2)}, u32[]{:S(2)}) %collective-permute-start.35) | collective-permute-done | bytes 131104 | tf_op jit(solution)/shard_map/ppermute | solution.py:84
  172.1 3.9 %project_back.1 = (bf16[256,1024]{1,0:T(8,128)(2,1)S(1)}, bf16[256,1024]{1,0:T(8,128)(2,1)S(1)}, bf16[800,256]{1,0:T(8,128)(2,1)S(1)}, bf16[800,256]{1,0:T(8,128)(2,1)S(1)}) custom-call(s32[7]{0:T(128)S(1)} %copy-done.8, bf16[512,1024]{1,0:T(8,128)(2,1)S(1)} %copy-done, bf16[512,1024]{1,0:T(8,128)(2,1)S(1)} %get-tuple-element.116.n_ref, ...), custom_call_target="tpu_custom_call" | custom-call | flops 16106127360 | bytes 6922240 | tf_op jit(solution)/shard_map/project_back/pallas_call | solution.py:37
  176.0 1.0 collective-permute-start.36
  177.0 1.5 collective-permute-done.36.got_ref
  179.4 1.2 collective-permute-start.38
  180.6 1.3 collective-permute-start.39
  181.9 2.8 %collective-permute-start.47 = (bf16[800,256]{1,0:T(8,128)(2,1)S(1)}, bf16[800,256]{1,0:T(8,128)(2,1)S(1)}, u32[]{:S(2)}, u32[]{:S(2)}) collective-permute-start(bf16[800,256]{1,0:T(8,128)(2,1)S(1)} %get-tuple-element.147), channel_id=1, source_target_pairs={{0,8},{8,0},{16,24},{24,16},{1,9},{9,1},{17,25},{25,17},{2,10},{10... | collective-permute-start | bytes 1228808 | tf_op jit(solution)/shard_map/ppermute | solution.py:84
  184.7 2.1 collective-permute-done.39.refs_3_
  188.5 1.4 collective-permute-start.41
  190.3 3.7 %collective-permute-done.49 = bf16[1728,256]{1,0:T(8,128)(2,1)S(1)} collective-permute-done((bf16[1728,256]{1,0:T(8,128)(2,1)S(1)}, bf16[1728,256]{1,0:T(8,128)(2,1)S(1)}, u32[]{:S(2)}, u32[]{:S(2)}) %collective-permute-start.49) | collective-permute-done | bytes 884768 | tf_op jit(solution)/shard_map/ppermute | solution.py:87
  195.0 7.7 %collective-permute-done.47 = bf16[800,256]{1,0:T(8,128)(2,1)S(1)} collective-permute-done((bf16[800,256]{1,0:T(8,128)(2,1)S(1)}, bf16[800,256]{1,0:T(8,128)(2,1)S(1)}, u32[]{:S(2)}, u32[]{:S(2)}) %collective-permute-start.47) | collective-permute-done | bytes 409632 | tf_op jit(solution)/shard_map/ppermute | solution.py:84
  202.9 11.3 %collective-permute-done.48 = bf16[400,256]{1,0:T(8,128)(2,1)S(1)} collective-permute-done((bf16[400,256]{1,0:T(8,128)(2,1)S(1)}, bf16[400,256]{1,0:T(8,128)(2,1)S(1)}, u32[]{:S(2)}, u32[]{:S(2)}) %collective-permute-start.48) | collective-permute-done | bytes 204832 | tf_op jit(solution)/shard_map/ppermute | solution.py:84
  215.8 1.1 collective-permute-start.53
  217.2 1.3 collective-permute-start.51
  218.5 2.4 %stack_rows.1 = (f32[512,1024]{1,0:T(8,128)}, bf16[512,1024]{1,0:T(8,128)(2,1)}) custom-call(s32[7]{0:T(128)S(1)} %copy-done.8, bf16[64,2048]{1,0:T(8,128)(2,1)S(1)} %norm_one_back.1.refs_0_, bf16[64,2048]{1,0:T(8,128)(2,1)S(1)} %collective-permute-done.40.refs_1_, bf16[64,2048]{1,0:T(8,128)(2,1)S(1)} %collective-permute-done.41.refs_2_, ...), custom_call_target="tpu_custom_call" | custom-call | bytes 5242880 | tf_op jit(solution)/shard_map/stack_rows/pallas_call | solution.py:37
  220.9 3.0 %place_ffn.1 = (f32[256,1152]{1,0:T(8,128)}, f32[256,1152]{1,0:T(8,128)}, f32[1152,256]{1,0:T(8,128)}) custom-call(s32[7]{0:T(128)S(1)} %copy-done.8, bf16[1728,256]{1,0:T(8,128)(2,1)S(1)} %add_convert_fusion.own_ref, bf16[1728,256]{1,0:T(8,128)(2,1)S(1)} %collective-permute-done.50.other_ref), custom_call_target="tpu_custom_call" | custom-call | bytes 5308416 | tf_op jit(solution)/shard_map/place_ffn/pallas_call | solution.py:37
  223.9 4.2 %collective-permute-done.52.refs_2_ = bf16[400,256]{1,0:T(8,128)(2,1)S(1)} collective-permute-done((bf16[400,256]{1,0:T(8,128)(2,1)S(1)}, bf16[400,256]{1,0:T(8,128)(2,1)S(1)}, u32[]{:S(2)}, u32[]{:S(2)}) %collective-permute-start.52) | collective-permute-done | bytes 204832 | tf_op jit(solution)/shard_map/ppermute | solution.py:84
  228.7 2.0 place.1
  (109 shorter events, 23.0 us)
Async XLA Ops:
  0.6 24.5 %copy-start = (bf16[512,1024]{1,0:T(8,128)(2,1)S(1)}, bf16[512,1024]{1,0:T(8,128)(2,1)}, u32[]{:S(2)}) copy-start(bf16[512,1024]{1,0:T(8,128)(2,1)} %x_ref.7) | copy-start | bytes 3145732
  3.7 29.6 %copy-start.3 = (bf16[256,1152]{1,0:T(8,128)(2,1)S(1)}, bf16[256,1152]{1,0:T(8,128)(2,1)}, u32[]{:S(2)}) copy-start(bf16[256,1152]{1,0:T(8,128)(2,1)} %g_hbm.1) | copy-start | bytes 1769476
  3.8 12.3 %collective-permute-start.2 = (bf16[400,256]{1,0:T(8,128)(2,1)}, bf16[400,256]{1,0:T(8,128)(2,1)S(1)}, u32[]{:S(2)}, u32[]{:S(2)}) collective-permute-start(bf16[400,256]{1,0:T(8,128)(2,1)} %share_attn.1.refs_0_.refs_4_), channel_id=1, source_target_pairs={{0,24},{8,16},{16,8},{24,0},{1,25},{9,17},{17,9},{25,1},{2,26},{10... | collective-permute-start | bytes 614408 | tf_op jit(solution)/shard_map/ppermute | solution.py:84
  8.0 10.2 %collective-permute-start.1 = (bf16[400,256]{1,0:T(8,128)(2,1)}, bf16[400,256]{1,0:T(8,128)(2,1)S(1)}, u32[]{:S(2)}, u32[]{:S(2)}) collective-permute-start(bf16[400,256]{1,0:T(8,128)(2,1)} %share_attn.1.refs_0_.refs_4_), channel_id=1, source_target_pairs={{0,16},{8,0},{16,24},{24,8},{1,17},{9,1},{17,25},{25,9},{2,18},{10... | collective-permute-start | bytes 614408 | tf_op jit(solution)/shard_map/ppermute | solution.py:87
  8.0 17.2 %collective-permute-start = (bf16[400,256]{1,0:T(8,128)(2,1)}, bf16[400,256]{1,0:T(8,128)(2,1)S(1)}, u32[]{:S(2)}, u32[]{:S(2)}) collective-permute-start(bf16[400,256]{1,0:T(8,128)(2,1)} %share_attn.1.refs_0_.refs_4_), channel_id=1, source_target_pairs={{0,8},{8,24},{16,0},{24,16},{1,9},{9,25},{17,1},{25,17},{2,10},{10... | collective-permute-start | bytes 614408 | tf_op jit(solution)/shard_map/ppermute | solution.py:87
  9.4 0.7 copy-start.6
  13.4 20.0 %copy-start.8 = (s32[7]{0:T(128)S(1)}, s32[7]{0:T(128)}, u32[]{:S(2)}) copy-start(s32[7]{0:T(128)} %stack.28.ids_ref) | copy-start | bytes 88
  25.2 0.9 copy-start.1
  26.8 6.6 %copy-start.4 = (bf16[256,1152]{1,0:T(8,128)(2,1)S(1)}, bf16[256,1152]{1,0:T(8,128)(2,1)}, u32[]{:S(2)}) copy-start(bf16[256,1152]{1,0:T(8,128)(2,1)} %u_hbm.1) | copy-start | bytes 1769476
  26.8 6.6 %copy-start.5 = (bf16[1152,256]{1,0:T(8,128)(2,1)S(1)}, bf16[1152,256]{1,0:T(8,128)(2,1)}, u32[]{:S(2)}) copy-start(bf16[1152,256]{1,0:T(8,128)(2,1)} %d_hbm.1) | copy-start | bytes 1769476
  29.8 30.4 %copy-start.2 = (bf16[400,256]{1,0:T(8,128)(2,1)S(1)}, bf16[400,256]{1,0:T(8,128)(2,1)}, u32[]{:S(2)}) copy-start(bf16[400,256]{1,0:T(8,128)(2,1)} %share_attn.1.refs_0_.refs_4_) | copy-start | bytes 614404
  29.8 6.5 %collective-permute-start.5 = (bf16[512,128]{1,0:T(8,128)(2,1)S(1)}, bf16[512,128]{1,0:T(8,128)(2,1)S(1)}, u32[]{:S(2)}, u32[]{:S(2)}) collective-permute-start(bf16[512,128]{1,0:T(8,128)(2,1)S(1)} %get-tuple-element.90.refs_0_.refs_8_), channel_id=1, source_target_pairs={{0,24},{8,16},{16,8},{24,0},{1,25},{9,17},{17,9},{25,1},{2,26},{10... | collective-permute-start | bytes 393224 | tf_op jit(solution)/shard_map/ppermute | solution.py:84
  31.9 7.7 %collective-permute-start.4 = (bf16[512,128]{1,0:T(8,128)(2,1)S(1)}, bf16[512,128]{1,0:T(8,128)(2,1)S(1)}, u32[]{:S(2)}, u32[]{:S(2)}) collective-permute-start(bf16[512,128]{1,0:T(8,128)(2,1)S(1)} %get-tuple-element.90.refs_0_.refs_8_), channel_id=1, source_target_pairs={{0,16},{8,0},{16,24},{24,8},{1,17},{9,1},{17,25},{25,9},{2,18},{10... | collective-permute-start | bytes 393224 | tf_op jit(solution)/shard_map/ppermute | solution.py:87
  31.9 28.3 %collective-permute-start.3 = (bf16[512,128]{1,0:T(8,128)(2,1)S(1)}, bf16[512,128]{1,0:T(8,128)(2,1)S(1)}, u32[]{:S(2)}, u32[]{:S(2)}) collective-permute-start(bf16[512,128]{1,0:T(8,128)(2,1)S(1)} %get-tuple-element.90.refs_0_.refs_8_), channel_id=1, source_target_pairs={{0,8},{8,24},{16,0},{24,16},{1,9},{9,25},{17,1},{25,17},{2,10},{10... | collective-permute-start | bytes 393224 | tf_op jit(solution)/shard_map/ppermute | solution.py:87
  34.8 44.0 %collective-permute-start.18 = (bf16[1728,256]{1,0:T(8,128)(2,1)S(1)}, bf16[1728,256]{1,0:T(8,128)(2,1)S(1)}, u32[]{:S(2)}, u32[]{:S(2)}) collective-permute-start(bf16[1728,256]{1,0:T(8,128)(2,1)S(1)} %share_ffn.1.refs_0_), channel_id=1, source_target_pairs={{0,16},{8,0},{16,24},{24,8},{1,17},{9,1},{17,25},{25,9},{2,18},{10... | collective-permute-start | bytes 2654216 | tf_op jit(solution)/shard_map/ppermute | solution.py:87
  35.8 45.1 %collective-permute-start.17 = (bf16[1728,256]{1,0:T(8,128)(2,1)S(1)}, bf16[1728,256]{1,0:T(8,128)(2,1)S(1)}, u32[]{:S(2)}, u32[]{:S(2)}) collective-permute-start(bf16[1728,256]{1,0:T(8,128)(2,1)S(1)} %share_ffn.1.refs_0_), channel_id=1, source_target_pairs={{0,8},{8,24},{16,0},{24,16},{1,9},{9,25},{17,1},{25,17},{2,10},{10... | collective-permute-start | bytes 2654216 | tf_op jit(solution)/shard_map/ppermute | solution.py:87
  60.8 6.5 %collective-permute-start.8 = (bf16[128,1024]{1,0:T(8,128)(2,1)S(1)}, bf16[128,1024]{1,0:T(8,128)(2,1)S(1)}, u32[]{:S(2)}, u32[]{:S(2)}) collective-permute-start(bf16[128,1024]{1,0:T(8,128)(2,1)S(1)} %beside.1.refs_0_.wo_ref), channel_id=1, source_target_pairs={{0,3},{1,2},{2,1},{3,0},{4,7},{5,6},{6,5},{7,4},{8,11},{9,10},{10,... | collective-permute-start | bytes 786440 | tf_op jit(solution)/shard_map/ppermute | solution.py:84
  63.0 13.3 %collective-permute-start.7 = (bf16[128,1024]{1,0:T(8,128)(2,1)S(1)}, bf16[128,1024]{1,0:T(8,128)(2,1)S(1)}, u32[]{:S(2)}, u32[]{:S(2)}) collective-permute-start(bf16[128,1024]{1,0:T(8,128)(2,1)S(1)} %beside.1.refs_0_.wo_ref), channel_id=1, source_target_pairs={{0,2},{1,3},{2,0},{3,1},{4,6},{5,7},{6,4},{7,5},{8,10},{9,11},{10,... | collective-permute-start | bytes 786440 | tf_op jit(solution)/shard_map/ppermute | solution.py:84
  63.2 14.9 %collective-permute-start.6 = (bf16[128,1024]{1,0:T(8,128)(2,1)S(1)}, bf16[128,1024]{1,0:T(8,128)(2,1)S(1)}, u32[]{:S(2)}, u32[]{:S(2)}) collective-permute-start(bf16[128,1024]{1,0:T(8,128)(2,1)S(1)} %beside.1.refs_0_.wo_ref), channel_id=1, source_target_pairs={{0,1},{1,0},{2,3},{3,2},{4,5},{5,4},{6,7},{7,6},{8,9},{9,8},{10,11... | collective-permute-start | bytes 786440 | tf_op jit(solution)/shard_map/ppermute | solution.py:84
  67.3 13.7 %collective-permute-start.12 = (bf16[512,128]{1,0:T(8,128)(2,1)S(1)}, bf16[512,128]{1,0:T(8,128)(2,1)S(1)}, u32[]{:S(2)}, u32[]{:S(2)}) collective-permute-start(bf16[512,128]{1,0:T(8,128)(2,1)S(1)} %get-tuple-element.96.refs_2_.att_ref), channel_id=1, source_target_pairs={{0,3},{1,2},{2,1},{3,0},{4,7},{5,6},{6,5},{7,4},{8,11},{9,10},{10,... | collective-permute-start | bytes 393224 | tf_op jit(solution)/shard_map/ppermute | solution.py:84
  76.3 4.7 %collective-permute-start.11 = (bf16[512,128]{1,0:T(8,128)(2,1)S(1)}, bf16[512,128]{1,0:T(8,128)(2,1)S(1)}, u32[]{:S(2)}, u32[]{:S(2)}) collective-permute-start(bf16[512,128]{1,0:T(8,128)(2,1)S(1)} %get-tuple-element.96.refs_2_.att_ref), channel_id=1, source_target_pairs={{0,2},{1,3},{2,0},{3,1},{4,6},{5,7},{6,4},{7,5},{8,10},{9,11},{10,... | collective-permute-start | bytes 393224 | tf_op jit(solution)/shard_map/ppermute | solution.py:84
  78.2 4.2 %collective-permute-start.10 = (bf16[512,128]{1,0:T(8,128)(2,1)S(1)}, bf16[512,128]{1,0:T(8,128)(2,1)S(1)}, u32[]{:S(2)}, u32[]{:S(2)}) collective-permute-start(bf16[512,128]{1,0:T(8,128)(2,1)S(1)} %get-tuple-element.96.refs_2_.att_ref), channel_id=1, source_target_pairs={{0,1},{1,0},{2,3},{3,2},{4,5},{5,4},{6,7},{7,6},{8,9},{9,8},{10,11... | collective-permute-start | bytes 393224 | tf_op jit(solution)/shard_map/ppermute | solution.py:84
  78.8 7.6 %collective-permute-start.9 = (bf16[512,1024]{1,0:T(8,128)(2,1)S(1)}, bf16[512,1024]{1,0:T(8,128)(2,1)S(1)}, u32[]{:S(2)}, u32[]{:S(2)}) collective-permute-start(bf16[512,1024]{1,0:T(8,128)(2,1)S(1)} %below.1.refs_0_), channel_id=1, source_target_pairs={{0,4},{4,0},{1,5},{5,1},{2,6},{6,2},{3,7},{7,3},{8,12},{12,8},{9,1... | collective-permute-start | bytes 3145736 | tf_op jit(solution)/shard_map/ppermute | solution.py:84
  82.3 19.4 %collective-permute-start.19 = (bf16[1728,256]{1,0:T(8,128)(2,1)S(1)}, bf16[1728,256]{1,0:T(8,128)(2,1)S(1)}, u32[]{:S(2)}, u32[]{:S(2)}) collective-permute-start(bf16[1728,256]{1,0:T(8,128)(2,1)S(1)} %broadcast_select_fusion), channel_id=1, source_target_pairs={{0,8},{8,0},{16,24},{24,16},{1,9},{9,1},{17,25},{25,17},{2,10},{10... | collective-permute-start | bytes 2654216 | tf_op jit(solution)/shard_map/ppermute | solution.py:84
  82.3 2.7 %collective-permute-start.13 = (bf16[512,128]{1,0:T(8,128)(2,1)S(1)}, bf16[512,128]{1,0:T(8,128)(2,1)S(1)}, u32[]{:S(2)}, u32[]{:S(2)}) collective-permute-start(bf16[512,128]{1,0:T(8,128)(2,1)S(1)} %get-tuple-element.96.refs_2_.att_ref), channel_id=1, source_target_pairs={{0,4},{4,0},{1,5},{5,1},{2,6},{6,2},{3,7},{7,3},{8,12},{12,8},{9,1... | collective-permute-start | bytes 393224 | tf_op jit(solution)/shard_map/ppermute | solution.py:84
  84.1 1.4 collective-permute-start.16
  84.1 1.5 collective-permute-start.15
  85.1 1.3 collective-permute-start.14
  86.4 15.3 %copy-start.14 = (bf16[512,1024]{1,0:T(8,128)(2,1)S(1)}, bf16[512,1024]{1,0:T(8,128)(2,1)}, u32[]{:S(2)}) copy-start(bf16[512,1024]{1,0:T(8,128)(2,1)} %og_ref.1) | copy-start | bytes 3145732
  108.7 5.5 %collective-permute-start.20 = (bf16[256,2048]{1,0:T(8,128)(2,1)S(1)}, bf16[256,2048]{1,0:T(8,128)(2,1)S(1)}, u32[]{:S(2)}, u32[]{:S(2)}) collective-permute-start(bf16[256,2048]{1,0:T(8,128)(2,1)S(1)} %get-tuple-element.103), channel_id=1, source_target_pairs={{0,4},{4,0},{1,5},{5,1},{2,6},{6,2},{3,7},{7,3},{8,12},{12,8},{9,1... | collective-permute-start | bytes 3145736 | tf_op jit(solution)/shard_map/ppermute | solution.py:84
  114.1 21.3 %collective-permute-start.31 = (bf16[1728,256]{1,0:T(8,128)(2,1)S(1)}, bf16[1728,256]{1,0:T(8,128)(2,1)S(1)}, u32[]{:S(2)}, u32[]{:S(2)}) collective-permute-start(bf16[1728,256]{1,0:T(8,128)(2,1)S(1)} %get-tuple-element.127), channel_id=1, source_target_pairs={{0,8},{8,0},{16,24},{24,16},{1,9},{9,1},{17,25},{25,17},{2,10},{10... | collective-permute-start | bytes 2654216 | tf_op jit(solution)/shard_map/ppermute | solution.py:84
  115.0 7.7 %collective-permute-start.21 = (bf16[64,2048]{1,0:T(8,128)(2,1)S(1)}, bf16[64,2048]{1,0:T(8,128)(2,1)S(1)}, u32[]{:S(2)}, u32[]{:S(2)}) collective-permute-start(bf16[64,2048]{1,0:T(8,128)(2,1)S(1)} %get-tuple-element.110), channel_id=1, source_target_pairs={{0,1},{1,0},{2,3},{3,2},{4,5},{5,4},{6,7},{7,6},{8,9},{9,8},{10,11... | collective-permute-start | bytes 786440 | tf_op jit(solution)/shard_map/ppermute | solution.py:84
  115.3 7.5 %collective-permute-start.22 = (bf16[64,2048]{1,0:T(8,128)(2,1)S(1)}, bf16[64,2048]{1,0:T(8,128)(2,1)S(1)}, u32[]{:S(2)}, u32[]{:S(2)}) collective-permute-start(bf16[64,2048]{1,0:T(8,128)(2,1)S(1)} %get-tuple-element.111), channel_id=1, source_target_pairs={{0,2},{1,3},{2,0},{3,1},{4,6},{5,7},{6,4},{7,5},{8,10},{9,11},{10,... | collective-permute-start | bytes 786440 | tf_op jit(solution)/shard_map/ppermute | solution.py:84
  116.4 12.0 %collective-permute-start.23 = (bf16[64,2048]{1,0:T(8,128)(2,1)S(1)}, bf16[64,2048]{1,0:T(8,128)(2,1)S(1)}, u32[]{:S(2)}, u32[]{:S(2)}) collective-permute-start(bf16[64,2048]{1,0:T(8,128)(2,1)S(1)} %get-tuple-element.112), channel_id=1, source_target_pairs={{0,3},{1,2},{2,1},{3,0},{4,7},{5,6},{6,5},{7,4},{8,11},{9,10},{10,... | collective-permute-start | bytes 786440 | tf_op jit(solution)/shard_map/ppermute | solution.py:84
  136.0 20.4 %collective-permute-start.32 = (bf16[1728,256]{1,0:T(8,128)(2,1)S(1)}, bf16[1728,256]{1,0:T(8,128)(2,1)S(1)}, u32[]{:S(2)}, u32[]{:S(2)}) collective-permute-start(bf16[1728,256]{1,0:T(8,128)(2,1)S(1)} %get-tuple-element.160), channel_id=1, source_target_pairs={{8,0},{24,8},{0,16},{16,24},{9,1},{25,9},{1,17},{17,25},{10,2},{26... | collective-permute-start | bytes 2654216 | tf_op jit(solution)/shard_map/ppermute | solution.py:87
  136.1 5.2 %collective-permute-start.26 = (bf16[64,1024]{1,0:T(8,128)(2,1)S(1)}, bf16[64,1024]{1,0:T(8,128)(2,1)S(1)}, u32[]{:S(2)}, u32[]{:S(2)}) collective-permute-start(bf16[64,1024]{1,0:T(8,128)(2,1)S(1)} %get-tuple-element.119.refs_0_), channel_id=1, source_target_pairs={{0,3},{1,2},{2,1},{3,0},{4,7},{5,6},{6,5},{7,4},{8,11},{9,10},{10,... | collective-permute-start | bytes 393224 | tf_op jit(solution)/shard_map/ppermute | solution.py:84
  137.7 7.3 %collective-permute-start.25 = (bf16[64,1024]{1,0:T(8,128)(2,1)S(1)}, bf16[64,1024]{1,0:T(8,128)(2,1)S(1)}, u32[]{:S(2)}, u32[]{:S(2)}) collective-permute-start(bf16[64,1024]{1,0:T(8,128)(2,1)S(1)} %get-tuple-element.119.refs_0_), channel_id=1, source_target_pairs={{0,2},{1,3},{2,0},{3,1},{4,6},{5,7},{6,4},{7,5},{8,10},{9,11},{10,... | collective-permute-start | bytes 393224 | tf_op jit(solution)/shard_map/ppermute | solution.py:84
  137.9 7.9 %collective-permute-start.24 = (bf16[64,1024]{1,0:T(8,128)(2,1)S(1)}, bf16[64,1024]{1,0:T(8,128)(2,1)S(1)}, u32[]{:S(2)}, u32[]{:S(2)}) collective-permute-start(bf16[64,1024]{1,0:T(8,128)(2,1)S(1)} %get-tuple-element.119.refs_0_), channel_id=1, source_target_pairs={{0,1},{1,0},{2,3},{3,2},{4,5},{5,4},{6,7},{7,6},{8,9},{9,8},{10,11... | collective-permute-start | bytes 393224 | tf_op jit(solution)/shard_map/ppermute | solution.py:84
  138.8 7.0 %collective-permute-start.27 = (bf16[64,1024]{1,0:T(8,128)(2,1)S(1)}, bf16[64,1024]{1,0:T(8,128)(2,1)S(1)}, u32[]{:S(2)}, u32[]{:S(2)}) collective-permute-start(bf16[64,1024]{1,0:T(8,128)(2,1)S(1)} %get-tuple-element.119.refs_0_), channel_id=1, source_target_pairs={{0,4},{4,0},{1,5},{5,1},{2,6},{6,2},{3,7},{7,3},{8,12},{12,8},{9,1... | collective-permute-start | bytes 393224 | tf_op jit(solution)/shard_map/ppermute | solution.py:84
  141.2 4.5 %collective-permute-start.30 = (bf16[64,1024]{1,0:T(8,128)(2,1)S(1)}, bf16[64,1024]{1,0:T(8,128)(2,1)S(1)}, u32[]{:S(2)}, u32[]{:S(2)}) collective-permute-start(bf16[64,1024]{1,0:T(8,128)(2,1)S(1)} %collective-permute-done.26.refs_3_), channel_id=1, source_target_pairs={{0,4},{4,0},{1,5},{5,1},{2,6},{6,2},{3,7},{7,3},{8,12},{12,8},{9,1... | collective-permute-start | bytes 393224 | tf_op jit(solution)/shard_map/ppermute | solution.py:84
  144.9 1.8 collective-permute-start.29
  145.7 1.3 collective-permute-start.28
  156.4 8.5 %collective-permute-start.33 = (bf16[512,128]{1,0:T(8,128)(2,1)S(1)}, bf16[512,128]{1,0:T(8,128)(2,1)S(1)}, u32[]{:S(2)}, u32[]{:S(2)}) collective-permute-start(bf16[512,128]{1,0:T(8,128)(2,1)S(1)} %get-tuple-element.130), channel_id=1, source_target_pairs={{8,0},{24,8},{0,16},{16,24},{9,1},{25,9},{1,17},{17,25},{10,2},{26... | collective-permute-start | bytes 393224 | tf_op jit(solution)/shard_map/ppermute | solution.py:87
  158.5 11.0 %collective-permute-start.34 = (bf16[512,128]{1,0:T(8,128)(2,1)S(1)}, bf16[512,128]{1,0:T(8,128)(2,1)S(1)}, u32[]{:S(2)}, u32[]{:S(2)}) collective-permute-start(bf16[512,128]{1,0:T(8,128)(2,1)S(1)} %get-tuple-element.131), channel_id=1, source_target_pairs={{16,0},{0,8},{24,16},{8,24},{17,1},{1,9},{25,17},{9,25},{18,2},{2,... | collective-permute-start | bytes 393224 | tf_op jit(solution)/shard_map/ppermute | solution.py:87
  158.5 13.5 %collective-permute-start.35 = (bf16[512,128]{1,0:T(8,128)(2,1)S(1)}, bf16[512,128]{1,0:T(8,128)(2,1)S(1)}, u32[]{:S(2)}, u32[]{:S(2)}) collective-permute-start(bf16[512,128]{1,0:T(8,128)(2,1)S(1)} %get-tuple-element.132), channel_id=1, source_target_pairs={{0,24},{8,16},{16,8},{24,0},{1,25},{9,17},{17,9},{25,1},{2,26},{10... | collective-permute-start | bytes 393224 | tf_op jit(solution)/shard_map/ppermute | solution.py:84
  164.0 30.0 %collective-permute-start.49 = (bf16[1728,256]{1,0:T(8,128)(2,1)S(1)}, bf16[1728,256]{1,0:T(8,128)(2,1)S(1)}, u32[]{:S(2)}, u32[]{:S(2)}) collective-permute-start(bf16[1728,256]{1,0:T(8,128)(2,1)S(1)} %get-tuple-element.149), channel_id=1, source_target_pairs={{16,0},{0,8},{24,16},{8,24},{17,1},{1,9},{25,17},{9,25},{18,2},{2,... | collective-permute-start | bytes 2654216 | tf_op jit(solution)/shard_map/ppermute | solution.py:87
  176.0 2.5 %collective-permute-start.36 = (bf16[256,1024]{1,0:T(8,128)(2,1)S(1)}, bf16[256,1024]{1,0:T(8,128)(2,1)S(1)}, u32[]{:S(2)}, u32[]{:S(2)}) collective-permute-start(bf16[256,1024]{1,0:T(8,128)(2,1)S(1)} %get-tuple-element.139), channel_id=1, source_target_pairs={{0,4},{4,0},{1,5},{5,1},{2,6},{6,2},{3,7},{7,3},{8,12},{12,8},{9,1... | collective-permute-start | bytes 1572872 | tf_op jit(solution)/shard_map/ppermute | solution.py:84
  179.2 5.5 %collective-permute-start.37 = (bf16[64,1024]{1,0:T(8,128)(2,1)S(1)}, bf16[64,1024]{1,0:T(8,128)(2,1)S(1)}, u32[]{:S(2)}, u32[]{:S(2)}) collective-permute-start(bf16[64,1024]{1,0:T(8,128)(2,1)S(1)} %get-tuple-element.141), channel_id=1, source_target_pairs={{0,1},{1,0},{2,3},{3,2},{4,5},{5,4},{6,7},{7,6},{8,9},{9,8},{10,11... | collective-permute-start | bytes 393224 | tf_op jit(solution)/shard_map/ppermute | solution.py:84
  179.4 5.3 %collective-permute-start.38 = (bf16[64,1024]{1,0:T(8,128)(2,1)S(1)}, bf16[64,1024]{1,0:T(8,128)(2,1)S(1)}, u32[]{:S(2)}, u32[]{:S(2)}) collective-permute-start(bf16[64,1024]{1,0:T(8,128)(2,1)S(1)} %get-tuple-element.142), channel_id=1, source_target_pairs={{0,2},{1,3},{2,0},{3,1},{4,6},{5,7},{6,4},{7,5},{8,10},{9,11},{10,... | collective-permute-start | bytes 393224 | tf_op jit(solution)/shard_map/ppermute | solution.py:84
  180.6 6.2 %collective-permute-start.39 = (bf16[64,1024]{1,0:T(8,128)(2,1)S(1)}, bf16[64,1024]{1,0:T(8,128)(2,1)S(1)}, u32[]{:S(2)}, u32[]{:S(2)}) collective-permute-start(bf16[64,1024]{1,0:T(8,128)(2,1)S(1)} %get-tuple-element.143), channel_id=1, source_target_pairs={{0,3},{1,2},{2,1},{3,0},{4,7},{5,6},{6,5},{7,4},{8,11},{9,10},{10,... | collective-permute-start | bytes 393224 | tf_op jit(solution)/shard_map/ppermute | solution.py:84
  181.9 20.8 %collective-permute-start.47 = (bf16[800,256]{1,0:T(8,128)(2,1)S(1)}, bf16[800,256]{1,0:T(8,128)(2,1)S(1)}, u32[]{:S(2)}, u32[]{:S(2)}) collective-permute-start(bf16[800,256]{1,0:T(8,128)(2,1)S(1)} %get-tuple-element.147), channel_id=1, source_target_pairs={{0,8},{8,0},{16,24},{24,16},{1,9},{9,1},{17,25},{25,17},{2,10},{10... | collective-permute-start | bytes 1228808 | tf_op jit(solution)/shard_map/ppermute | solution.py:84
  187.6 27.1 %collective-permute-start.42 = (bf16[64,2048]{1,0:T(8,128)(2,1)S(1)}, bf16[64,2048]{1,0:T(8,128)(2,1)S(1)}, u32[]{:S(2)}, u32[]{:S(2)}) collective-permute-start(bf16[64,2048]{1,0:T(8,128)(2,1)S(1)} %norm_one_back.1.refs_0_), channel_id=1, source_target_pairs={{0,3},{1,2},{2,1},{3,0},{4,7},{5,6},{6,5},{7,4},{8,11},{9,10},{10,... | collective-permute-start | bytes 786440 | tf_op jit(solution)/shard_map/ppermute | solution.py:84
  188.5 26.2 %collective-permute-start.41 = (bf16[64,2048]{1,0:T(8,128)(2,1)S(1)}, bf16[64,2048]{1,0:T(8,128)(2,1)S(1)}, u32[]{:S(2)}, u32[]{:S(2)}) collective-permute-start(bf16[64,2048]{1,0:T(8,128)(2,1)S(1)} %norm_one_back.1.refs_0_), channel_id=1, source_target_pairs={{0,2},{1,3},{2,0},{3,1},{4,6},{5,7},{6,4},{7,5},{8,10},{9,11},{10,... | collective-permute-start | bytes 786440 | tf_op jit(solution)/shard_map/ppermute | solution.py:84
  189.9 25.3 %collective-permute-start.40 = (bf16[64,2048]{1,0:T(8,128)(2,1)S(1)}, bf16[64,2048]{1,0:T(8,128)(2,1)S(1)}, u32[]{:S(2)}, u32[]{:S(2)}) collective-permute-start(bf16[64,2048]{1,0:T(8,128)(2,1)S(1)} %norm_one_back.1.refs_0_), channel_id=1, source_target_pairs={{0,1},{1,0},{2,3},{3,2},{4,5},{5,4},{6,7},{7,6},{8,9},{9,8},{10,11... | collective-permute-start | bytes 786440 | tf_op jit(solution)/shard_map/ppermute | solution.py:84
  194.4 26.5 %collective-permute-start.50 = (bf16[1728,256]{1,0:T(8,128)(2,1)S(1)}, bf16[1728,256]{1,0:T(8,128)(2,1)S(1)}, u32[]{:S(2)}, u32[]{:S(2)}) collective-permute-start(bf16[1728,256]{1,0:T(8,128)(2,1)S(1)} %add_convert_fusion.own_ref), channel_id=1, source_target_pairs={{0,4},{4,0},{1,5},{5,1},{2,6},{6,2},{3,7},{7,3},{8,12},{12,8},{9,1... | collective-permute-start | bytes 2654216 | tf_op jit(solution)/shard_map/ppermute | solution.py:84
  202.8 11.3 %collective-permute-start.48 = (bf16[400,256]{1,0:T(8,128)(2,1)S(1)}, bf16[400,256]{1,0:T(8,128)(2,1)S(1)}, u32[]{:S(2)}, u32[]{:S(2)}) collective-permute-start(bf16[400,256]{1,0:T(8,128)(2,1)S(1)} %slice.60), channel_id=1, source_target_pairs={{0,16},{8,24},{16,0},{24,8},{1,17},{9,25},{17,1},{25,9},{2,18},{10... | collective-permute-start | bytes 614408 | tf_op jit(solution)/shard_map/ppermute | solution.py:84
  214.1 1.7 collective-permute-start.43
  214.6 2.2 collective-permute-start.46
  214.7 2.5 %collective-permute-start.45 = (bf16[64,2048]{1,0:T(8,128)(2,1)S(1)}, bf16[64,2048]{1,0:T(8,128)(2,1)S(1)}, u32[]{:S(2)}, u32[]{:S(2)}) collective-permute-start(bf16[64,2048]{1,0:T(8,128)(2,1)S(1)} %collective-permute-done.41.refs_2_), channel_id=1, source_target_pairs={{0,4},{4,0},{1,5},{5,1},{2,6},{6,2},{3,7},{7,3},{8,12},{12,8},{9,1... | collective-permute-start | bytes 786440 | tf_op jit(solution)/shard_map/ppermute | solution.py:84
  215.2 3.3 %collective-permute-start.44 = (bf16[64,2048]{1,0:T(8,128)(2,1)S(1)}, bf16[64,2048]{1,0:T(8,128)(2,1)S(1)}, u32[]{:S(2)}, u32[]{:S(2)}) collective-permute-start(bf16[64,2048]{1,0:T(8,128)(2,1)S(1)} %collective-permute-done.40.refs_1_), channel_id=1, source_target_pairs={{0,4},{4,0},{1,5},{5,1},{2,6},{6,2},{3,7},{7,3},{8,12},{12,8},{9,1... | collective-permute-start | bytes 786440 | tf_op jit(solution)/shard_map/ppermute | solution.py:84
  215.8 8.1 %collective-permute-start.53 = (bf16[400,256]{1,0:T(8,128)(2,1)S(1)}, bf16[400,256]{1,0:T(8,128)(2,1)S(1)}, u32[]{:S(2)}, u32[]{:S(2)}) collective-permute-start(bf16[400,256]{1,0:T(8,128)(2,1)S(1)} %add_convert_fusion.2.refs_0_), channel_id=1, source_target_pairs={{0,3},{1,2},{2,1},{3,0},{4,7},{5,6},{6,5},{7,4},{8,11},{9,10},{10,... | collective-permute-start | bytes 614408 | tf_op jit(solution)/shard_map/ppermute | solution.py:84
  216.9 11.2 %collective-permute-start.52 = (bf16[400,256]{1,0:T(8,128)(2,1)S(1)}, bf16[400,256]{1,0:T(8,128)(2,1)S(1)}, u32[]{:S(2)}, u32[]{:S(2)}) collective-permute-start(bf16[400,256]{1,0:T(8,128)(2,1)S(1)} %add_convert_fusion.2.refs_0_), channel_id=1, source_target_pairs={{0,2},{1,3},{2,0},{3,1},{4,6},{5,7},{6,4},{7,5},{8,10},{9,11},{10,... | collective-permute-start | bytes 614408 | tf_op jit(solution)/shard_map/ppermute | solution.py:84
  217.2 10.9 %collective-permute-start.51 = (bf16[400,256]{1,0:T(8,128)(2,1)S(1)}, bf16[400,256]{1,0:T(8,128)(2,1)S(1)}, u32[]{:S(2)}, u32[]{:S(2)}) collective-permute-start(bf16[400,256]{1,0:T(8,128)(2,1)S(1)} %add_convert_fusion.2.refs_0_), channel_id=1, source_target_pairs={{0,1},{1,0},{2,3},{3,2},{4,5},{5,4},{6,7},{7,6},{8,9},{9,8},{10,11... | collective-permute-start | bytes 614408 | tf_op jit(solution)/shard_map/ppermute | solution.py:84
  228.1 2.5 %collective-permute-start.54 = (f32[16,256]{1,0:T(8,128)S(1)}, f32[16,256]{1,0:T(8,128)S(1)}, u32[]{:S(2)}, u32[]{:S(2)}) collective-permute-start(f32[16,256]{1,0:T(8,128)S(1)} %add_add_fusion), channel_id=1, source_target_pairs={{0,4},{4,0},{1,5},{5,1},{2,6},{6,2},{3,7},{7,3},{8,12},{12,8},{9,1... | collective-permute-start | bytes 49160 | tf_op jit(solution)/shard_map/ppermute | solution.py:84
  (6 other events, 3.9 us)
